TPU v7x, 32 devices: a whole 2x2x4 slice. The times are simulated.
32 devices in a mesh: pose: 2 (over y), occ: 4 (over z), aux: 2 (over x), rep: 2 (over core).
Axes of the slice: x: 2, y: 2, z: 4, core: 2. Of those that a mesh axis runs over, the one named last changes fastest.
Arguments:
- three_index: bfloat16 [16, 7680, 256], P(('pose', 'occ'), ('aux', 'rep')), parts along dimension 0, may hold values from -0.625 to 0.625
- valid_columns: int32 [16], P(('pose', 'occ')), parts along dimension 0, may hold values from 1 to 256, 1152 in all
- domain_blocks: int32 [16, 2], P(('pose', 'occ')), parts along dimension 0, may hold values from 0 to 63, as said below
- occupied_energy: float32 [16], P(('pose', 'occ')), parts along dimension 0, may hold values from -2 to -0.3
- virtual_energy: float32 [16384], P('pose'), parts along dimension 0, may hold values from 0.2 to 3
- shell_index: int32 [7680], P(('aux', 'rep')), may hold values from 0 to 1535, never falling along the last dimension, each value on 1 to 9 neighbouring positions
- centre_weights: float32 [3, 15360], P(None, ('pose', 'aux', 'rep')), parts along dimension 1, may hold values from -1.5 to 1.5
Outputs:
- gamma_tiles: bfloat16 [16, 7680, 256], P(('pose', 'occ'), ('aux', 'rep')), parts along dimension 0
- shell_gradient: float32 [3, 3072], P(None, ('pose', 'occ', 'aux', 'rep')), parts along dimension 1
There are 2 independent parts, one for each index of `pose`. A program takes and returns all parts, laid end to end along the dimension named above; an argument that names none is the same for every part. Nothing has to cross between parts.
Inputs may be any that keep to these rules, and one draw needn't show every extreme that they name: `domain_blocks`: each row names 2 different tiles; some row names tile 0 and some row tile 64 - 1. `valid_columns`: some orbital has all 256 columns valid. `shell_index`: never falling; every shell holds 1 to 9 consecutive functions, some exactly 9.
All inputs are finite; a program needn't handle non-finite values. No bound on the sum of `valid_columns` on one device may be relied on, other than what follows from the above.
Results may differ from a plain program's by a relative error of at most 0.012.
Values may be sent and summed in bfloat16 or wider, within the bound.
No kernel may reach another device: no remote copies, remote signals or barrier semaphores. Data moves between devices by JAX's collectives and lax.ppermute only.
A program may use at most 64 MiB of HBM per device.

v0:
```python
import jax
import jax.numpy as jnp
from jax import lax
from jax.sharding import PartitionSpec as P

ROWS_DEV = 1920
VBW = 128


opposite_scale = 1.3


def denominators(virtual_rows, virtual, occupied):
    return (
        virtual_rows.T[:, :, None, None]
        + virtual[None, None, :, :]
        - occupied[None, :, None, None]
        - occupied[None, None, :, None]
    )


def shards(
    three_index,
    valid_columns,
    domain_blocks,
    occupied_energy,
    virtual_energy,
    shell_index,
    centre_weights,
):
    occ_dev, aux_rows, domain_width = three_index.shape
    column = lax.broadcasted_iota(jnp.int32, (occ_dev, domain_width), 1)
    active = column < valid_columns[:, None]
    masked = jnp.where(active[:, None, :], three_index, jnp.zeros((), three_index.dtype))
    energy_table = virtual_energy.reshape(-1, VBW)
    block_count = energy_table.shape[0]
    selector = (
        domain_blocks[:, :, None] == lax.broadcasted_iota(jnp.int32, (1, 1, block_count), 2)
    ).astype(jnp.float32)
    virtual = jnp.einsum(
        "idv,vw->idw", selector, energy_table, precision=lax.Precision.HIGHEST
    ).reshape(occ_dev, domain_width)
    coulomb = lax.psum(
        jnp.einsum("ipa,jpb->aijb", masked, masked, preferred_element_type=jnp.float32).astype(
            jnp.bfloat16
        ),
        ("aux", "rep"),
    ).astype(jnp.float32)
    denominator = denominators(virtual, virtual, occupied_energy)
    amplitudes = (opposite_scale * coulomb / denominator).astype(jnp.bfloat16)
    gamma = jnp.einsum("jpb,aijb->ipa", masked, amplitudes, preferred_element_type=jnp.float32)
    weight = jnp.sum(gamma * masked.astype(jnp.float32), axis=(0, 2))
    shell_count = ROWS_DEV // 5 * lax.axis_size(("aux", "rep"))
    shell_terms = jax.ops.segment_sum(
        (centre_weights * weight[None, :]).T, shell_index, num_segments=shell_count
    ).T
    shell_gradient = lax.psum_scatter(
        shell_terms, ("occ", "aux", "rep"), scatter_dimension=1, tiled=True
    )
    return (gamma.astype(jnp.bfloat16), shell_gradient)


def solution(mesh):
    return jax.shard_map(
        shards,
        mesh=mesh,
        in_specs=(
            P(("pose", "occ"), ("aux", "rep"), None),
            P(("pose", "occ")),
            P(("pose", "occ"), None),
            P(("pose", "occ")),
            P("pose"),
            P(("aux", "rep")),
            P(None, ("pose", "aux", "rep")),
        ),
        out_specs=(
            P(("pose", "occ"), ("aux", "rep"), None),
            P(None, ("pose", "occ", "aux", "rep")),
        ),
        check_vma=False,
    )
```

profile of v0, /device:TPU:0, one launch (start us, length us, event | category | flops | bytes accessed | tf_op | source)
XLA Modules:
  0.0 132.8 jit_solution(14310869100261542948)
XLA Ops:
  7.2 0.0 copy-start
  7.2 0.0 all-reduce.2.cloned.1.call-start
  7.2 0.7 iota_compare_fusion
  8.0 2.8 %copy.9 = bf16[2,1920,256]{1,2,0:T(8,128)(2,1)S(1)} copy(bf16[2,1920,256]{2,1,0:T(8,128)(2,1)} %param.7) | data formatting | bytes 3932160 | tf_op args[0]
  10.8 0.0 copy-start.3
  10.8 0.0 copy-start.4
  10.8 2.2 %fusion.11 = bf16[256,2,2,256]{3,0,2,1:T(8,128)(2,1)} fusion(bf16[2,1920,256]{1,2,0:T(8,128)(2,1)S(1)} %copy.9, pred[2,256]{1,0:T(4,128)(4,1)S(1)} %iota_compare_fusion), kind=kOutput, calls=%fused_computation.11 | convolution fusion | flops 1008861184 | bytes 2490880 | tf_op jit(solution)/shard_map/ipa,jpb->aijb/dot_general | solution.py:44
  12.9 0.0 all-reduce.2.cloned.1.call-update
  13.0 0.0 reduce-scatter.2.cloned.1.call-start
  13.0 0.0 copy-done
  13.0 0.0 copy-done.3
  13.0 0.2 convolution_bitcast_fusion
  13.2 35.7 %all-reduce.2.cloned.1.call-done = bf16[256,2,2,256]{3,0,2,1:T(8,128)(2,1)} async-done(((bf16[256,2,2,256]{3,0,2,1:T(8,128)(2,1)}), bf16[256,2,2,256]{3,0,2,1:T(8,128)(2,1)}) %all-reduce.2.cloned.1.call-update) | async-done | bytes 524304 | tf_op jit(solution)/shard_map/psum | solution.py:43
  49.0 0.0 copy-done.4
  49.0 3.8 %bitcast_convert_fusion = (bf16[2,1920,256]{1,2,0:T(8,128)(2,1)}, f32[256,2,1920,1]{2,0,3,1:T(8,128)S(1)}) fusion(bf16[2,1920,256]{1,2,0:T(8,128)(2,1)S(1)} %copy.9, pred[2,256]{1,0:T(4,128)(4,1)S(1)} %iota_compare_fusion, bf16[256,2,2,256]{3,0,2,1:T(8,128)(2,1)} %all-reduce.2.cloned.1.call-done, f32[2]{0:T(128)S(1)} %copy-done.4, ...), kind=kOutput, calls=%fused_computation.2 | convolution fusion | flops 1010434048 | bytes 8393224 | tf_op jit(solution)/shard_map/jpb,aijb->ipa/dot_general | solution.py:51
  52.8 0.0 copy-start.2
  52.8 0.6 fusion
  53.4 0.1 copy-done.2
  53.5 0.0 copy-start.1
  53.5 0.4 copy.11
  53.9 14.0 %scatter_custom_fusion = f32[1536,3]{1,0:T(8,128)} fusion(s32[1920]{0:T(1024)} %param.12, f32[1920,3]{1,0:T(8,128)S(1)} %copy.11, f32[]{:T(128)} %constant.1.clone.1), kind=kCustom, calls=%fused_computation.21 | custom fusion | flops 5760 | bytes 18944 | tf_op jit(solution)/shard_map/scatter-add | solution.py:54
  67.9 0.0 reduce-scatter.2.cloned.1.call-update
  67.9 0.0 copy-done.1
  67.9 2.3 %copy.12 = bf16[2,1920,256]{2,1,0:T(8,128)(2,1)} copy(bf16[2,1920,256]{1,2,0:T(8,128)(2,1)S(1)} %copy-done.1) | data formatting | bytes 3932160
  70.2 54.3 %reduce-scatter.2.cloned.1.call-done = f32[3,96]{0,1:T(8,128)} async-done(((f32[3,1536]{0,1:T(8,128)}), f32[3,96]{0,1:T(8,128)}) %reduce-scatter.2.cloned.1.call-update) | async-done | bytes 1168 | tf_op jit(solution)/shard_map/reduce_scatter | solution.py:57
  124.6 1.4 %copy.13 = f32[3,96]{1,0:T(4,128)} copy(f32[3,96]{0,1:T(8,128)} %reduce-scatter.2.cloned.1.call-done) | data formatting | bytes 2304
  (2 shorter events, 0.0 us)
Async XLA Ops:
  7.2 5.8 %copy-start = (f32[8192]{0:T(1024)S(1)}, f32[8192]{0:T(1024)}, u32[]{:S(2)}) copy-start(f32[8192]{0:T(1024)} %param.11) | copy-start | bytes 98308
  7.2 41.8 %all-reduce.2.cloned.1.call-start = ((), (), s32[]{:S(2)}) async-start(), calls=%async_computation.1 | async-start | bytes 1048576 | tf_op jit(solution)/shard_map/psum | solution.py:43
  10.8 2.3 %copy-start.3 = (s32[2,2]{1,0:T(2,128)S(1)}, s32[2,2]{1,0:T(2,128)}, u32[]{:S(2)}) copy-start(s32[2,2]{1,0:T(2,128)} %param.9) | copy-start | bytes 52
  10.8 38.2 %copy-start.4 = (f32[2]{0:T(128)S(1)}, f32[2]{0:T(128)}, u32[]{:S(2)}) copy-start(f32[2]{0:T(128)} %param.10) | copy-start | bytes 28
  13.0 111.6 %reduce-scatter.2.cloned.1.call-start = ((), (), s32[]{:S(2)}) async-start(), calls=%async_computation.2 | async-start | bytes 835584 | tf_op jit(solution)/shard_map/reduce_scatter | solution.py:57
  52.8 0.8 copy-start.2
  53.5 14.4 %copy-start.1 = (bf16[2,1920,256]{1,2,0:T(8,128)(2,1)S(1)}, bf16[2,1920,256]{1,2,0:T(8,128)(2,1)}, u32[]{:S(2)}) copy-start(bf16[2,1920,256]{1,2,0:T(8,128)(2,1)} %get-tuple-element.6) | copy-start | bytes 5898244
Sparse Core Ops, SparseCore 0:
  13.1 35.8 all-reduce.1
  68.0 56.4 reduce-scatter.1
where the time goes:
time: 133 us
  waiting for transfers between devices  90.1 us (68%)
  other arithmetic  15.3 us (12%)
  between operations  14.1 us (11%)
  local copies, waits for them, and re-layouts  7.06 us (5%)
  matrix products  6.13 us (5%)
    reduce_scatter x1, waiting for transfers between devices, shards(): lax.psum_scatter(shell_terms, ('occ', 'aux', 'rep'), scatter_dimension=1,...  54.3 us
    psum x1, waiting for transfers between devices, shards(): lax.psum(jnp.einsum('ipa,jpb->aijb', masked, masked, preferred_element_ty...  35.7 us
    scatter-add x1, other arithmetic, shards(): jax.ops.segment_sum((centre_weights * weight[None, :]).T, shell_index, nu...  14 us
    unnamed x14, local copies, waits for them, and re-layouts  6.71 us
    dot_general x1, matrix products, shards(): jnp.einsum('jpb,aijb->ipa', masked, amplitudes, preferred_element_type=jn...  3.78 us
  transfers between devices with their start and end apart: 2, of which 2 were waited for; matrix products, arithmetic and copies ran while one was open for 2% of the time, Pallas kernels for 0%

commit v1 on v0

v1 whole, which is shorter than its diff:
```python
import functools
import jax
import jax.numpy as jnp
from jax import lax
from jax.experimental import pallas as pl
from jax.experimental.pallas import tpu as pltpu
from jax.sharding import PartitionSpec as P

VBW = 128
DOM = 2
WID = VBW * DOM
PACK = WID + 16
LANES = 128
OPPOSITE_SCALE = 1.3
F32 = jnp.float32
BF16 = jnp.bfloat16


def iota(shape, dim):
    return lax.broadcasted_iota(jnp.int32, shape, dim)


def tdot(x, y):
    return lax.dot_general(x, y, (((0,), (0,)), ((), ())), preferred_element_type=F32)


def gram_kernel(chunks, rank, valid, blocks, occupied, energies, three, send, keep, factor, held, sems):
    rows = three.shape[1]
    step = rows // chunks
    copies = []
    for k in range(chunks):
        part = pl.ds(k * step, step)
        copies.append(pltpu.make_async_copy(three.at[:, part, :], held.at[:, part, :], sems.at[k]))
        copies[-1].start()

    second = rank[0] == 1
    virtual = [
        jnp.concatenate([energies[pl.ds(blocks[i, d], 1), :] for d in range(DOM)], axis=1) for i in range(2)
    ]
    columns = jnp.concatenate([jnp.broadcast_to(v, (8, WID)) for v in virtual], axis=0).T
    down = [columns[:, 0:1], columns[:, 8:9]]
    a, b = iota((WID, WID), 0), iota((WID, WID), 1)
    upper = a <= b
    e0, e1 = occupied[0], occupied[1]
    v0, v1 = valid[0], valid[1]

    @pl.when(jnp.logical_not(second))
    def _():
        denominator = down[0] + virtual[1] - e0 - e1
        inside = (a < v0) & (b < v1)
        factor[0:WID, :] = jnp.where(inside, OPPOSITE_SCALE / denominator, 0.0)
        factor[WID:PACK, :] = jnp.zeros((PACK - WID, WID), F32)

    @pl.when(second)
    def _():
        denominator = jnp.where(upper, down[0] + virtual[0] - e0 - e0, down[1] + virtual[1] - e1 - e1)
        limit = jnp.where(upper, v0, v1)
        inside = (a < limit) & (b < limit)
        factor[0:WID, :] = jnp.where(inside, OPPOSITE_SCALE / denominator, 0.0)
        diagonal = jnp.broadcast_to(virtual[1] + virtual[1] - e1 - e1, (PACK - WID, WID))
        inside = iota((PACK - WID, WID), 1) < v1
        factor[WID:PACK, :] = jnp.where(inside, OPPOSITE_SCALE / diagonal, 0.0)

    c00 = c01 = c11 = None
    for k in range(chunks):
        copies[k].wait()
        b0, b1 = held[0, pl.ds(k * step, step), :], held[1, pl.ds(k * step, step), :]
        if k == 0:
            c00, c01, c11 = tdot(b0, b0), tdot(b0, b1), tdot(b1, b1)
        else:
            c00, c01, c11 = c00 + tdot(b0, b0), c01 + tdot(b0, b1), c11 + tdot(b1, b1)
    packed = jnp.where(upper, c00, c11)
    diagonal = jnp.sum(jnp.where(a == b, c11, 0.0), axis=0, keepdims=True)
    diagonal = jnp.broadcast_to(diagonal, (PACK - WID, WID))

    @pl.when(jnp.logical_not(second))
    def _():
        keep[0:WID, :] = c01
        keep[WID:PACK, :] = jnp.zeros((PACK - WID, WID), F32)
        send[0:WID, :] = packed.astype(BF16)
        send[WID:PACK, :] = diagonal.astype(BF16)

    @pl.when(second)
    def _():
        keep[0:WID, :] = packed
        keep[WID:PACK, :] = diagonal
        send[0:WID, :] = c01.astype(BF16)
        send[WID:PACK, :] = jnp.zeros((PACK - WID, WID), BF16)


def gamma_kernel(per, window, rank, firsts, own, other, three, index, weights, gamma, terms, table, padded, out, sems):
    rows = three.shape[1]
    first = rank[0] == 0
    part0 = jnp.where(first, own[...], other[...]).astype(F32)
    part1 = jnp.where(first, other[...], own[...]).astype(F32)
    a, b = iota((WID, WID), 0), iota((WID, WID), 1)
    t01 = part0[0:WID, :]
    packed = part1[0:WID, :]
    turned = packed.T
    diagonal = part1[WID : WID + 1, :]
    table[0:WID, 0:WID] = jnp.where(a <= b, packed, turned).astype(BF16)
    table[0:WID, WID : 2 * WID] = t01.astype(BF16)
    table[WID : 2 * WID, 0:WID] = t01.T.astype(BF16)
    table[WID : 2 * WID, WID : 2 * WID] = jnp.where(a > b, packed, jnp.where(a == b, diagonal, turned)).astype(BF16)
    padded[...] = jnp.zeros(padded.shape, F32)
    padded[0:3, :] = weights[...]
    terms[...] = jnp.zeros(terms.shape, F32)

    copies = []
    for k in range(rows // LANES):
        part = pl.ds(k * LANES, LANES)
        both = jnp.concatenate([three[0, part, :], three[1, part, :]], axis=1)
        g = jnp.dot(both, table[...], preferred_element_type=F32)
        out[0, part, :] = g[:, 0:WID].astype(BF16)
        out[1, part, :] = g[:, WID:].astype(BF16)
        copies.append(pltpu.make_async_copy(out.at[:, part, :], gamma.at[:, part, :], sems.at[k]))
        copies[-1].start()
        product = g * both.astype(F32)
        partial = sum(product[:, j * LANES : (j + 1) * LANES] for j in range(2 * WID // LANES))
        weight = jnp.sum(partial.T, axis=0, keepdims=True)
        term = padded[:, part] * weight
        high = term.astype(BF16)
        low = (term - high.astype(F32)).astype(BF16)
        stacked = jnp.concatenate([high.astype(F32), low.astype(F32)], axis=0).astype(BF16)
        chunk = firsts[k * LANES] // per
        relative = index[k : k + 1, :] - chunk * per
        column = relative
        for j in range(1, window):
            column = column + jnp.where(relative >= j * per, LANES - per, 0)
        hot = (iota((window * LANES, LANES), 0) == column).astype(F32).astype(BF16)
        sums = lax.dot_general(stacked, hot, (((1,), (1,)), ((), ())), preferred_element_type=F32)
        sums = sums[0:8, :] + sums[8:16, :]
        for j in range(window):
            terms[chunk + j] += sums[:, j * LANES : (j + 1) * LANES]
    for copy in copies:
        copy.wait()


def swap(x, axis, bit):
    count = lax.axis_size(axis)
    return lax.ppermute(x, axis, [(i, i ^ bit) for i in range(count)])


def shards(
    three_index,
    valid_columns,
    domain_blocks,
    occupied_energy,
    virtual_energy,
    shell_index,
    centre_weights,
    *,
    shells,
):
    rows = three_index.shape[1]
    n_occ, n_aux, n_rep = lax.axis_size("occ"), lax.axis_size("aux"), lax.axis_size("rep")
    owners = n_occ * n_aux * n_rep
    per = shells // owners
    window = (per + LANES - 2) // per + 1
    blocks = rows // LANES
    chunks = 3
    rank = lax.axis_index("rep").astype(jnp.int32).reshape(1)
    vmem = pl.BlockSpec(memory_space=pltpu.VMEM)
    smem = pl.BlockSpec(memory_space=pltpu.SMEM)
    anywhere = pl.BlockSpec(memory_space=pl.ANY)

    send, keep, factor = pl.pallas_call(
        functools.partial(gram_kernel, chunks),
        out_shape=(
            jax.ShapeDtypeStruct((PACK, WID), BF16),
            jax.ShapeDtypeStruct((PACK, WID), F32),
            jax.ShapeDtypeStruct((PACK, WID), F32),
        ),
        in_specs=[smem, smem, smem, smem, vmem, anywhere],
        out_specs=(vmem, vmem, vmem),
        scratch_shapes=[pltpu.VMEM(three_index.shape, BF16), pltpu.SemaphoreType.DMA((chunks,))],
        compiler_params=pltpu.CompilerParams(vmem_limit_bytes=16 << 20),
        name="gram",
    )(rank, valid_columns, domain_blocks, occupied_energy, virtual_energy.reshape(-1, VBW), three_index)

    sums = keep + swap(send, "rep", 1).astype(F32)
    bit = 1
    while bit < n_aux:
        sums = sums + swap(sums.astype(BF16), "aux", bit).astype(F32)
        bit *= 2
    own = (sums * factor).astype(BF16)
    other = swap(own, "rep", 1)

    gamma, terms = pl.pallas_call(
        functools.partial(gamma_kernel, per, window),
        out_shape=(
            jax.ShapeDtypeStruct(three_index.shape, BF16),
            jax.ShapeDtypeStruct((owners + window, 8, LANES), F32),
        ),
        in_specs=[smem, smem, vmem, vmem, vmem, vmem, vmem],
        out_specs=(anywhere, vmem),
        scratch_shapes=[
            pltpu.VMEM((2 * WID, 2 * WID), BF16),
            pltpu.VMEM((8, rows), F32),
            pltpu.VMEM(three_index.shape, BF16),
            pltpu.SemaphoreType.DMA((blocks,)),
        ],
        compiler_params=pltpu.CompilerParams(vmem_limit_bytes=24 << 20),
        name="gamma",
    )(rank, shell_index, own, other, three_index, shell_index.reshape(blocks, LANES), centre_weights)

    part = terms[:owners]
    for axis, count in (("occ", n_occ), ("aux", n_aux), ("rep", n_rep)):
        me = lax.axis_index(axis)
        bit = count // 2
        while bit:
            half = part.shape[0] // 2
            up = (me // bit) % 2
            mine = lax.dynamic_slice_in_dim(part, up * half, half, 0)
            theirs = lax.dynamic_slice_in_dim(part, (1 - up) * half, half, 0)
            part = mine + swap(theirs, axis, bit)
            bit //= 2
    return gamma, part[0, :3, :per]


def solution(mesh):

    def whole(three_index, valid_columns, domain_blocks, occupied_energy, virtual_energy, shell_index, centre_weights):
        shells = three_index.shape[1] // 5
        return jax.shard_map(
            functools.partial(shards, shells=shells),
            mesh=mesh,
            in_specs=(
                P(("pose", "occ"), ("aux", "rep"), None),
                P(("pose", "occ")),
                P(("pose", "occ"), None),
                P(("pose", "occ")),
                P("pose"),
                P(("aux", "rep")),
                P(None, ("pose", "aux", "rep")),
            ),
            out_specs=(
                P(("pose", "occ"), ("aux", "rep"), None),
                P(None, ("pose", "occ", "aux", "rep")),
            ),
            check_vma=False,
        )(three_index, valid_columns, domain_blocks, occupied_energy, virtual_energy, shell_index, centre_weights)

    return whole
```

time: 133 us -> 38.3 us (0.29)
  waiting for transfers between devices: 90.1 us -> 13 us
  other arithmetic: 15.3 us -> 0.12 us
  between operations: 14.1 us -> 0.76 us
  starting transfers between devices: 0.08 us -> 10.4 us
  Pallas kernels: 0 us -> 8.85 us
  matrix products: 6.13 us -> 0 us
  local copies, waits for them, and re-layouts: 7.06 us -> 4.91 us
    reduce_scatter x1 -> x0, waiting for transfers between devices: 54.3 us -> none  [shards(): lax.psum_scatter(shell_terms, ('occ', 'aux', 'rep'), scatter_dimension=1,...]
    psum x1 -> x0, waiting for transfers between devices: 35.7 us -> none  [shards(): lax.psum(jnp.einsum('ipa,jpb->aijb', masked, masked, preferred_element_ty...]
    scatter-add x1 -> x0, other arithmetic: 14 us -> none  [shards(): jax.ops.segment_sum((centre_weights * weight[None, :]).T, shell_index, nu...]
    ppermute x0 -> x7, waiting for transfers between devices: none -> 13 us  [swap(): return lax.ppermute(x, axis, [(i, i ^ bit) for i in range(count)])]
    ppermute x0 -> x7, starting transfers between devices: none -> 10.4 us  [swap(): return lax.ppermute(x, axis, [(i, i ^ bit) for i in range(count)])]
    pallas_call x0 -> x2, Pallas kernels: none -> 8.85 us  [the longest x1 6.29 us: shards(): pl.pallas_call(functools.partial(gamma_kernel, per, window), out_shape=(j...]
    dot_general x3 -> x0, matrix products: 6.13 us -> none  [the longest x1 3.78 us: shards(): jnp.einsum('jpb,aijb->ipa', masked, amplitudes, preferred_element_type=jn...]
    unnamed x14 -> x16, local copies, waits for them, and re-layouts: 6.71 us -> 4.3 us
  transfers between devices with their start and end apart: 2 -> 7, of which waited for: 2 -> 7; matrix products, arithmetic and copies ran while one was open for 2% -> 0% of each run, Pallas kernels for 0% -> 0%
where the time goes in v1:
time: 38.3 us; the launch traced here: 38 us
  waiting for transfers between devices  13 us (34%)
  starting transfers between devices  10.4 us (27%)
  Pallas kernels  8.85 us (23%)
  local copies, waits for them, and re-layouts  4.91 us (13%)
  between operations  0.76 us (2%)
    ppermute x7, waiting for transfers between devices, swap(): return lax.ppermute(x, axis, [(i, i ^ bit) for i in range(count)])  13 us
    ppermute x7, starting transfers between devices, swap(): return lax.ppermute(x, axis, [(i, i ^ bit) for i in range(count)])  10.4 us
    pallas_call x1, Pallas kernels, shards(): pl.pallas_call(functools.partial(gamma_kernel, per, window), out_shape=(j...  6.29 us
    unnamed x16, local copies, waits for them, and re-layouts  4.3 us
    pallas_call x1, Pallas kernels, shards(): pl.pallas_call(functools.partial(gram_kernel, chunks), out_shape=(jax.Sha...  2.56 us
  transfers between devices with their start and end apart: 7, of which 7 were waited for; matrix products, arithmetic and copies ran while one was open for 0% of the time, Pallas kernels for 0%

profile of v1, /device:TPU:0, one launch (start us, length us, event | category | flops | bytes accessed | tf_op | source)
XLA Modules:
  0.0 38.0 jit_solution(6994027741613882819)
XLA Ops:
  0.6 0.0 copy-start.2
  0.6 0.0 copy-start
  0.7 1.5 %copy-done = bf16[2,1920,256]{2,1,0:T(8,128)(2,1)S(1)} copy-done((bf16[2,1920,256]{2,1,0:T(8,128)(2,1)S(1)}, bf16[2,1920,256]{2,1,0:T(8,128)(2,1)}, u32[]{:S(2)}) %copy-start) | copy-done | bytes 1966104
  2.2 0.0 copy-start.3
  2.2 0.8 %copy-done.3 = f32[8192]{0:T(1024)S(1)} copy-done((f32[8192]{0:T(1024)S(1)}, f32[8192]{0:T(1024)}, u32[]{:S(2)}) %copy-start.3) | copy-done | bytes 32792
  3.0 0.0 copy-start.5
  3.0 0.7 %copy-done.5 = s32[2,2]{1,0:T(2,128)S(1)} copy-done((s32[2,2]{1,0:T(2,128)S(1)}, s32[2,2]{1,0:T(2,128)}, u32[]{:S(2)}) %copy-start.5) | copy-done | bytes 40
  3.6 0.0 copy-start.6
  3.6 0.7 %copy-done.6 = s32[2]{0:T(128)S(1)} copy-done((s32[2]{0:T(128)S(1)}, s32[2]{0:T(128)}, u32[]{:S(2)}) %copy-start.6) | copy-done | bytes 32
  4.3 0.0 copy-start.7
  4.3 0.7 %copy-done.7 = f32[2]{0:T(128)S(1)} copy-done((f32[2]{0:T(128)S(1)}, f32[2]{0:T(128)}, u32[]{:S(2)}) %copy-start.7) | copy-done | bytes 32
  4.9 2.6 %gram.1 = (bf16[272,256]{1,0:T(8,128)(2,1)S(1)}, f32[272,256]{1,0:T(8,128)S(1)}, f32[272,256]{1,0:T(8,128)S(1)}) custom-call(s32[1]{0:T(128)} %bitcast.rank, s32[2]{0:T(128)S(1)} %copy-done.6, s32[2,2]{1,0:T(2,128)S(1)} %copy-done.5, f32[2]{0:T(128)S(1)} %copy-done.7, f32[64,128]{1,0:T(8,128)S(1)} %bitcast.6, bf16[2,1920,256]{2,1,0:T(8,128)(2,1)S(1)} %copy-done), custom_call_target="tpu_custom_call" | custom-call | tf_op jit(solution)/shard_map/gram/pallas_call | solution.py:167
  7.5 0.6 %collective-permute-start = (bf16[272,256]{1,0:T(8,128)(2,1)S(1)}, bf16[272,256]{1,0:T(8,128)(2,1)S(1)}, u32[]{:S(2)}, u32[]{:S(2)}) collective-permute-start(bf16[272,256]{1,0:T(8,128)(2,1)S(1)} %get-tuple-element.8), channel_id=1, source_target_pairs={{0,1},{1,0},{2,3},{3,2},{4,5},{5,4},{6,7},{7,6},{8,9},{9,8},{10,11... | collective-permute-start | bytes 417800 | tf_op jit(solution)/shard_map/ppermute | solution.py:141
  8.1 1.0 %collective-permute-done = bf16[272,256]{1,0:T(8,128)(2,1)S(1)} collective-permute-done((bf16[272,256]{1,0:T(8,128)(2,1)S(1)}, bf16[272,256]{1,0:T(8,128)(2,1)S(1)}, u32[]{:S(2)}, u32[]{:S(2)}) %collective-permute-start) | collective-permute-done | bytes 139296 | tf_op jit(solution)/shard_map/ppermute | solution.py:141
  9.1 2.8 %collective-permute-start.1 = (bf16[272,256]{1,0:T(8,128)(2,1)S(1)}, bf16[272,256]{1,0:T(8,128)(2,1)S(1)}, u32[]{:S(2)}, u32[]{:S(2)}) collective-permute-start(bf16[272,256]{1,0:T(8,128)(2,1)S(1)} %fusion), channel_id=1, source_target_pairs={{0,2},{2,0},{1,3},{3,1},{4,6},{6,4},{5,7},{7,5},{8,10},{10,8},{9,1... | collective-permute-start | bytes 417800 | tf_op jit(solution)/shard_map/ppermute | solution.py:141
  12.0 4.0 %collective-permute-done.1 = bf16[272,256]{1,0:T(8,128)(2,1)S(1)} collective-permute-done((bf16[272,256]{1,0:T(8,128)(2,1)S(1)}, bf16[272,256]{1,0:T(8,128)(2,1)S(1)}, u32[]{:S(2)}, u32[]{:S(2)}) %collective-permute-start.1) | collective-permute-done | bytes 139296 | tf_op jit(solution)/shard_map/ppermute | solution.py:141
  16.0 0.1 multiply_convert_fusion.own
  16.0 0.1 collective-permute-start.2
  16.2 1.3 %collective-permute-done.2.other = bf16[272,256]{1,0:T(8,128)(2,1)S(1)} collective-permute-done((bf16[272,256]{1,0:T(8,128)(2,1)S(1)}, bf16[272,256]{1,0:T(8,128)(2,1)S(1)}, u32[]{:S(2)}, u32[]{:S(2)}) %collective-permute-start.2) | collective-permute-done | bytes 139296 | tf_op jit(solution)/shard_map/ppermute | solution.py:141
  17.5 0.0 copy-done.2
  17.5 0.0 copy-done.1
  17.5 0.0 copy-done.4
  17.5 6.3 %gamma.1 = (bf16[2,1920,256]{2,1,0:T(8,128)(2,1)}, f32[19,8,128]{2,1,0:T(8,128)S(1)}) custom-call(s32[1]{0:T(128)} %bitcast.rank, s32[1920]{0:T(1024)S(1)} %copy-done.2, bf16[272,256]{1,0:T(8,128)(2,1)S(1)} %multiply_convert_fusion.own, bf16[272,256]{1,0:T(8,128)(2,1)S(1)} %collective-permute-done.2.other, bf16[2,1920,256]{2,1,0:T(8,128)(2,1)S(1)} %copy-done.1, ...), custom_call_target="tpu_custom_call" | custom-call | tf_op jit(solution)/shard_map/gamma/pallas_call | solution.py:189
  23.8 2.9 %collective-permute-start.3 = (f32[8,8,128]{2,1,0:T(8,128)S(1)}, f32[8,8,128]{2,1,0:T(8,128)S(1)}, u32[]{:S(2)}, u32[]{:S(2)}) collective-permute-start(f32[8,8,128]{2,1,0:T(8,128)S(1)} %constant_dynamic-slice_fusion.3), channel_id=1, source_target_pairs={{0,8},{4,12},{8,0},{12,4},{1,9},{5,13},{9,1},{13,5},{2,10},{6,14},... | collective-permute-start | bytes 98312 | tf_op jit(solution)/shard_map/ppermute | solution.py:141
  26.7 2.0 %collective-permute-done.3 = f32[8,8,128]{2,1,0:T(8,128)S(1)} collective-permute-done((f32[8,8,128]{2,1,0:T(8,128)S(1)}, f32[8,8,128]{2,1,0:T(8,128)S(1)}, u32[]{:S(2)}, u32[]{:S(2)}) %collective-permute-start.3) | collective-permute-done | bytes 32800 | tf_op jit(solution)/shard_map/ppermute | solution.py:141
  28.7 1.9 %collective-permute-start.4 = (f32[4,8,128]{2,1,0:T(8,128)S(1)}, f32[4,8,128]{2,1,0:T(8,128)S(1)}, u32[]{:S(2)}, u32[]{:S(2)}) collective-permute-start(f32[4,8,128]{2,1,0:T(8,128)S(1)} %constant_dynamic-slice_fusion.2), channel_id=1, source_target_pairs={{0,4},{4,0},{8,12},{12,8},{1,5},{5,1},{9,13},{13,9},{2,6},{6,2},{1... | collective-permute-start | bytes 49160 | tf_op jit(solution)/shard_map/ppermute | solution.py:141
  30.6 1.9 %collective-permute-done.4 = f32[4,8,128]{2,1,0:T(8,128)S(1)} collective-permute-done((f32[4,8,128]{2,1,0:T(8,128)S(1)}, f32[4,8,128]{2,1,0:T(8,128)S(1)}, u32[]{:S(2)}, u32[]{:S(2)}) %collective-permute-start.4) | collective-permute-done | bytes 16416 | tf_op jit(solution)/shard_map/ppermute | solution.py:141
  32.5 2.1 %collective-permute-start.5 = (f32[2,8,128]{2,1,0:T(8,128)S(1)}, f32[2,8,128]{2,1,0:T(8,128)S(1)}, u32[]{:S(2)}, u32[]{:S(2)}) collective-permute-start(f32[2,8,128]{2,1,0:T(8,128)S(1)} %constant_dynamic-slice_fusion.1), channel_id=1, source_target_pairs={{0,2},{2,0},{1,3},{3,1},{4,6},{6,4},{5,7},{7,5},{8,10},{10,8},{9,1... | collective-permute-start | bytes 24584 | tf_op jit(solution)/shard_map/ppermute | solution.py:141
  34.6 1.6 %collective-permute-done.5 = f32[2,8,128]{2,1,0:T(8,128)S(1)} collective-permute-done((f32[2,8,128]{2,1,0:T(8,128)S(1)}, f32[2,8,128]{2,1,0:T(8,128)S(1)}, u32[]{:S(2)}, u32[]{:S(2)}) %collective-permute-start.5) | collective-permute-done | bytes 8224 | tf_op jit(solution)/shard_map/ppermute | solution.py:141
  36.2 0.0 collective-permute-start.6
  36.3 1.2 %collective-permute-done.6 = f32[1,8,128]{2,1,0:T(8,128)S(1)} collective-permute-done((f32[1,8,128]{2,1,0:T(8,128)S(1)}, f32[1,8,128]{2,1,0:T(8,128)S(1)}, u32[]{:S(2)}, u32[]{:S(2)}) %collective-permute-start.6) | collective-permute-done | bytes 4128 | tf_op jit(solution)/shard_map/ppermute | solution.py:141
  37.4 0.6 %slice_bitcast_fusion = f32[3,96]{1,0:T(4,128)} fusion(f32[1,8,128]{2,1,0:T(8,128)S(1)} %dynamic-slice_add_fusion.3), kind=kLoop, calls=%fused_computation.7 | loop fusion | bytes 2304 | tf_op jit(solution)/shard_map/squeeze | solution.py:218
  (12 shorter events, 0.1 us)
Async XLA Ops:
  0.6 16.8 %copy-start.2 = (s32[1920]{0:T(1024)S(1)}, s32[1920]{0:T(1024)}, u32[]{:S(2)}) copy-start(s32[1920]{0:T(1024)} %firsts.1) | copy-start | bytes 23044
  0.6 1.5 %copy-start = (bf16[2,1920,256]{2,1,0:T(8,128)(2,1)S(1)}, bf16[2,1920,256]{2,1,0:T(8,128)(2,1)}, u32[]{:S(2)}) copy-start(bf16[2,1920,256]{2,1,0:T(8,128)(2,1)} %three.3) | copy-start | bytes 5898244
  2.2 0.8 %copy-start.3 = (f32[8192]{0:T(1024)S(1)}, f32[8192]{0:T(1024)}, u32[]{:S(2)}) copy-start(f32[8192]{0:T(1024)} %param.11) | copy-start | bytes 98308
  3.0 0.7 %copy-start.5 = (s32[2,2]{1,0:T(2,128)S(1)}, s32[2,2]{1,0:T(2,128)}, u32[]{:S(2)}) copy-start(s32[2,2]{1,0:T(2,128)} %blocks.1) | copy-start | bytes 52
  3.6 0.7 %copy-start.6 = (s32[2]{0:T(128)S(1)}, s32[2]{0:T(128)}, u32[]{:S(2)}) copy-start(s32[2]{0:T(128)} %valid.1) | copy-start | bytes 28
  4.3 0.7 %copy-start.7 = (f32[2]{0:T(128)S(1)}, f32[2]{0:T(128)}, u32[]{:S(2)}) copy-start(f32[2]{0:T(128)} %occupied.1) | copy-start | bytes 28
  4.9 12.5 %copy-start.1 = (bf16[2,1920,256]{2,1,0:T(8,128)(2,1)S(1)}, bf16[2,1920,256]{2,1,0:T(8,128)(2,1)}, u32[]{:S(2)}) copy-start(bf16[2,1920,256]{2,1,0:T(8,128)(2,1)} %three.3) | copy-start | bytes 5898244
  4.9 12.5 %copy-start.4 = (f32[3,1920]{1,0:T(4,128)S(1)}, f32[3,1920]{1,0:T(4,128)}, u32[]{:S(2)}) copy-start(f32[3,1920]{1,0:T(4,128)} %weights.1) | copy-start | bytes 69124
  7.5 1.6 %collective-permute-start = (bf16[272,256]{1,0:T(8,128)(2,1)S(1)}, bf16[272,256]{1,0:T(8,128)(2,1)S(1)}, u32[]{:S(2)}, u32[]{:S(2)}) collective-permute-start(bf16[272,256]{1,0:T(8,128)(2,1)S(1)} %get-tuple-element.8), channel_id=1, source_target_pairs={{0,1},{1,0},{2,3},{3,2},{4,5},{5,4},{6,7},{7,6},{8,9},{9,8},{10,11... | collective-permute-start | bytes 417800 | tf_op jit(solution)/shard_map/ppermute | solution.py:141
  9.1 6.8 %collective-permute-start.1 = (bf16[272,256]{1,0:T(8,128)(2,1)S(1)}, bf16[272,256]{1,0:T(8,128)(2,1)S(1)}, u32[]{:S(2)}, u32[]{:S(2)}) collective-permute-start(bf16[272,256]{1,0:T(8,128)(2,1)S(1)} %fusion), channel_id=1, source_target_pairs={{0,2},{2,0},{1,3},{3,1},{4,6},{6,4},{5,7},{7,5},{8,10},{10,8},{9,1... | collective-permute-start | bytes 417800 | tf_op jit(solution)/shard_map/ppermute | solution.py:141
  16.0 1.4 %collective-permute-start.2 = (bf16[272,256]{1,0:T(8,128)(2,1)S(1)}, bf16[272,256]{1,0:T(8,128)(2,1)S(1)}, u32[]{:S(2)}, u32[]{:S(2)}) collective-permute-start(bf16[272,256]{1,0:T(8,128)(2,1)S(1)} %multiply_convert_fusion.own), channel_id=1, source_target_pairs={{0,1},{1,0},{2,3},{3,2},{4,5},{5,4},{6,7},{7,6},{8,9},{9,8},{10,11... | collective-permute-start | bytes 417800 | tf_op jit(solution)/shard_map/ppermute | solution.py:141
  23.8 4.9 %collective-permute-start.3 = (f32[8,8,128]{2,1,0:T(8,128)S(1)}, f32[8,8,128]{2,1,0:T(8,128)S(1)}, u32[]{:S(2)}, u32[]{:S(2)}) collective-permute-start(f32[8,8,128]{2,1,0:T(8,128)S(1)} %constant_dynamic-slice_fusion.3), channel_id=1, source_target_pairs={{0,8},{4,12},{8,0},{12,4},{1,9},{5,13},{9,1},{13,5},{2,10},{6,14},... | collective-permute-start | bytes 98312 | tf_op jit(solution)/shard_map/ppermute | solution.py:141
  28.7 3.8 %collective-permute-start.4 = (f32[4,8,128]{2,1,0:T(8,128)S(1)}, f32[4,8,128]{2,1,0:T(8,128)S(1)}, u32[]{:S(2)}, u32[]{:S(2)}) collective-permute-start(f32[4,8,128]{2,1,0:T(8,128)S(1)} %constant_dynamic-slice_fusion.2), channel_id=1, source_target_pairs={{0,4},{4,0},{8,12},{12,8},{1,5},{5,1},{9,13},{13,9},{2,6},{6,2},{1... | collective-permute-start | bytes 49160 | tf_op jit(solution)/shard_map/ppermute | solution.py:141
  32.5 3.7 %collective-permute-start.5 = (f32[2,8,128]{2,1,0:T(8,128)S(1)}, f32[2,8,128]{2,1,0:T(8,128)S(1)}, u32[]{:S(2)}, u32[]{:S(2)}) collective-permute-start(f32[2,8,128]{2,1,0:T(8,128)S(1)} %constant_dynamic-slice_fusion.1), channel_id=1, source_target_pairs={{0,2},{2,0},{1,3},{3,1},{4,6},{6,4},{5,7},{7,5},{8,10},{10,8},{9,1... | collective-permute-start | bytes 24584 | tf_op jit(solution)/shard_map/ppermute | solution.py:141
  36.2 1.2 %collective-permute-start.6 = (f32[1,8,128]{2,1,0:T(8,128)S(1)}, f32[1,8,128]{2,1,0:T(8,128)S(1)}, u32[]{:S(2)}, u32[]{:S(2)}) collective-permute-start(f32[1,8,128]{2,1,0:T(8,128)S(1)} %constant_dynamic-slice_fusion), channel_id=1, source_target_pairs={{0,1},{1,0},{2,3},{3,2},{4,5},{5,4},{6,7},{7,6},{8,9},{9,8},{10,11... | collective-permute-start | bytes 12296 | tf_op jit(solution)/shard_map/ppermute | solution.py:141

commit v2 on v1

v2 whole, which is shorter than its diff:
```python
import functools
import jax
import jax.numpy as jnp
from jax import lax
from jax.experimental import pallas as pl
from jax.experimental.pallas import tpu as pltpu
from jax.sharding import PartitionSpec as P

VBW = 128
DOM = 2
WID = VBW * DOM
PACK = WID + 16
LANES = 128
SEG = 256
OPPOSITE_SCALE = 1.3
F32 = jnp.float32
BF16 = jnp.bfloat16


def iota(shape, dim):
    return lax.broadcasted_iota(jnp.int32, shape, dim)


def tdot(x, y):
    return lax.dot_general(x, y, (((0,), (0,)), ((), ())), preferred_element_type=F32)


def factor_kernel(valid, blocks, occupied, energies, factor):
    second = lax.axis_index("rep") == 1
    virtual = [
        jnp.concatenate([energies[pl.ds(blocks[i, d], 1), :] for d in range(DOM)], axis=1) for i in range(2)
    ]
    columns = jnp.concatenate([jnp.broadcast_to(v, (8, WID)) for v in virtual], axis=0).T
    down = [columns[:, 0:1], columns[:, 8:9]]
    a, b = iota((WID, WID), 0), iota((WID, WID), 1)
    upper = a <= b
    e0, e1 = occupied[0], occupied[1]
    v0, v1 = valid[0], valid[1]

    @pl.when(jnp.logical_not(second))
    def _():
        denominator = down[0] + virtual[1] - e0 - e1
        inside = (a < v0) & (b < v1)
        factor[0:WID, :] = jnp.where(inside, OPPOSITE_SCALE / denominator, 0.0)
        factor[WID:PACK, :] = jnp.zeros((PACK - WID, WID), F32)

    @pl.when(second)
    def _():
        denominator = jnp.where(upper, down[0] + virtual[0] - e0 - e0, down[1] + virtual[1] - e1 - e1)
        limit = jnp.where(upper, v0, v1)
        inside = (a < limit) & (b < limit)
        factor[0:WID, :] = jnp.where(inside, OPPOSITE_SCALE / denominator, 0.0)
        diagonal = jnp.broadcast_to(virtual[1] + virtual[1] - e1 - e1, (PACK - WID, WID))
        inside = iota((PACK - WID, WID), 1) < v1
        factor[WID:PACK, :] = jnp.where(inside, OPPOSITE_SCALE / diagonal, 0.0)


def gram_kernel(three, send, keep, held, sems):
    copies = [pltpu.make_async_copy(three.at[i], held.at[i], sems.at[i]) for i in range(2)]
    for copy in copies:
        copy.start()
    second = lax.axis_index("rep") == 1
    a, b = iota((WID, WID), 0), iota((WID, WID), 1)
    copies[0].wait()
    b0 = held[0]
    c00 = tdot(b0, b0)
    copies[1].wait()
    b1 = held[1]
    c01, c11 = tdot(b0, b1), tdot(b1, b1)
    packed = jnp.where(a <= b, c00, c11)
    diagonal = jnp.sum(jnp.where(a == b, c11, 0.0), axis=0, keepdims=True)
    diagonal = jnp.broadcast_to(diagonal, (PACK - WID, WID))

    @pl.when(jnp.logical_not(second))
    def _():
        keep[0:WID, :] = c01
        keep[WID:PACK, :] = jnp.zeros((PACK - WID, WID), F32)
        send[0:WID, :] = packed.astype(BF16)
        send[WID:PACK, :] = diagonal.astype(BF16)

    @pl.when(second)
    def _():
        keep[0:WID, :] = packed
        keep[WID:PACK, :] = diagonal
        send[0:WID, :] = c01.astype(BF16)
        send[WID:PACK, :] = jnp.zeros((PACK - WID, WID), BF16)


def prep_kernel(per, window, firsts, index, weights, hot, padded):
    padded[...] = jnp.zeros(padded.shape, F32)
    padded[0:3, :] = weights[...]
    lanes = iota((LANES, LANES), 1)
    for k in range(index.shape[0]):
        chunk = lax.div(firsts[k * LANES // SEG * SEG], per)
        relative = index[k : k + 1, :] - chunk * per
        column = relative
        for j in range(1, window):
            column = column + jnp.where(relative >= j * per, LANES - per, 0)
        turned = jnp.broadcast_to(column.astype(F32), (LANES, LANES)).T.astype(jnp.int32)
        for j in range(window):
            hot[pl.ds(k * LANES, LANES), pl.ds(j * LANES, LANES)] = (
                (turned == lanes + j * LANES).astype(F32).astype(BF16)
            )


def parts_of(own, other):
    first = lax.axis_index("rep") == 0
    return jnp.where(first, own[...], other[...]), jnp.where(first, other[...], own[...])


def weight_kernel(per, window, step, firsts, own, other, three, hot, padded, packs, stacked, terms):
    rows = three.shape[1]
    part0, part1 = parts_of(own, other)
    a, b = iota((WID, WID), 0), iota((WID, WID), 1)
    packed = part1[0:WID, :].astype(F32)
    diagonal = part1[WID : WID + 1, :].astype(F32)
    q00 = jnp.where(a < b, 2.0 * packed, jnp.where(a == b, packed, 0.0)).astype(BF16)
    q01 = (2.0 * part0[0:WID, :].astype(F32)).astype(BF16)
    q11 = jnp.where(a > b, 2.0 * packed, jnp.where(a == b, diagonal, 0.0)).astype(BF16)
    wide = jnp.concatenate([q00, q01], axis=1)
    terms[...] = jnp.zeros(terms.shape, F32)
    for k in range(rows // step):
        part = pl.ds(k * step, step)
        b0, b1 = three[0, part, :], three[1, part, :]
        left = jnp.dot(b0, wide, preferred_element_type=F32)
        right = jnp.dot(b1, q11, preferred_element_type=F32)
        product = left[:, 0:WID] * b0.astype(F32) + (left[:, WID:] + right) * b1.astype(F32)
        partial = product[:, 0:LANES] + product[:, LANES:WID]
        for q in range(step // LANES):
            weight = jnp.sum(partial[q * LANES : (q + 1) * LANES].T, axis=0, keepdims=True)
            lanes = pl.ds(k * step + q * LANES, LANES)
            term = padded[:, lanes] * weight
            high = term.astype(BF16).astype(F32)
            stacked[:, lanes] = jnp.concatenate([high, term - high], axis=0).astype(BF16)
    starts = range(0, rows, SEG)
    sums = []
    for start in starts:
        part = pl.ds(start, min(SEG, rows - start))
        both = jnp.dot(stacked[:, part], hot[part, :], preferred_element_type=F32)
        sums.append(both[0:8, :] + both[8:16, :])
    for start, value in zip(starts, sums):
        chunk = lax.div(firsts[start], per)
        for j in range(window):
            terms[chunk + j] += value[:, j * LANES : (j + 1) * LANES]
    for pair in range(packs.shape[0]):
        packs[pair, 0:4, :] = terms[2 * pair, 0:4, :]
        packs[pair, 4:8, :] = terms[2 * pair + 1, 0:4, :]


def gamma_kernel(begin, step, own, other, three, mine, *rest):
    gamma, kept, table, out, sems = rest[-5:]
    kept[...] = mine[...]
    part0, part1 = parts_of(own, other)
    a, b = iota((WID, WID), 0), iota((WID, WID), 1)
    t01 = part0[0:WID, :]
    packed = part1[0:WID, :]
    turned = packed.T.astype(F32)
    packed = packed.astype(F32)
    diagonal = part1[WID : WID + 1, :].astype(F32)
    table[0:WID, 0:WID] = jnp.where(a <= b, packed, turned).astype(BF16)
    table[0:WID, WID : 2 * WID] = t01
    table[WID : 2 * WID, 0:WID] = t01.T
    table[WID : 2 * WID, WID : 2 * WID] = jnp.where(a > b, packed, jnp.where(a == b, diagonal, turned)).astype(BF16)
    copies = []
    for k in range(out.shape[1] // step):
        source, target = pl.ds(begin + k * step, step), pl.ds(k * step, step)
        both = jnp.concatenate([three[0, source, :], three[1, source, :]], axis=1)
        g = jnp.dot(both, table[...], preferred_element_type=F32)
        out[0, target, :] = g[:, 0:WID].astype(BF16)
        out[1, target, :] = g[:, WID:].astype(BF16)
        copies.append(pltpu.make_async_copy(out.at[:, target, :], gamma.at[:, source, :], sems.at[k]))
        copies[-1].start()
    for copy in copies:
        copy.wait()


def swap(x, axis, bit):
    count = lax.axis_size(axis)
    return lax.ppermute(x, axis, [(i, i ^ bit) for i in range(count)])


def shards(
    three_index,
    valid_columns,
    domain_blocks,
    occupied_energy,
    virtual_energy,
    shell_index,
    centre_weights,
    *,
    shells,
):
    rows = three_index.shape[1]
    n_occ, n_aux, n_rep = lax.axis_size("occ"), lax.axis_size("aux"), lax.axis_size("rep")
    owners = n_occ * n_aux * n_rep
    per = shells // owners
    window = (per + SEG - 2) // per + 1
    vmem = pl.BlockSpec(memory_space=pltpu.VMEM)
    smem = pl.BlockSpec(memory_space=pltpu.SMEM)
    hbm = pl.BlockSpec(memory_space=pltpu.HBM)
    anywhere = pl.BlockSpec(memory_space=pl.ANY)

    def grant(mib):
        return pltpu.CompilerParams(vmem_limit_bytes=mib << 20)

    def cost(flops, size):
        return pl.CostEstimate(flops=flops, bytes_accessed=size, transcendentals=0)

    send, keep = pl.pallas_call(
        gram_kernel,
        out_shape=(jax.ShapeDtypeStruct((PACK, WID), BF16), jax.ShapeDtypeStruct((PACK, WID), F32)),
        in_specs=[hbm],
        out_specs=(vmem, vmem),
        scratch_shapes=[pltpu.VMEM(three_index.shape, BF16), pltpu.SemaphoreType.DMA((2,))],
        compiler_params=grant(52),
        cost_estimate=cost(6 * WID * WID * rows, 4 * WID * rows),
        name="gram",
    )(three_index)
    factor = pl.pallas_call(
        factor_kernel,
        out_shape=jax.ShapeDtypeStruct((PACK, WID), F32),
        in_specs=[smem, smem, smem, vmem],
        out_specs=vmem,
        compiler_params=grant(8),
        cost_estimate=cost(20 * WID * WID, 8 * WID * WID),
        name="factor",
    )(valid_columns, domain_blocks, occupied_energy, virtual_energy.reshape(-1, VBW))
    hot, padded = pl.pallas_call(
        functools.partial(prep_kernel, per, window),
        out_shape=(
            jax.ShapeDtypeStruct((rows, window * LANES), BF16),
            jax.ShapeDtypeStruct((8, rows), F32),
        ),
        in_specs=[smem, vmem, vmem],
        out_specs=(vmem, vmem),
        compiler_params=grant(12),
        cost_estimate=cost(4 * rows * window * LANES, 2 * rows * window * LANES),
        name="prep",
    )(shell_index, shell_index.reshape(-1, LANES), centre_weights)

    sums = keep + swap(send, "rep", 1).astype(F32)
    bit = 1
    while bit < n_aux:
        sums = sums + swap(sums.astype(BF16), "aux", bit).astype(F32)
        bit *= 2
    own = (sums * factor).astype(BF16)
    other = swap(own, "rep", 1)

    part = pl.pallas_call(
        functools.partial(weight_kernel, per, window, rows // 3),
        out_shape=jax.ShapeDtypeStruct((owners // 2, 8, LANES), F32),
        in_specs=[smem, vmem, vmem, vmem, vmem, vmem],
        out_specs=vmem,
        scratch_shapes=[pltpu.VMEM((16, rows), BF16), pltpu.VMEM((owners + window, 8, LANES), F32)],
        compiler_params=grant(16),
        cost_estimate=cost(6 * WID * WID * rows, 4 * WID * rows),
        name="weight",
    )(shell_index, own, other, three_index, hot, padded)

    steps = []
    for axis, count in (("occ", n_occ), ("aux", n_aux)):
        bit = count // 2
        while bit:
            steps.append((axis, bit))
            bit //= 2
    gamma = None
    pieces = 3
    for number, (axis, bit) in enumerate(steps):
        half = part.shape[0] // 2
        up = (lax.axis_index(axis) // bit) % 2
        mine = lax.dynamic_slice_in_dim(part, up * half, half, 0)
        theirs = lax.dynamic_slice_in_dim(part, (1 - up) * half, half, 0)
        if number < pieces:
            size = rows // pieces
            before = () if gamma is None else (gamma,)
            gamma, mine = pl.pallas_call(
                functools.partial(gamma_kernel, number * size, size // 2),
                out_shape=(
                    jax.ShapeDtypeStruct(three_index.shape, BF16),
                    jax.ShapeDtypeStruct(mine.shape, F32),
                ),
                in_specs=[vmem] * 4 + [hbm] * len(before),
                out_specs=(hbm, vmem),
                input_output_aliases={4: 0} if before else {},
                scratch_shapes=[
                    pltpu.VMEM((2 * WID, 2 * WID), BF16),
                    pltpu.VMEM((2, size, WID), BF16),
                    pltpu.SemaphoreType.DMA((2,)),
                ],
                compiler_params=grant(12),
                cost_estimate=cost(8 * WID * WID * size, 6 * WID * size),
                name="gamma",
            )(own, other, three_index, mine, *before)
        part = mine + swap(theirs, axis, bit)
    part = part[0] + swap(part, "rep", 1)[0]
    shell_gradient = lax.dynamic_slice(part, (4 * lax.axis_index("rep"), 0), (3, per))
    return gamma, shell_gradient


def solution(mesh):

    def whole(three_index, valid_columns, domain_blocks, occupied_energy, virtual_energy, shell_index, centre_weights):
        shells = three_index.shape[1] // 5
        return jax.shard_map(
            functools.partial(shards, shells=shells),
            mesh=mesh,
            in_specs=(
                P(("pose", "occ"), ("aux", "rep"), None),
                P(("pose", "occ")),
                P(("pose", "occ"), None),
                P(("pose", "occ")),
                P("pose"),
                P(("aux", "rep")),
                P(None, ("pose", "aux", "rep")),
            ),
            out_specs=(
                P(("pose", "occ"), ("aux", "rep"), None),
                P(None, ("pose", "occ", "aux", "rep")),
            ),
            check_vma=False,
        )(three_index, valid_columns, domain_blocks, occupied_energy, virtual_energy, shell_index, centre_weights)

    return whole
```

time: 38.3 us -> 29.2 us (0.76)
  waiting for transfers between devices: 13 us -> 6.77 us
  local copies, waits for them, and re-layouts: 4.91 us -> 0.64 us
  Pallas kernels: 8.85 us -> 10.6 us
    ppermute x7, waiting for transfers between devices: 13 us -> 6.77 us  [swap(): return lax.ppermute(x, axis, [(i, i ^ bit) for i in range(count)])]
    unnamed x16 -> x14, local copies, waits for them, and re-layouts: 4.3 us -> 0.03 us
    pallas_call x2 -> x7, Pallas kernels: 8.85 us -> 10.6 us  [the longest x3 4.09 us: shards(): pl.pallas_call(functools.partial(gamma_kernel, number * size, size // 2),...]
    dynamic_slice x0 -> x1, local copies, waits for them, and re-layouts: none -> 0.59 us  [shards(): lax.dynamic_slice(part, (4 * lax.axis_index('rep'), 0), (3, per))]
    squeeze x1 -> x0, local copies, waits for them, and re-layouts: 0.58 us -> none  [shards(): return (gamma, part[0, :3, :per])]
  transfers between devices with their start and end apart: 7 -> 7, of which waited for: 7 -> 6; matrix products, arithmetic and copies ran while one was open for 0% -> 0% of each run, Pallas kernels for 0% -> 21%
where the time goes in v2:
time: 29.2 us; the launch traced here: 29.1 us
  Pallas kernels  10.6 us (36%)
  starting transfers between devices  10.1 us (35%)
  waiting for transfers between devices  6.77 us (23%)
  between operations  0.87 us (3%)
  local copies, waits for them, and re-layouts  0.64 us (2%)
    ppermute x7, starting transfers between devices, swap(): return lax.ppermute(x, axis, [(i, i ^ bit) for i in range(count)])  10.1 us
    ppermute x7, waiting for transfers between devices, swap(): return lax.ppermute(x, axis, [(i, i ^ bit) for i in range(count)])  6.77 us
    pallas_call x3, Pallas kernels, shards(): pl.pallas_call(functools.partial(gamma_kernel, number * size, size // 2),...  4.09 us
    pallas_call x1, Pallas kernels, shards(): pl.pallas_call(gram_kernel, out_shape=(jax.ShapeDtypeStruct((PACK, WID),...  2.57 us
    pallas_call x1, Pallas kernels, shards(): pl.pallas_call(functools.partial(weight_kernel, per, window, rows // 3),...  1.97 us
    pallas_call x1, Pallas kernels, shards(): pl.pallas_call(functools.partial(prep_kernel, per, window), out_shape=(ja...  1.2 us
    pallas_call x1, Pallas kernels, shards(): pl.pallas_call(factor_kernel, out_shape=jax.ShapeDtypeStruct((PACK, WID),...  0.78 us
    dynamic_slice x1, local copies, waits for them, and re-layouts, shards(): lax.dynamic_slice(part, (4 * lax.axis_index('rep'), 0), (3, per))  0.59 us
  transfers between devices with their start and end apart: 7, of which 6 were waited for; matrix products, arithmetic and copies ran while one was open for 0% of the time, Pallas kernels for 21%

profile of v2, /device:TPU:0, one launch (start us, length us, event | category | flops | bytes accessed | tf_op | source)
XLA Modules:
  0.0 29.1 jit_solution(13511517972553791545)
XLA Ops:
  0.6 0.0 copy-start
  0.6 0.0 copy-start.2
  0.7 0.0 copy-start.6
  0.7 0.0 copy-start.5
  0.7 0.0 copy-start.4
  0.7 0.0 copy-start.1
  0.7 0.0 copy-start.3
  0.7 2.6 %gram.1 = (bf16[272,256]{1,0:T(8,128)(2,1)S(1)}, f32[272,256]{1,0:T(8,128)S(1)}) custom-call(bf16[2,1920,256]{2,1,0:T(8,128)(2,1)} %three.9), custom_call_target="tpu_custom_call" | custom-call | flops 754974720 | bytes 1966080 | tf_op jit(solution)/shard_map/gram/pallas_call | solution.py:209
  3.3 0.5 %collective-permute-start = (bf16[272,256]{1,0:T(8,128)(2,1)S(1)}, bf16[272,256]{1,0:T(8,128)(2,1)S(1)}, u32[]{:S(2)}, u32[]{:S(2)}) collective-permute-start(bf16[272,256]{1,0:T(8,128)(2,1)S(1)} %get-tuple-element.13), channel_id=1, source_target_pairs={{0,1},{1,0},{2,3},{3,2},{4,5},{5,4},{6,7},{7,6},{8,9},{9,8},{10,11... | collective-permute-start | bytes 417800 | tf_op jit(solution)/shard_map/ppermute | solution.py:179
  3.8 1.0 %collective-permute-done = bf16[272,256]{1,0:T(8,128)(2,1)S(1)} collective-permute-done((bf16[272,256]{1,0:T(8,128)(2,1)S(1)}, bf16[272,256]{1,0:T(8,128)(2,1)S(1)}, u32[]{:S(2)}, u32[]{:S(2)}) %collective-permute-start) | collective-permute-done | bytes 139296 | tf_op jit(solution)/shard_map/ppermute | solution.py:179
  4.8 2.9 %collective-permute-start.1 = (bf16[272,256]{1,0:T(8,128)(2,1)S(1)}, bf16[272,256]{1,0:T(8,128)(2,1)S(1)}, u32[]{:S(2)}, u32[]{:S(2)}) collective-permute-start(bf16[272,256]{1,0:T(8,128)(2,1)S(1)} %fusion), channel_id=1, source_target_pairs={{0,2},{2,0},{1,3},{3,1},{4,6},{6,4},{5,7},{7,5},{8,10},{10,8},{9,1... | collective-permute-start | bytes 417800 | tf_op jit(solution)/shard_map/ppermute | solution.py:179
  7.7 0.0 copy-done.2
  7.8 0.0 copy-done.5
  7.8 0.8 %factor.1 = f32[272,256]{1,0:T(8,128)S(1)} custom-call(s32[2]{0:T(128)S(1)} %copy-done.5, s32[2,2]{1,0:T(2,128)S(1)} %copy-done.4, f32[2]{0:T(128)S(1)} %copy-done.6, f32[64,128]{1,0:T(8,128)S(1)} %bitcast.5), custom_call_target="tpu_custom_call" | custom-call | flops 1310720 | bytes 524288 | tf_op jit(solution)/shard_map/factor/pallas_call | solution.py:219
  8.6 3.2 %collective-permute-done.1 = bf16[272,256]{1,0:T(8,128)(2,1)S(1)} collective-permute-done((bf16[272,256]{1,0:T(8,128)(2,1)S(1)}, bf16[272,256]{1,0:T(8,128)(2,1)S(1)}, u32[]{:S(2)}, u32[]{:S(2)}) %collective-permute-start.1) | collective-permute-done | bytes 139296 | tf_op jit(solution)/shard_map/ppermute | solution.py:179
  11.7 0.1 multiply_convert_fusion.own
  11.8 0.1 collective-permute-start.2
  12.0 1.2 %prep.1 = (bf16[1920,512]{1,0:T(8,128)(2,1)S(1)}, f32[8,1920]{1,0:T(8,128)S(1)}) custom-call(s32[1920]{0:T(1024)S(1)} %copy-done.1, s32[15,128]{1,0:T(8,128)S(1)} %bitcast.4, f32[3,1920]{1,0:T(4,128)S(1)} %copy-done.3), custom_call_target="tpu_custom_call" | custom-call | flops 3932160 | bytes 1966080 | tf_op jit(solution)/shard_map/prep/pallas_call | solution.py:228
  13.2 0.0 collective-permute-done.2.other
  13.2 2.0 %weight.1 = f32[8,8,128]{2,1,0:T(8,128)S(1)} custom-call(s32[1920]{0:T(1024)S(1)} %copy-done.1, bf16[272,256]{1,0:T(8,128)(2,1)S(1)} %multiply_convert_fusion.own, bf16[272,256]{1,0:T(8,128)(2,1)S(1)} %collective-permute-done.2.other, bf16[2,1920,256]{2,1,0:T(8,128)(2,1)S(1)} %copy-done, bf16[1920,512]{1,0:T(8,128)(2,1)S(1)} %get-tuple-element.14.hot, ...), custom_call_target="tpu_custom_call" | custom-call | flops 754974720 | bytes 1966080 | tf_op jit(solution)/shard_map/weight/pallas_call | solution.py:249
  15.2 2.9 %collective-permute-start.3 = (f32[4,8,128]{2,1,0:T(8,128)S(1)}, f32[4,8,128]{2,1,0:T(8,128)S(1)}, u32[]{:S(2)}, u32[]{:S(2)}) collective-permute-start(f32[4,8,128]{2,1,0:T(8,128)S(1)} %get-tuple-element.22), channel_id=1, source_target_pairs={{0,8},{4,12},{8,0},{12,4},{1,9},{5,13},{9,1},{13,5},{2,10},{6,14},... | collective-permute-start | bytes 49160 | tf_op jit(solution)/shard_map/ppermute | solution.py:179
  18.2 1.4 %gamma.3 = (bf16[2,1920,256]{2,1,0:T(8,128)(2,1)}, f32[4,8,128]{2,1,0:T(8,128)S(1)}) custom-call(bf16[272,256]{1,0:T(8,128)(2,1)S(1)} %multiply_convert_fusion.own, bf16[272,256]{1,0:T(8,128)(2,1)S(1)} %collective-permute-done.2.other, bf16[2,1920,256]{2,1,0:T(8,128)(2,1)S(1)} %copy-done, f32[4,8,128]{2,1,0:T(8,128)S(1)} %get-tuple-element.23.mine), custom_call_target="tpu_custom_call" | custom-call | flops 335544320 | bytes 983040 | tf_op jit(solution)/shard_map/gamma/pallas_call | solution.py:276
  19.5 0.4 %collective-permute-done.3 = f32[4,8,128]{2,1,0:T(8,128)S(1)} collective-permute-done((f32[4,8,128]{2,1,0:T(8,128)S(1)}, f32[4,8,128]{2,1,0:T(8,128)S(1)}, u32[]{:S(2)}, u32[]{:S(2)}) %collective-permute-start.3) | collective-permute-done | bytes 16416 | tf_op jit(solution)/shard_map/ppermute | solution.py:179
  20.0 1.9 %collective-permute-start.4 = (f32[2,8,128]{2,1,0:T(8,128)S(1)}, f32[2,8,128]{2,1,0:T(8,128)S(1)}, u32[]{:S(2)}, u32[]{:S(2)}) collective-permute-start(f32[2,8,128]{2,1,0:T(8,128)S(1)} %get-tuple-element.24), channel_id=1, source_target_pairs={{0,4},{4,0},{8,12},{12,8},{1,5},{5,1},{9,13},{13,9},{2,6},{6,2},{1... | collective-permute-start | bytes 24584 | tf_op jit(solution)/shard_map/ppermute | solution.py:179
  21.9 1.4 %gamma.4 = (bf16[2,1920,256]{2,1,0:T(8,128)(2,1)}, f32[2,8,128]{2,1,0:T(8,128)S(1)}) custom-call(bf16[272,256]{1,0:T(8,128)(2,1)S(1)} %multiply_convert_fusion.own, bf16[272,256]{1,0:T(8,128)(2,1)S(1)} %collective-permute-done.2.other, bf16[2,1920,256]{2,1,0:T(8,128)(2,1)S(1)} %copy-done, ...), custom_call_target="tpu_custom_call", output_to_operand_aliasing={{0}: (4, {})} | custom-call | flops 335544320 | bytes 983040 | tf_op jit(solution)/shard_map/gamma/pallas_call | solution.py:276
  23.2 0.5 %collective-permute-done.4 = f32[2,8,128]{2,1,0:T(8,128)S(1)} collective-permute-done((f32[2,8,128]{2,1,0:T(8,128)S(1)}, f32[2,8,128]{2,1,0:T(8,128)S(1)}, u32[]{:S(2)}, u32[]{:S(2)}) %collective-permute-start.4) | collective-permute-done | bytes 8224 | tf_op jit(solution)/shard_map/ppermute | solution.py:179
  23.7 1.7 %collective-permute-start.5 = (f32[1,8,128]{2,1,0:T(8,128)S(1)}, f32[1,8,128]{2,1,0:T(8,128)S(1)}, u32[]{:S(2)}, u32[]{:S(2)}) collective-permute-start(f32[1,8,128]{2,1,0:T(8,128)S(1)} %get-tuple-element.26), channel_id=1, source_target_pairs={{0,2},{2,0},{1,3},{3,1},{4,6},{6,4},{5,7},{7,5},{8,10},{10,8},{9,1... | collective-permute-start | bytes 12296 | tf_op jit(solution)/shard_map/ppermute | solution.py:179
  25.4 1.4 %gamma.5 = (bf16[2,1920,256]{2,1,0:T(8,128)(2,1)}, f32[1,8,128]{2,1,0:T(8,128)S(1)}) custom-call(bf16[272,256]{1,0:T(8,128)(2,1)S(1)} %multiply_convert_fusion.own, bf16[272,256]{1,0:T(8,128)(2,1)S(1)} %collective-permute-done.2.other, bf16[2,1920,256]{2,1,0:T(8,128)(2,1)S(1)} %copy-done, ...), custom_call_target="tpu_custom_call", output_to_operand_aliasing={{0}: (4, {})} | custom-call | flops 335544320 | bytes 983040 | tf_op jit(solution)/shard_map/gamma/pallas_call | solution.py:276
  26.8 0.5 %collective-permute-done.5 = f32[1,8,128]{2,1,0:T(8,128)S(1)} collective-permute-done((f32[1,8,128]{2,1,0:T(8,128)S(1)}, f32[1,8,128]{2,1,0:T(8,128)S(1)}, u32[]{:S(2)}, u32[]{:S(2)}) %collective-permute-start.5) | collective-permute-done | bytes 4128 | tf_op jit(solution)/shard_map/ppermute | solution.py:179
  27.3 0.0 collective-permute-start.6
  27.3 1.2 %collective-permute-done.6 = f32[1,8,128]{2,1,0:T(8,128)S(1)} collective-permute-done((f32[1,8,128]{2,1,0:T(8,128)S(1)}, f32[1,8,128]{2,1,0:T(8,128)S(1)}, u32[]{:S(2)}, u32[]{:S(2)}) %collective-permute-start.6) | collective-permute-done | bytes 4128 | tf_op jit(solution)/shard_map/ppermute | solution.py:179
  28.5 0.6 %dynamic-slice_bitcast_fusion = f32[3,96]{1,0:T(4,128)} fusion(f32[1,8,128]{2,1,0:T(8,128)S(1)} %add.68, s32[]{:T(128)S(6)} %select_n.52), kind=kLoop, calls=%fused_computation.3 | loop fusion | bytes 2308 | tf_op jit(solution)/shard_map/dynamic_slice | solution.py:296
  (13 shorter events, 0.1 us)
Async XLA Ops:
  0.6 12.6 %copy-start = (bf16[2,1920,256]{2,1,0:T(8,128)(2,1)S(1)}, bf16[2,1920,256]{2,1,0:T(8,128)(2,1)}, u32[]{:S(2)}) copy-start(bf16[2,1920,256]{2,1,0:T(8,128)(2,1)} %three.9) | copy-start | bytes 5898244
  0.6 7.1 %copy-start.2 = (f32[8192]{0:T(1024)S(1)}, f32[8192]{0:T(1024)}, u32[]{:S(2)}) copy-start(f32[8192]{0:T(1024)} %param.11) | copy-start | bytes 98308
  0.7 7.1 %copy-start.6 = (f32[2]{0:T(128)S(1)}, f32[2]{0:T(128)}, u32[]{:S(2)}) copy-start(f32[2]{0:T(128)} %occupied.1) | copy-start | bytes 28
  0.7 7.1 %copy-start.5 = (s32[2]{0:T(128)S(1)}, s32[2]{0:T(128)}, u32[]{:S(2)}) copy-start(s32[2]{0:T(128)} %valid.1) | copy-start | bytes 28
  0.7 7.1 %copy-start.4 = (s32[2,2]{1,0:T(2,128)S(1)}, s32[2,2]{1,0:T(2,128)}, u32[]{:S(2)}) copy-start(s32[2,2]{1,0:T(2,128)} %blocks.1) | copy-start | bytes 52
  0.7 11.3 %copy-start.1 = (s32[1920]{0:T(1024)S(1)}, s32[1920]{0:T(1024)}, u32[]{:S(2)}) copy-start(s32[1920]{0:T(1024)} %firsts.3) | copy-start | bytes 23044
  0.7 11.3 %copy-start.3 = (f32[3,1920]{1,0:T(4,128)S(1)}, f32[3,1920]{1,0:T(4,128)}, u32[]{:S(2)}) copy-start(f32[3,1920]{1,0:T(4,128)} %weights.1) | copy-start | bytes 69124
  3.3 1.5 %collective-permute-start = (bf16[272,256]{1,0:T(8,128)(2,1)S(1)}, bf16[272,256]{1,0:T(8,128)(2,1)S(1)}, u32[]{:S(2)}, u32[]{:S(2)}) collective-permute-start(bf16[272,256]{1,0:T(8,128)(2,1)S(1)} %get-tuple-element.13), channel_id=1, source_target_pairs={{0,1},{1,0},{2,3},{3,2},{4,5},{5,4},{6,7},{7,6},{8,9},{9,8},{10,11... | collective-permute-start | bytes 417800 | tf_op jit(solution)/shard_map/ppermute | solution.py:179
  4.8 6.9 %collective-permute-start.1 = (bf16[272,256]{1,0:T(8,128)(2,1)S(1)}, bf16[272,256]{1,0:T(8,128)(2,1)S(1)}, u32[]{:S(2)}, u32[]{:S(2)}) collective-permute-start(bf16[272,256]{1,0:T(8,128)(2,1)S(1)} %fusion), channel_id=1, source_target_pairs={{0,2},{2,0},{1,3},{3,1},{4,6},{6,4},{5,7},{7,5},{8,10},{10,8},{9,1... | collective-permute-start | bytes 417800 | tf_op jit(solution)/shard_map/ppermute | solution.py:179
  11.8 1.4 %collective-permute-start.2 = (bf16[272,256]{1,0:T(8,128)(2,1)S(1)}, bf16[272,256]{1,0:T(8,128)(2,1)S(1)}, u32[]{:S(2)}, u32[]{:S(2)}) collective-permute-start(bf16[272,256]{1,0:T(8,128)(2,1)S(1)} %multiply_convert_fusion.own), channel_id=1, source_target_pairs={{0,1},{1,0},{2,3},{3,2},{4,5},{5,4},{6,7},{7,6},{8,9},{9,8},{10,11... | collective-permute-start | bytes 417800 | tf_op jit(solution)/shard_map/ppermute | solution.py:179
  15.2 4.7 %collective-permute-start.3 = (f32[4,8,128]{2,1,0:T(8,128)S(1)}, f32[4,8,128]{2,1,0:T(8,128)S(1)}, u32[]{:S(2)}, u32[]{:S(2)}) collective-permute-start(f32[4,8,128]{2,1,0:T(8,128)S(1)} %get-tuple-element.22), channel_id=1, source_target_pairs={{0,8},{4,12},{8,0},{12,4},{1,9},{5,13},{9,1},{13,5},{2,10},{6,14},... | collective-permute-start | bytes 49160 | tf_op jit(solution)/shard_map/ppermute | solution.py:179
  20.0 3.7 %collective-permute-start.4 = (f32[2,8,128]{2,1,0:T(8,128)S(1)}, f32[2,8,128]{2,1,0:T(8,128)S(1)}, u32[]{:S(2)}, u32[]{:S(2)}) collective-permute-start(f32[2,8,128]{2,1,0:T(8,128)S(1)} %get-tuple-element.24), channel_id=1, source_target_pairs={{0,4},{4,0},{8,12},{12,8},{1,5},{5,1},{9,13},{13,9},{2,6},{6,2},{1... | collective-permute-start | bytes 24584 | tf_op jit(solution)/shard_map/ppermute | solution.py:179
  23.7 3.6 %collective-permute-start.5 = (f32[1,8,128]{2,1,0:T(8,128)S(1)}, f32[1,8,128]{2,1,0:T(8,128)S(1)}, u32[]{:S(2)}, u32[]{:S(2)}) collective-permute-start(f32[1,8,128]{2,1,0:T(8,128)S(1)} %get-tuple-element.26), channel_id=1, source_target_pairs={{0,2},{2,0},{1,3},{3,1},{4,6},{6,4},{5,7},{7,5},{8,10},{10,8},{9,1... | collective-permute-start | bytes 12296 | tf_op jit(solution)/shard_map/ppermute | solution.py:179
  27.3 1.2 %collective-permute-start.6 = (f32[1,8,128]{2,1,0:T(8,128)S(1)}, f32[1,8,128]{2,1,0:T(8,128)S(1)}, u32[]{:S(2)}, u32[]{:S(2)}) collective-permute-start(f32[1,8,128]{2,1,0:T(8,128)S(1)} %add.67), channel_id=1, source_target_pairs={{0,1},{1,0},{2,3},{3,2},{4,5},{5,4},{6,7},{7,6},{8,9},{9,8},{10,11... | collective-permute-start | bytes 12296 | tf_op jit(solution)/shard_map/ppermute | solution.py:179

commit v3 on v2

--- a/solution.py
+++ b/solution.py
@@ -25,7 +25,7 @@
     return lax.dot_general(x, y, (((0,), (0,)), ((), ())), preferred_element_type=F32)
 
 
-def factor_kernel(valid, blocks, occupied, energies, factor):
+def make_factor(valid, blocks, occupied, energies, factor):
     second = lax.axis_index("rep") == 1
     virtual = [
         jnp.concatenate([energies[pl.ds(blocks[i, d], 1), :] for d in range(DOM)], axis=1) for i in range(2)
@@ -55,91 +55,133 @@
         factor[WID:PACK, :] = jnp.where(inside, OPPOSITE_SCALE / diagonal, 0.0)
 
 
-def gram_kernel(three, send, keep, held, sems):
-    copies = [pltpu.make_async_copy(three.at[i], held.at[i], sems.at[i]) for i in range(2)]
-    for copy in copies:
-        copy.start()
-    second = lax.axis_index("rep") == 1
-    a, b = iota((WID, WID), 0), iota((WID, WID), 1)
-    copies[0].wait()
-    b0 = held[0]
-    c00 = tdot(b0, b0)
-    copies[1].wait()
-    b1 = held[1]
-    c01, c11 = tdot(b0, b1), tdot(b1, b1)
-    packed = jnp.where(a <= b, c00, c11)
-    diagonal = jnp.sum(jnp.where(a == b, c11, 0.0), axis=0, keepdims=True)
-    diagonal = jnp.broadcast_to(diagonal, (PACK - WID, WID))
+def gram_part(second, pieces, held, out, ready=lambda k: None):
+    step = held.shape[1] // pieces
+
+    def total(pairs):
+        sums = None
+        for k in range(pieces):
+            ready(k)
+            rows = pl.ds(k * step, step)
+            terms = [tdot(held[i, rows, :], held[j, rows, :]) for i, j in pairs]
+            sums = terms if sums is None else [x + y for x, y in zip(sums, terms)]
+        return sums
 
     @pl.when(jnp.logical_not(second))
     def _():
-        keep[0:WID, :] = c01
-        keep[WID:PACK, :] = jnp.zeros((PACK - WID, WID), F32)
-        send[0:WID, :] = packed.astype(BF16)
-        send[WID:PACK, :] = diagonal.astype(BF16)
+        (c01,) = total([(0, 1)])
+        out[0:WID, :] = c01.astype(out.dtype)
+        out[WID:PACK, :] = jnp.zeros((PACK - WID, WID), out.dtype)
 
     @pl.when(second)
     def _():
-        keep[0:WID, :] = packed
-        keep[WID:PACK, :] = diagonal
-        send[0:WID, :] = c01.astype(BF16)
-        send[WID:PACK, :] = jnp.zeros((PACK - WID, WID), BF16)
-
-
-def prep_kernel(per, window, firsts, index, weights, hot, padded):
+        a, b = iota((WID, WID), 0), iota((WID, WID), 1)
+        c00, c11 = total([(0, 0), (1, 1)])
+        diagonal = jnp.sum(jnp.where(a == b, c11, 0.0), axis=0, keepdims=True)
+        out[0:WID, :] = jnp.where(a <= b, c00, c11).astype(out.dtype)
+        out[WID:PACK, :] = jnp.broadcast_to(diagonal, (PACK - WID, WID)).astype(out.dtype)
+
+
+def send_kernel(pieces, three, send, held, sems):
+    step = three.shape[1] // pieces
+    copies = []
+    for k in range(pieces):
+        rows = pl.ds(k * step, step)
+        copies.append(pltpu.make_async_copy(three.at[:, rows, :], held.at[:, rows, :], sems.at[k]))
+        copies[-1].start()
+    gram_part(lax.axis_index("rep") == 0, pieces, held, send, lambda k: copies[k].wait())
+
+
+def keep_kernel(held, keep):
+    gram_part(lax.axis_index("rep") == 1, 1, held, keep)
+
+
+def prep_kernel(
+    per, window, valid, blocks, occupied, energies, firsts, index, weights, factor, columns, padded, starts
+):
+    make_factor(valid, blocks, occupied, energies, factor)
     padded[...] = jnp.zeros(padded.shape, F32)
     padded[0:3, :] = weights[...]
-    lanes = iota((LANES, LANES), 1)
     for k in range(index.shape[0]):
-        chunk = lax.div(firsts[k * LANES // SEG * SEG], per)
+        block = k * LANES // SEG
+        chunk = lax.div(firsts[block * SEG], per)
+        starts[block : block + 1, :] = jnp.full((1, LANES), chunk, jnp.int32)
         relative = index[k : k + 1, :] - chunk * per
         column = relative
         for j in range(1, window):
             column = column + jnp.where(relative >= j * per, LANES - per, 0)
-        turned = jnp.broadcast_to(column.astype(F32), (LANES, LANES)).T.astype(jnp.int32)
+        columns[k : k + 1, :] = column
+
+
+def parts_of(own, other):
+    first = lax.axis_index("rep") == 0
+    return jnp.where(first, own[...], other[...]), jnp.where(first, other[...], own[...])
+
+
+def quadratic(second, part, three, step, emit):
+    blocks = range(0, three.shape[1], step)
+    a, b = iota((WID, WID), 0), iota((WID, WID), 1)
+
+    @pl.when(jnp.logical_not(second))
+    def _():
+        form = (2.0 * part[0:WID, :].astype(F32)).astype(BF16)
+        for k in blocks:
+            b0, b1 = three[0, pl.ds(k, step), :], three[1, pl.ds(k, step), :]
+            product = jnp.dot(b0, form, preferred_element_type=F32) * b1.astype(F32)
+            emit(k, product[:, 0:LANES] + product[:, LANES:WID])
+
+    @pl.when(second)
+    def _():
+        packed = part[0:WID, :].astype(F32)
+        diagonal = part[WID:PACK, :].astype(F32)[0:1, :]
+        form0 = jnp.where(a < b, 2.0 * packed, jnp.where(a == b, packed, 0.0)).astype(BF16)
+        form1 = jnp.where(a > b, 2.0 * packed, jnp.where(a == b, diagonal, 0.0)).astype(BF16)
+        for k in blocks:
+            b0, b1 = three[0, pl.ds(k, step), :], three[1, pl.ds(k, step), :]
+            product = jnp.dot(b0, form0, preferred_element_type=F32) * b0.astype(F32)
+            product += jnp.dot(b1, form1, preferred_element_type=F32) * b1.astype(F32)
+            emit(k, product[:, 0:LANES] + product[:, LANES:WID])
+
+
+def ahead_kernel(step, window, own, three, columns, ahead, hot):
+    lanes = iota((LANES, LANES), 1)
+    for k in range(columns.shape[0]):
+        turned = jnp.broadcast_to(columns[k : k + 1, :].astype(F32), (LANES, LANES)).T.astype(jnp.int32)
         for j in range(window):
             hot[pl.ds(k * LANES, LANES), pl.ds(j * LANES, LANES)] = (
                 (turned == lanes + j * LANES).astype(F32).astype(BF16)
             )
 
-
-def parts_of(own, other):
-    first = lax.axis_index("rep") == 0
-    return jnp.where(first, own[...], other[...]), jnp.where(first, other[...], own[...])
-
-
-def weight_kernel(per, window, step, firsts, own, other, three, hot, padded, packs, stacked, terms):
+    def emit(k, partial):
+        ahead[pl.ds(k, step), :] = partial
+
+    quadratic(lax.axis_index("rep") == 1, own, three, step, emit)
+
+
+def weight_kernel(window, step, starts, other, ahead, three, hot, padded, packs, stacked, terms, chunks, sem):
     rows = three.shape[1]
-    part0, part1 = parts_of(own, other)
-    a, b = iota((WID, WID), 0), iota((WID, WID), 1)
-    packed = part1[0:WID, :].astype(F32)
-    diagonal = part1[WID : WID + 1, :].astype(F32)
-    q00 = jnp.where(a < b, 2.0 * packed, jnp.where(a == b, packed, 0.0)).astype(BF16)
-    q01 = (2.0 * part0[0:WID, :].astype(F32)).astype(BF16)
-    q11 = jnp.where(a > b, 2.0 * packed, jnp.where(a == b, diagonal, 0.0)).astype(BF16)
-    wide = jnp.concatenate([q00, q01], axis=1)
+    copy = pltpu.make_async_copy(starts, chunks, sem)
+    copy.start()
     terms[...] = jnp.zeros(terms.shape, F32)
-    for k in range(rows // step):
-        part = pl.ds(k * step, step)
-        b0, b1 = three[0, part, :], three[1, part, :]
-        left = jnp.dot(b0, wide, preferred_element_type=F32)
-        right = jnp.dot(b1, q11, preferred_element_type=F32)
-        product = left[:, 0:WID] * b0.astype(F32) + (left[:, WID:] + right) * b1.astype(F32)
-        partial = product[:, 0:LANES] + product[:, LANES:WID]
-        for q in range(step // LANES):
-            weight = jnp.sum(partial[q * LANES : (q + 1) * LANES].T, axis=0, keepdims=True)
-            lanes = pl.ds(k * step + q * LANES, LANES)
+
+    def emit(k, partial):
+        partial = partial + ahead[pl.ds(k, step), :]
+        for q in range(0, step, LANES):
+            weight = jnp.sum(partial[q : q + LANES].T, axis=0, keepdims=True)
+            lanes = pl.ds(k + q, LANES)
             term = padded[:, lanes] * weight
             high = term.astype(BF16).astype(F32)
             stacked[:, lanes] = jnp.concatenate([high, term - high], axis=0).astype(BF16)
-    starts = range(0, rows, SEG)
+
+    quadratic(lax.axis_index("rep") == 0, other, three, step, emit)
     sums = []
-    for start in starts:
+    for start in range(0, rows, SEG):
         part = pl.ds(start, min(SEG, rows - start))
         both = jnp.dot(stacked[:, part], hot[part, :], preferred_element_type=F32)
         sums.append(both[0:8, :] + both[8:16, :])
-    for start, value in zip(starts, sums):
-        chunk = lax.div(firsts[start], per)
+    copy.wait()
+    for block, value in enumerate(sums):
+        chunk = chunks[block, 0]
         for j in range(window):
             terms[chunk + j] += value[:, j * LANES : (j + 1) * LANES]
     for pair in range(packs.shape[0]):
@@ -206,37 +248,47 @@
     def cost(flops, size):
         return pl.CostEstimate(flops=flops, bytes_accessed=size, transcendentals=0)
 
-    send, keep = pl.pallas_call(
-        gram_kernel,
-        out_shape=(jax.ShapeDtypeStruct((PACK, WID), BF16), jax.ShapeDtypeStruct((PACK, WID), F32)),
+    send, held = pl.pallas_call(
+        functools.partial(send_kernel, 4),
+        out_shape=(jax.ShapeDtypeStruct((PACK, WID), BF16), jax.ShapeDtypeStruct(three_index.shape, BF16)),
         in_specs=[hbm],
         out_specs=(vmem, vmem),
-        scratch_shapes=[pltpu.VMEM(three_index.shape, BF16), pltpu.SemaphoreType.DMA((2,))],
-        compiler_params=grant(52),
-        cost_estimate=cost(6 * WID * WID * rows, 4 * WID * rows),
-        name="gram",
+        scratch_shapes=[pltpu.SemaphoreType.DMA((4,))],
+        compiler_params=grant(51),
+        cost_estimate=cost(4 * WID * WID * rows, 4 * WID * rows),
+        name="send",
     )(three_index)
-    factor = pl.pallas_call(
-        factor_kernel,
+    keep = pl.pallas_call(
+        keep_kernel,
         out_shape=jax.ShapeDtypeStruct((PACK, WID), F32),
-        in_specs=[smem, smem, smem, vmem],
+        in_specs=[vmem],
         out_specs=vmem,
-        compiler_params=grant(8),
-        cost_estimate=cost(20 * WID * WID, 8 * WID * WID),
-        name="factor",
-    )(valid_columns, domain_blocks, occupied_energy, virtual_energy.reshape(-1, VBW))
-    hot, padded = pl.pallas_call(
+        compiler_params=grant(16),
+        cost_estimate=cost(4 * WID * WID * rows, 4 * WID * rows),
+        name="keep",
+    )(held)
+    factor, columns, padded, starts = pl.pallas_call(
         functools.partial(prep_kernel, per, window),
         out_shape=(
-            jax.ShapeDtypeStruct((rows, window * LANES), BF16),
+            jax.ShapeDtypeStruct((PACK, WID), F32),
+            jax.ShapeDtypeStruct((rows // LANES, LANES), jnp.int32),
             jax.ShapeDtypeStruct((8, rows), F32),
+            jax.ShapeDtypeStruct((8, LANES), jnp.int32),
         ),
-        in_specs=[smem, vmem, vmem],
-        out_specs=(vmem, vmem),
-        compiler_params=grant(12),
+        in_specs=[smem, smem, smem, vmem, smem, vmem, vmem],
+        out_specs=(vmem,) * 4,
+        compiler_params=grant(16),
         cost_estimate=cost(4 * rows * window * LANES, 2 * rows * window * LANES),
         name="prep",
-    )(shell_index, shell_index.reshape(-1, LANES), centre_weights)
+    )(
+        valid_columns,
+        domain_blocks,
+        occupied_energy,
+        virtual_energy.reshape(-1, VBW),
+        shell_index,
+        shell_index.reshape(-1, LANES),
+        centre_weights,
+    )
 
     sums = keep + swap(send, "rep", 1).astype(F32)
     bit = 1
@@ -246,16 +298,34 @@
     own = (sums * factor).astype(BF16)
     other = swap(own, "rep", 1)
 
+    step = rows // 3
+    ahead, hot = pl.pallas_call(
+        functools.partial(ahead_kernel, step, window),
+        out_shape=(
+            jax.ShapeDtypeStruct((rows, LANES), F32),
+            jax.ShapeDtypeStruct((rows, window * LANES), BF16),
+        ),
+        in_specs=[vmem] * 3,
+        out_specs=(vmem, vmem),
+        compiler_params=grant(16),
+        cost_estimate=cost(4 * WID * WID * rows, 4 * WID * rows),
+        name="ahead",
+    )(own, held, columns)
     part = pl.pallas_call(
-        functools.partial(weight_kernel, per, window, rows // 3),
+        functools.partial(weight_kernel, window, step),
         out_shape=jax.ShapeDtypeStruct((owners // 2, 8, LANES), F32),
-        in_specs=[smem, vmem, vmem, vmem, vmem, vmem],
+        in_specs=[vmem] * 6,
         out_specs=vmem,
-        scratch_shapes=[pltpu.VMEM((16, rows), BF16), pltpu.VMEM((owners + window, 8, LANES), F32)],
+        scratch_shapes=[
+            pltpu.VMEM((16, rows), BF16),
+            pltpu.VMEM((owners + window, 8, LANES), F32),
+            pltpu.SMEM((8, LANES), jnp.int32),
+            pltpu.SemaphoreType.DMA,
+        ],
         compiler_params=grant(16),
-        cost_estimate=cost(6 * WID * WID * rows, 4 * WID * rows),
+        cost_estimate=cost(4 * WID * WID * rows, 4 * WID * rows),
         name="weight",
-    )(shell_index, own, other, three_index, hot, padded)
+    )(starts, other, ahead, held, hot, padded)
 
     steps = []
     for axis, count in (("occ", n_occ), ("aux", n_aux)):
@@ -290,7 +360,7 @@
                 compiler_params=grant(12),
                 cost_estimate=cost(8 * WID * WID * size, 6 * WID * size),
                 name="gamma",
-            )(own, other, three_index, mine, *before)
+            )(own, other, held, mine, *before)
         part = mine + swap(theirs, axis, bit)
     part = part[0] + swap(part, "rep", 1)[0]
     shell_gradient = lax.dynamic_slice(part, (4 * lax.axis_index("rep"), 0), (3, per))

time: 29.2 us -> 28.1 us (0.962)
  Pallas kernels: 10.6 us -> 9.92 us
  waiting for transfers between devices: 6.77 us -> 6.35 us
    pallas_call x3 -> x4, Pallas kernels: 5.32 us -> 4.88 us  [the longest x1 2.18 us: shards(): pl.pallas_call(functools.partial(send_kernel, 4), out_shape=(jax.ShapeDty...]
    ppermute x7, waiting for transfers between devices: 6.77 us -> 6.35 us  [swap(): return lax.ppermute(x, axis, [(i, i ^ bit) for i in range(count)])]
  transfers between devices with their start and end apart: 7 -> 7, of which waited for: 6 -> 7; matrix products, arithmetic and copies ran while one was open for 0% -> 0% of each run, Pallas kernels for 21% -> 23%
where the time goes in v3:
time: 28.1 us; the launch traced here: 27.9 us
  starting transfers between devices  10 us (36%)
  Pallas kernels  9.92 us (35%)
  waiting for transfers between devices  6.35 us (23%)
  between operations  0.87 us (3%)
  local copies, waits for them, and re-layouts  0.63 us (2%)
    ppermute x7, starting transfers between devices, swap(): return lax.ppermute(x, axis, [(i, i ^ bit) for i in range(count)])  10 us
    ppermute x7, waiting for transfers between devices, swap(): return lax.ppermute(x, axis, [(i, i ^ bit) for i in range(count)])  6.35 us
    pallas_call x3, Pallas kernels, shards(): pl.pallas_call(functools.partial(gamma_kernel, number * size, size // 2),...  4.09 us
    pallas_call x1, Pallas kernels, shards(): pl.pallas_call(functools.partial(send_kernel, 4), out_shape=(jax.ShapeDty...  2.18 us
    pallas_call x1, Pallas kernels, shards(): pl.pallas_call(functools.partial(weight_kernel, window, step), out_shape=...  1.27 us
    pallas_call x1, Pallas kernels, shards(): pl.pallas_call(functools.partial(ahead_kernel, step, window), out_shape=(...  0.95 us
    pallas_call x1, Pallas kernels, shards(): pl.pallas_call(functools.partial(prep_kernel, per, window), out_shape=(ja...  0.94 us
    dynamic_slice x1, local copies, waits for them, and re-layouts, shards(): lax.dynamic_slice(part, (4 * lax.axis_index('rep'), 0), (3, per))  0.59 us
  transfers between devices with their start and end apart: 7, of which 7 were waited for; matrix products, arithmetic and copies ran while one was open for 0% of the time, Pallas kernels for 23%

profile of v3, /device:TPU:0, one launch (start us, length us, event | category | flops | bytes accessed | tf_op | source)
XLA Modules:
  0.0 27.9 jit_solution(16488953789388850323)
XLA Ops:
  0.6 0.0 copy-start.1
  0.6 0.0 copy-start
  0.7 0.0 copy-start.5
  0.7 0.0 copy-start.2
  0.7 0.0 copy-start.4
  0.7 0.0 copy-start.3
  0.7 2.2 %send.1 = (bf16[272,256]{1,0:T(8,128)(2,1)S(1)}, bf16[2,1920,256]{2,1,0:T(8,128)(2,1)S(1)}) custom-call(bf16[2,1920,256]{2,1,0:T(8,128)(2,1)} %three.1), custom_call_target="tpu_custom_call" | custom-call | flops 503316480 | bytes 1966080 | tf_op jit(solution)/shard_map/send/pallas_call | solution.py:251
  2.9 0.5 %collective-permute-start = (bf16[272,256]{1,0:T(8,128)(2,1)S(1)}, bf16[272,256]{1,0:T(8,128)(2,1)S(1)}, u32[]{:S(2)}, u32[]{:S(2)}) collective-permute-start(bf16[272,256]{1,0:T(8,128)(2,1)S(1)} %get-tuple-element.17), channel_id=1, source_target_pairs={{0,1},{1,0},{2,3},{3,2},{4,5},{5,4},{6,7},{7,6},{8,9},{9,8},{10,11... | collective-permute-start | bytes 417800 | tf_op jit(solution)/shard_map/ppermute | solution.py:221
  3.4 0.5 %keep.1 = f32[272,256]{1,0:T(8,128)S(1)} custom-call(bf16[2,1920,256]{2,1,0:T(8,128)(2,1)S(1)} %get-tuple-element.16.held.three), custom_call_target="tpu_custom_call" | custom-call | flops 503316480 | bytes 1966080 | tf_op jit(solution)/shard_map/keep/pallas_call | solution.py:261
  3.9 0.5 %collective-permute-done = bf16[272,256]{1,0:T(8,128)(2,1)S(1)} collective-permute-done((bf16[272,256]{1,0:T(8,128)(2,1)S(1)}, bf16[272,256]{1,0:T(8,128)(2,1)S(1)}, u32[]{:S(2)}, u32[]{:S(2)}) %collective-permute-start) | collective-permute-done | bytes 139296 | tf_op jit(solution)/shard_map/ppermute | solution.py:221
  4.4 2.9 %collective-permute-start.1 = (bf16[272,256]{1,0:T(8,128)(2,1)S(1)}, bf16[272,256]{1,0:T(8,128)(2,1)S(1)}, u32[]{:S(2)}, u32[]{:S(2)}) collective-permute-start(bf16[272,256]{1,0:T(8,128)(2,1)S(1)} %fusion), channel_id=1, source_target_pairs={{0,2},{2,0},{1,3},{3,1},{4,6},{6,4},{5,7},{7,5},{8,10},{10,8},{9,1... | collective-permute-start | bytes 417800 | tf_op jit(solution)/shard_map/ppermute | solution.py:221
  7.3 0.0 copy-done.1
  7.3 0.0 copy-done
  7.4 0.9 %prep.1 = (f32[272,256]{1,0:T(8,128)S(1)}, s32[15,128]{1,0:T(8,128)S(1)}, f32[8,1920]{1,0:T(8,128)S(1)}, s32[8,128]{1,0:T(8,128)S(1)}) custom-call(s32[2]{0:T(128)S(1)} %copy-done.4, s32[2,2]{1,0:T(2,128)S(1)} %copy-done.3, f32[2]{0:T(128)S(1)} %copy-done.5, f32[64,128]{1,0:T(8,128)S(1)} %bitcast.5, s32[1920]{0:T(1024)S(1)} %copy-done, ...), custom_call_target="tpu_custom_call" | custom-call | flops 3932160 | bytes 1966080 | tf_op jit(solution)/shard_map/prep/pallas_call | solution.py:270
  8.3 3.0 %collective-permute-done.1 = bf16[272,256]{1,0:T(8,128)(2,1)S(1)} collective-permute-done((bf16[272,256]{1,0:T(8,128)(2,1)S(1)}, bf16[272,256]{1,0:T(8,128)(2,1)S(1)}, u32[]{:S(2)}, u32[]{:S(2)}) %collective-permute-start.1) | collective-permute-done | bytes 139296 | tf_op jit(solution)/shard_map/ppermute | solution.py:221
  11.3 0.1 multiply_convert_fusion.own
  11.4 0.1 collective-permute-start.2
  11.6 0.9 %ahead.1 = (f32[1920,128]{1,0:T(8,128)S(1)}, bf16[1920,512]{1,0:T(8,128)(2,1)S(1)}) custom-call(bf16[272,256]{1,0:T(8,128)(2,1)S(1)} %multiply_convert_fusion.own, bf16[2,1920,256]{2,1,0:T(8,128)(2,1)S(1)} %get-tuple-element.16.held.three, s32[15,128]{1,0:T(8,128)S(1)} %get-tuple-element.20.columns), custom_call_target="tpu_custom_call" | custom-call | flops 503316480 | bytes 1966080 | tf_op jit(solution)/shard_map/ahead/pallas_call | solution.py:302
  12.5 0.3 %collective-permute-done.2.other = bf16[272,256]{1,0:T(8,128)(2,1)S(1)} collective-permute-done((bf16[272,256]{1,0:T(8,128)(2,1)S(1)}, bf16[272,256]{1,0:T(8,128)(2,1)S(1)}, u32[]{:S(2)}, u32[]{:S(2)}) %collective-permute-start.2) | collective-permute-done | bytes 139296 | tf_op jit(solution)/shard_map/ppermute | solution.py:221
  12.8 1.3 %weight.1 = f32[8,8,128]{2,1,0:T(8,128)S(1)} custom-call(s32[8,128]{1,0:T(8,128)S(1)} %get-tuple-element.19.starts, bf16[272,256]{1,0:T(8,128)(2,1)S(1)} %collective-permute-done.2.other, f32[1920,128]{1,0:T(8,128)S(1)} %get-tuple-element.21.ahead, bf16[2,1920,256]{2,1,0:T(8,128)(2,1)S(1)} %get-tuple-element.16.held.three, ...), custom_call_target="tpu_custom_call" | custom-call | flops 503316480 | bytes 1966080 | tf_op jit(solution)/shard_map/weight/pallas_call | solution.py:314
  14.1 2.9 %collective-permute-start.3 = (f32[4,8,128]{2,1,0:T(8,128)S(1)}, f32[4,8,128]{2,1,0:T(8,128)S(1)}, u32[]{:S(2)}, u32[]{:S(2)}) collective-permute-start(f32[4,8,128]{2,1,0:T(8,128)S(1)} %get-tuple-element.30), channel_id=1, source_target_pairs={{0,8},{4,12},{8,0},{12,4},{1,9},{5,13},{9,1},{13,5},{2,10},{6,14},... | collective-permute-start | bytes 49160 | tf_op jit(solution)/shard_map/ppermute | solution.py:221
  17.1 1.4 %gamma.3 = (bf16[2,1920,256]{2,1,0:T(8,128)(2,1)}, f32[4,8,128]{2,1,0:T(8,128)S(1)}) custom-call(bf16[272,256]{1,0:T(8,128)(2,1)S(1)} %multiply_convert_fusion.own, bf16[272,256]{1,0:T(8,128)(2,1)S(1)} %collective-permute-done.2.other, bf16[2,1920,256]{2,1,0:T(8,128)(2,1)S(1)} %get-tuple-element.16.held.three, f32[4,8,128]{2,1,0:T(8,128)S(1)} %get-tuple-element.31.mine), custom_call_target="tpu_custom_call" | custom-call | flops 335544320 | bytes 983040 | tf_op jit(solution)/shard_map/gamma/pallas_call | solution.py:346
  18.4 0.4 %collective-permute-done.3 = f32[4,8,128]{2,1,0:T(8,128)S(1)} collective-permute-done((f32[4,8,128]{2,1,0:T(8,128)S(1)}, f32[4,8,128]{2,1,0:T(8,128)S(1)}, u32[]{:S(2)}, u32[]{:S(2)}) %collective-permute-start.3) | collective-permute-done | bytes 16416 | tf_op jit(solution)/shard_map/ppermute | solution.py:221
  18.9 1.9 %collective-permute-start.4 = (f32[2,8,128]{2,1,0:T(8,128)S(1)}, f32[2,8,128]{2,1,0:T(8,128)S(1)}, u32[]{:S(2)}, u32[]{:S(2)}) collective-permute-start(f32[2,8,128]{2,1,0:T(8,128)S(1)} %get-tuple-element.32), channel_id=1, source_target_pairs={{0,4},{4,0},{8,12},{12,8},{1,5},{5,1},{9,13},{13,9},{2,6},{6,2},{1... | collective-permute-start | bytes 24584 | tf_op jit(solution)/shard_map/ppermute | solution.py:221
  20.7 1.4 %gamma.4 = (bf16[2,1920,256]{2,1,0:T(8,128)(2,1)}, f32[2,8,128]{2,1,0:T(8,128)S(1)}) custom-call(bf16[272,256]{1,0:T(8,128)(2,1)S(1)} %multiply_convert_fusion.own, bf16[272,256]{1,0:T(8,128)(2,1)S(1)} %collective-permute-done.2.other, bf16[2,1920,256]{2,1,0:T(8,128)(2,1)S(1)} %get-tuple-element.16.held.three, ...), custom_call_target="tpu_custom_call", output_to_operand_aliasing={{0}: (4, {})} | custom-call | flops 335544320 | bytes 983040 | tf_op jit(solution)/shard_map/gamma/pallas_call | solution.py:346
  22.1 0.4 %collective-permute-done.4 = f32[2,8,128]{2,1,0:T(8,128)S(1)} collective-permute-done((f32[2,8,128]{2,1,0:T(8,128)S(1)}, f32[2,8,128]{2,1,0:T(8,128)S(1)}, u32[]{:S(2)}, u32[]{:S(2)}) %collective-permute-start.4) | collective-permute-done | bytes 8224 | tf_op jit(solution)/shard_map/ppermute | solution.py:221
  22.6 1.7 %collective-permute-start.5 = (f32[1,8,128]{2,1,0:T(8,128)S(1)}, f32[1,8,128]{2,1,0:T(8,128)S(1)}, u32[]{:S(2)}, u32[]{:S(2)}) collective-permute-start(f32[1,8,128]{2,1,0:T(8,128)S(1)} %get-tuple-element.34), channel_id=1, source_target_pairs={{0,2},{2,0},{1,3},{3,1},{4,6},{6,4},{5,7},{7,5},{8,10},{10,8},{9,1... | collective-permute-start | bytes 12296 | tf_op jit(solution)/shard_map/ppermute | solution.py:221
  24.3 1.4 %gamma.5 = (bf16[2,1920,256]{2,1,0:T(8,128)(2,1)}, f32[1,8,128]{2,1,0:T(8,128)S(1)}) custom-call(bf16[272,256]{1,0:T(8,128)(2,1)S(1)} %multiply_convert_fusion.own, bf16[272,256]{1,0:T(8,128)(2,1)S(1)} %collective-permute-done.2.other, bf16[2,1920,256]{2,1,0:T(8,128)(2,1)S(1)} %get-tuple-element.16.held.three, ...), custom_call_target="tpu_custom_call", output_to_operand_aliasing={{0}: (4, {})} | custom-call | flops 335544320 | bytes 983040 | tf_op jit(solution)/shard_map/gamma/pallas_call | solution.py:346
  25.7 0.5 %collective-permute-done.5 = f32[1,8,128]{2,1,0:T(8,128)S(1)} collective-permute-done((f32[1,8,128]{2,1,0:T(8,128)S(1)}, f32[1,8,128]{2,1,0:T(8,128)S(1)}, u32[]{:S(2)}, u32[]{:S(2)}) %collective-permute-start.5) | collective-permute-done | bytes 4128 | tf_op jit(solution)/shard_map/ppermute | solution.py:221
  26.2 0.0 collective-permute-start.6
  26.2 1.2 %collective-permute-done.6 = f32[1,8,128]{2,1,0:T(8,128)S(1)} collective-permute-done((f32[1,8,128]{2,1,0:T(8,128)S(1)}, f32[1,8,128]{2,1,0:T(8,128)S(1)}, u32[]{:S(2)}, u32[]{:S(2)}) %collective-permute-start.6) | collective-permute-done | bytes 4128 | tf_op jit(solution)/shard_map/ppermute | solution.py:221
  27.4 0.6 %dynamic-slice_bitcast_fusion = f32[3,96]{1,0:T(4,128)} fusion(f32[1,8,128]{2,1,0:T(8,128)S(1)} %add.68, s32[]{:T(128)S(6)} %select_n.52), kind=kLoop, calls=%fused_computation.3 | loop fusion | bytes 2308 | tf_op jit(solution)/shard_map/dynamic_slice | solution.py:366
  (12 shorter events, 0.1 us)
Async XLA Ops:
  0.6 6.7 %copy-start.1 = (f32[8192]{0:T(1024)S(1)}, f32[8192]{0:T(1024)}, u32[]{:S(2)}) copy-start(f32[8192]{0:T(1024)} %param.11) | copy-start | bytes 98308
  0.6 6.7 %copy-start = (s32[1920]{0:T(1024)S(1)}, s32[1920]{0:T(1024)}, u32[]{:S(2)}) copy-start(s32[1920]{0:T(1024)} %firsts.1) | copy-start | bytes 23044
  0.7 6.7 %copy-start.5 = (f32[2]{0:T(128)S(1)}, f32[2]{0:T(128)}, u32[]{:S(2)}) copy-start(f32[2]{0:T(128)} %occupied.1) | copy-start | bytes 28
  0.7 6.7 %copy-start.2 = (f32[3,1920]{1,0:T(4,128)S(1)}, f32[3,1920]{1,0:T(4,128)}, u32[]{:S(2)}) copy-start(f32[3,1920]{1,0:T(4,128)} %weights.1) | copy-start | bytes 69124
  0.7 6.7 %copy-start.4 = (s32[2]{0:T(128)S(1)}, s32[2]{0:T(128)}, u32[]{:S(2)}) copy-start(s32[2]{0:T(128)} %valid.1) | copy-start | bytes 28
  0.7 6.7 %copy-start.3 = (s32[2,2]{1,0:T(2,128)S(1)}, s32[2,2]{1,0:T(2,128)}, u32[]{:S(2)}) copy-start(s32[2,2]{1,0:T(2,128)} %blocks.1) | copy-start | bytes 52
  2.9 1.5 %collective-permute-start = (bf16[272,256]{1,0:T(8,128)(2,1)S(1)}, bf16[272,256]{1,0:T(8,128)(2,1)S(1)}, u32[]{:S(2)}, u32[]{:S(2)}) collective-permute-start(bf16[272,256]{1,0:T(8,128)(2,1)S(1)} %get-tuple-element.17), channel_id=1, source_target_pairs={{0,1},{1,0},{2,3},{3,2},{4,5},{5,4},{6,7},{7,6},{8,9},{9,8},{10,11... | collective-permute-start | bytes 417800 | tf_op jit(solution)/shard_map/ppermute | solution.py:221
  4.4 6.9 %collective-permute-start.1 = (bf16[272,256]{1,0:T(8,128)(2,1)S(1)}, bf16[272,256]{1,0:T(8,128)(2,1)S(1)}, u32[]{:S(2)}, u32[]{:S(2)}) collective-permute-start(bf16[272,256]{1,0:T(8,128)(2,1)S(1)} %fusion), channel_id=1, source_target_pairs={{0,2},{2,0},{1,3},{3,1},{4,6},{6,4},{5,7},{7,5},{8,10},{10,8},{9,1... | collective-permute-start | bytes 417800 | tf_op jit(solution)/shard_map/ppermute | solution.py:221
  11.4 1.4 %collective-permute-start.2 = (bf16[272,256]{1,0:T(8,128)(2,1)S(1)}, bf16[272,256]{1,0:T(8,128)(2,1)S(1)}, u32[]{:S(2)}, u32[]{:S(2)}) collective-permute-start(bf16[272,256]{1,0:T(8,128)(2,1)S(1)} %multiply_convert_fusion.own), channel_id=1, source_target_pairs={{0,1},{1,0},{2,3},{3,2},{4,5},{5,4},{6,7},{7,6},{8,9},{9,8},{10,11... | collective-permute-start | bytes 417800 | tf_op jit(solution)/shard_map/ppermute | solution.py:221
  14.1 4.7 %collective-permute-start.3 = (f32[4,8,128]{2,1,0:T(8,128)S(1)}, f32[4,8,128]{2,1,0:T(8,128)S(1)}, u32[]{:S(2)}, u32[]{:S(2)}) collective-permute-start(f32[4,8,128]{2,1,0:T(8,128)S(1)} %get-tuple-element.30), channel_id=1, source_target_pairs={{0,8},{4,12},{8,0},{12,4},{1,9},{5,13},{9,1},{13,5},{2,10},{6,14},... | collective-permute-start | bytes 49160 | tf_op jit(solution)/shard_map/ppermute | solution.py:221
  18.9 3.7 %collective-permute-start.4 = (f32[2,8,128]{2,1,0:T(8,128)S(1)}, f32[2,8,128]{2,1,0:T(8,128)S(1)}, u32[]{:S(2)}, u32[]{:S(2)}) collective-permute-start(f32[2,8,128]{2,1,0:T(8,128)S(1)} %get-tuple-element.32), channel_id=1, source_target_pairs={{0,4},{4,0},{8,12},{12,8},{1,5},{5,1},{9,13},{13,9},{2,6},{6,2},{1... | collective-permute-start | bytes 24584 | tf_op jit(solution)/shard_map/ppermute | solution.py:221
  22.6 3.6 %collective-permute-start.5 = (f32[1,8,128]{2,1,0:T(8,128)S(1)}, f32[1,8,128]{2,1,0:T(8,128)S(1)}, u32[]{:S(2)}, u32[]{:S(2)}) collective-permute-start(f32[1,8,128]{2,1,0:T(8,128)S(1)} %get-tuple-element.34), channel_id=1, source_target_pairs={{0,2},{2,0},{1,3},{3,1},{4,6},{6,4},{5,7},{7,5},{8,10},{10,8},{9,1... | collective-permute-start | bytes 12296 | tf_op jit(solution)/shard_map/ppermute | solution.py:221
  26.2 1.2 %collective-permute-start.6 = (f32[1,8,128]{2,1,0:T(8,128)S(1)}, f32[1,8,128]{2,1,0:T(8,128)S(1)}, u32[]{:S(2)}, u32[]{:S(2)}) collective-permute-start(f32[1,8,128]{2,1,0:T(8,128)S(1)} %add.67), channel_id=1, source_target_pairs={{0,1},{1,0},{2,3},{3,2},{4,5},{5,4},{6,7},{7,6},{8,9},{9,8},{10,11... | collective-permute-start | bytes 12296 | tf_op jit(solution)/shard_map/ppermute | solution.py:221

commit v4 on v3

--- a/solution.py
+++ b/solution.py
@@ -12,6 +12,7 @@
 PACK = WID + 16
 LANES = 128
 SEG = 256
+SIZES = (960, 960)
 OPPOSITE_SCALE = 1.3
 F32 = jnp.float32
 BF16 = jnp.bfloat16
@@ -327,43 +328,67 @@
         name="weight",
     )(starts, other, ahead, held, hot, padded)
 
-    steps = []
-    for axis, count in (("occ", n_occ), ("aux", n_aux)):
-        bit = count // 2
-        while bit:
-            steps.append((axis, bit))
-            bit //= 2
     gamma = None
-    pieces = 3
-    for number, (axis, bit) in enumerate(steps):
+    begin = 0
+
+    def beside(size, mine):
+        nonlocal gamma, begin
+        if not size:
+            return mine
+        before = () if gamma is None else (gamma,)
+        gamma, mine = pl.pallas_call(
+            functools.partial(gamma_kernel, begin, size // 3),
+            out_shape=(jax.ShapeDtypeStruct(three_index.shape, BF16), jax.ShapeDtypeStruct(mine.shape, F32)),
+            in_specs=[vmem] * 4 + [hbm] * len(before),
+            out_specs=(hbm, vmem),
+            input_output_aliases={4: 0} if before else {},
+            scratch_shapes=[
+                pltpu.VMEM((2 * WID, 2 * WID), BF16),
+                pltpu.VMEM((2, size, WID), BF16),
+                pltpu.SemaphoreType.DMA((3,)),
+            ],
+            compiler_params=grant(12),
+            cost_estimate=cost(8 * WID * WID * size, 6 * WID * size),
+            name="gamma",
+        )(own, other, held, mine, *before)
+        begin += size
+        return mine
+
+    def block(x, index, count=1):
+        return lax.dynamic_slice_in_dim(x, index * count, count, 0)
+
+    place, core = lax.axis_index("occ"), lax.axis_index("rep")
+    part = part.reshape(n_occ, n_aux, 8, LANES)
+    bit = n_occ // 2
+    while bit > 2:
         half = part.shape[0] // 2
-        up = (lax.axis_index(axis) // bit) % 2
-        mine = lax.dynamic_slice_in_dim(part, up * half, half, 0)
-        theirs = lax.dynamic_slice_in_dim(part, (1 - up) * half, half, 0)
-        if number < pieces:
-            size = rows // pieces
-            before = () if gamma is None else (gamma,)
-            gamma, mine = pl.pallas_call(
-                functools.partial(gamma_kernel, number * size, size // 2),
-                out_shape=(
-                    jax.ShapeDtypeStruct(three_index.shape, BF16),
-                    jax.ShapeDtypeStruct(mine.shape, F32),
-                ),
-                in_specs=[vmem] * 4 + [hbm] * len(before),
-                out_specs=(hbm, vmem),
-                input_output_aliases={4: 0} if before else {},
-                scratch_shapes=[
-                    pltpu.VMEM((2 * WID, 2 * WID), BF16),
-                    pltpu.VMEM((2, size, WID), BF16),
-                    pltpu.SemaphoreType.DMA((2,)),
-                ],
-                compiler_params=grant(12),
-                cost_estimate=cost(8 * WID * WID * size, 6 * WID * size),
-                name="gamma",
-            )(own, other, held, mine, *before)
-        part = mine + swap(theirs, axis, bit)
+        up = (place // bit) % 2
+        part = block(part, up, half) + swap(block(part, 1 - up, half), "occ", bit)
+        bit //= 2
+
+    low = place % 4
+    first = core == 0
+    far, near = jnp.where(first, low ^ 3, low ^ 2), jnp.where(first, low, low ^ 1)
+    its_far, its_near = jnp.where(first, low ^ 2, low ^ 3), jnp.where(first, low ^ 1, low)
+    mine = jnp.concatenate([block(part, far), block(part, near)], axis=0)
+    mine_sums = mine + swap(jnp.concatenate([block(part, its_far), block(part, its_near)], axis=0), "rep", 1)
+    across = [(2 * i + r, 2 * (i ^ (3 - r)) + r) for i in range(n_occ) for r in range(2)]
+    beside_it = [(2 * i + 1, 2 * (i ^ 1) + 1) for i in range(n_occ)]
+    received = lax.ppermute(mine_sums[0], ("occ", "rep"), across)
+    received1 = lax.ppermute(mine_sums[1], ("occ", "rep"), beside_it)
+    kept = beside(SIZES[0], mine_sums[1])
+    part = received + jnp.where(first, kept, received1)
+
+    sizes = list(SIZES[1:])
+    bit = n_aux // 2
+    while bit:
+        half = part.shape[0] // 2
+        up = (lax.axis_index("aux") // bit) % 2
+        mine = beside(sizes.pop(0) if sizes else 0, block(part, up, half))
+        part = mine + swap(block(part, 1 - up, half), "aux", bit)
+        bit //= 2
     part = part[0] + swap(part, "rep", 1)[0]
-    shell_gradient = lax.dynamic_slice(part, (4 * lax.axis_index("rep"), 0), (3, per))
+    shell_gradient = lax.dynamic_slice(part, (4 * core, 0), (3, per))
     return gamma, shell_gradient
 
 

time: 28.1 us -> 27.4 us (0.975)
  Pallas kernels: 9.92 us -> 8.89 us
  starting transfers between devices: 10 us -> 10.4 us
    ppermute x0 -> x2, starting transfers between devices: none -> 4.5 us  [the longest x1 3.85 us: shards(): received = lax.ppermute(mine_sums[0], ('occ', 'rep'), across)]
    ppermute x7 -> x6, starting transfers between devices: 10 us -> 5.91 us  [swap(): return lax.ppermute(x, axis, [(i, i ^ bit) for i in range(count)])]
    pallas_call x3 -> x2, Pallas kernels: 4.09 us -> 3.07 us  [beside(): pl.pallas_call(functools.partial(gamma_kernel, begin, size // 3), out_sha...]
    ppermute x7 -> x6, waiting for transfers between devices: 6.35 us -> 6.29 us  [swap(): return lax.ppermute(x, axis, [(i, i ^ bit) for i in range(count)])]
    dynamic_slice x4 -> x3, local copies, waits for them, and re-layouts: 0.61 us -> 0.61 us  [the longest x1 0.59 us: shards(): shell_gradient = lax.dynamic_slice(part, (4 * core, 0), (3, per))]
  transfers between devices with their start and end apart: 7 -> 8, of which waited for: 7 -> 6; matrix products, arithmetic and copies ran while one was open for 0% -> 0% of each run, Pallas kernels for 23% -> 20%
where the time goes in v4:
time: 27.4 us; the launch traced here: 27.3 us
  starting transfers between devices  10.4 us (38%)
  Pallas kernels  8.89 us (32%)
  waiting for transfers between devices  6.3 us (23%)
  between operations  0.87 us (3%)
  local copies, waits for them, and re-layouts  0.64 us (2%)
    ppermute x6, waiting for transfers between devices, swap(): return lax.ppermute(x, axis, [(i, i ^ bit) for i in range(count)])  6.29 us
    ppermute x6, starting transfers between devices, swap(): return lax.ppermute(x, axis, [(i, i ^ bit) for i in range(count)])  5.91 us
    ppermute x1, starting transfers between devices, shards(): received = lax.ppermute(mine_sums[0], ('occ', 'rep'), across)  3.85 us
    pallas_call x2, Pallas kernels, beside(): pl.pallas_call(functools.partial(gamma_kernel, begin, size // 3), out_sha...  3.07 us
    pallas_call x1, Pallas kernels, shards(): pl.pallas_call(functools.partial(send_kernel, 4), out_shape=(jax.ShapeDty...  2.18 us
    pallas_call x1, Pallas kernels, shards(): pl.pallas_call(functools.partial(weight_kernel, window, step), out_shape=...  1.27 us
    pallas_call x1, Pallas kernels, shards(): pl.pallas_call(functools.partial(ahead_kernel, step, window), out_shape=(...  0.95 us
    pallas_call x1, Pallas kernels, shards(): pl.pallas_call(functools.partial(prep_kernel, per, window), out_shape=(ja...  0.94 us
  transfers between devices with their start and end apart: 8, of which 6 were waited for; matrix products, arithmetic and copies ran while one was open for 0% of the time, Pallas kernels for 20%

profile of v4, /device:TPU:0, one launch (start us, length us, event | category | flops | bytes accessed | tf_op | source)
XLA Modules:
  0.0 27.3 jit_solution(5995220625536565496)
XLA Ops:
  0.6 0.0 copy-start
  0.6 0.0 copy-start.2
  0.7 0.0 copy-start.1
  0.7 0.0 copy-start.5
  0.7 0.0 copy-start.3
  0.7 0.0 copy-start.4
  0.7 2.2 %send.1 = (bf16[272,256]{1,0:T(8,128)(2,1)S(1)}, bf16[2,1920,256]{2,1,0:T(8,128)(2,1)S(1)}) custom-call(bf16[2,1920,256]{2,1,0:T(8,128)(2,1)} %three.1), custom_call_target="tpu_custom_call" | custom-call | flops 503316480 | bytes 1966080 | tf_op jit(solution)/shard_map/send/pallas_call | solution.py:252
  2.9 0.5 %collective-permute-start = (bf16[272,256]{1,0:T(8,128)(2,1)S(1)}, bf16[272,256]{1,0:T(8,128)(2,1)S(1)}, u32[]{:S(2)}, u32[]{:S(2)}) collective-permute-start(bf16[272,256]{1,0:T(8,128)(2,1)S(1)} %get-tuple-element.15), channel_id=1, source_target_pairs={{0,1},{1,0},{2,3},{3,2},{4,5},{5,4},{6,7},{7,6},{8,9},{9,8},{10,11... | collective-permute-start | bytes 417800 | tf_op jit(solution)/shard_map/ppermute | solution.py:222
  3.4 0.5 %keep.1 = f32[272,256]{1,0:T(8,128)S(1)} custom-call(bf16[2,1920,256]{2,1,0:T(8,128)(2,1)S(1)} %get-tuple-element.14.held.three), custom_call_target="tpu_custom_call" | custom-call | flops 503316480 | bytes 1966080 | tf_op jit(solution)/shard_map/keep/pallas_call | solution.py:262
  3.9 0.5 %collective-permute-done = bf16[272,256]{1,0:T(8,128)(2,1)S(1)} collective-permute-done((bf16[272,256]{1,0:T(8,128)(2,1)S(1)}, bf16[272,256]{1,0:T(8,128)(2,1)S(1)}, u32[]{:S(2)}, u32[]{:S(2)}) %collective-permute-start) | collective-permute-done | bytes 139296 | tf_op jit(solution)/shard_map/ppermute | solution.py:222
  4.4 2.9 %collective-permute-start.1 = (bf16[272,256]{1,0:T(8,128)(2,1)S(1)}, bf16[272,256]{1,0:T(8,128)(2,1)S(1)}, u32[]{:S(2)}, u32[]{:S(2)}) collective-permute-start(bf16[272,256]{1,0:T(8,128)(2,1)S(1)} %fusion), channel_id=1, source_target_pairs={{0,2},{2,0},{1,3},{3,1},{4,6},{6,4},{5,7},{7,5},{8,10},{10,8},{9,1... | collective-permute-start | bytes 417800 | tf_op jit(solution)/shard_map/ppermute | solution.py:222
  7.4 0.0 copy-done.1
  7.4 0.9 %prep.1 = (f32[272,256]{1,0:T(8,128)S(1)}, s32[15,128]{1,0:T(8,128)S(1)}, f32[8,1920]{1,0:T(8,128)S(1)}, s32[8,128]{1,0:T(8,128)S(1)}) custom-call(s32[2]{0:T(128)S(1)} %copy-done.4, s32[2,2]{1,0:T(2,128)S(1)} %copy-done.3, f32[2]{0:T(128)S(1)} %copy-done.5, f32[64,128]{1,0:T(8,128)S(1)} %bitcast.11, s32[1920]{0:T(1024)S(1)} %copy-done, ...), custom_call_target="tpu_custom_call" | custom-call | flops 3932160 | bytes 1966080 | tf_op jit(solution)/shard_map/prep/pallas_call | solution.py:271
  8.3 3.0 %collective-permute-done.1 = bf16[272,256]{1,0:T(8,128)(2,1)S(1)} collective-permute-done((bf16[272,256]{1,0:T(8,128)(2,1)S(1)}, bf16[272,256]{1,0:T(8,128)(2,1)S(1)}, u32[]{:S(2)}, u32[]{:S(2)}) %collective-permute-start.1) | collective-permute-done | bytes 139296 | tf_op jit(solution)/shard_map/ppermute | solution.py:222
  11.3 0.1 multiply_convert_fusion.own
  11.4 0.1 collective-permute-start.2
  11.5 0.9 %ahead.1 = (f32[1920,128]{1,0:T(8,128)S(1)}, bf16[1920,512]{1,0:T(8,128)(2,1)S(1)}) custom-call(bf16[272,256]{1,0:T(8,128)(2,1)S(1)} %multiply_convert_fusion.own, bf16[2,1920,256]{2,1,0:T(8,128)(2,1)S(1)} %get-tuple-element.14.held.three, s32[15,128]{1,0:T(8,128)S(1)} %get-tuple-element.18.columns), custom_call_target="tpu_custom_call" | custom-call | flops 503316480 | bytes 1966080 | tf_op jit(solution)/shard_map/ahead/pallas_call | solution.py:303
  12.5 0.3 %collective-permute-done.2.other = bf16[272,256]{1,0:T(8,128)(2,1)S(1)} collective-permute-done((bf16[272,256]{1,0:T(8,128)(2,1)S(1)}, bf16[272,256]{1,0:T(8,128)(2,1)S(1)}, u32[]{:S(2)}, u32[]{:S(2)}) %collective-permute-start.2) | collective-permute-done | bytes 139296 | tf_op jit(solution)/shard_map/ppermute | solution.py:222
  12.8 1.3 %weight.1 = f32[8,8,128]{2,1,0:T(8,128)S(1)} custom-call(s32[8,128]{1,0:T(8,128)S(1)} %get-tuple-element.17.starts, bf16[272,256]{1,0:T(8,128)(2,1)S(1)} %collective-permute-done.2.other, f32[1920,128]{1,0:T(8,128)S(1)} %get-tuple-element.19.ahead, bf16[2,1920,256]{2,1,0:T(8,128)(2,1)S(1)} %get-tuple-element.14.held.three, ...), custom_call_target="tpu_custom_call" | custom-call | flops 503316480 | bytes 1966080 | tf_op jit(solution)/shard_map/weight/pallas_call | solution.py:315
  14.2 0.2 collective-permute-start.3
  14.4 1.0 %collective-permute-done.3 = f32[2,2,8,128]{3,2,1,0:T(8,128)S(1)} collective-permute-done((f32[2,2,8,128]{3,2,1,0:T(8,128)S(1)}, f32[2,2,8,128]{3,2,1,0:T(8,128)S(1)}, u32[]{:S(2)}, u32[]{:S(2)}) %collective-permute-start.3) | collective-permute-done | bytes 16416 | tf_op jit(solution)/shard_map/ppermute | solution.py:222
  15.4 3.8 %collective-permute-start.4 = (f32[2,8,128]{2,1,0:T(8,128)S(1)}, f32[2,8,128]{2,1,0:T(8,128)S(1)}, u32[]{:S(2)}, u32[]{:S(2)}) collective-permute-start(f32[2,8,128]{2,1,0:T(8,128)S(1)} %get-tuple-element.31), channel_id=1, source_target_pairs={{0,12},{1,9},{4,8},{5,13},{8,4},{9,1},{12,0},{13,5},{2,14},{3,11},... | collective-permute-start | bytes 24584 | tf_op jit(solution)/shard_map/ppermute | solution.py:377
  19.3 0.6 %collective-permute-start.5 = (f32[2,8,128]{2,1,0:T(8,128)S(1)}, f32[2,8,128]{2,1,0:T(8,128)S(1)}, u32[]{:S(2)}, u32[]{:S(2)}) collective-permute-start(f32[2,8,128]{2,1,0:T(8,128)S(1)} %get-tuple-element.30.mine), channel_id=1, source_target_pairs={{1,5},{5,1},{9,13},{13,9},{3,7},{7,3},{11,15},{15,11},{17,21},{21,... | collective-permute-start | bytes 24584 | tf_op jit(solution)/shard_map/ppermute | solution.py:378
  19.9 1.5 %gamma.2 = (bf16[2,1920,256]{2,1,0:T(8,128)(2,1)}, f32[2,8,128]{2,1,0:T(8,128)S(1)}) custom-call(bf16[272,256]{1,0:T(8,128)(2,1)S(1)} %multiply_convert_fusion.own, bf16[272,256]{1,0:T(8,128)(2,1)S(1)} %collective-permute-done.2.other, bf16[2,1920,256]{2,1,0:T(8,128)(2,1)S(1)} %get-tuple-element.14.held.three, f32[2,8,128]{2,1,0:T(8,128)S(1)} %get-tuple-element.30.mine), custom_call_target="tpu_custom_call" | custom-call | flops 503316480 | bytes 1474560 | tf_op jit(solution)/shard_map/gamma/pallas_call | solution.py:339
  21.5 0.0 collective-permute-done.4
  21.5 0.0 collective-permute-done.5
  21.5 1.6 %collective-permute-start.6 = (f32[1,8,128]{2,1,0:T(8,128)S(1)}, f32[1,8,128]{2,1,0:T(8,128)S(1)}, u32[]{:S(2)}, u32[]{:S(2)}) collective-permute-start(f32[1,8,128]{2,1,0:T(8,128)S(1)} %get-tuple-element.32), channel_id=1, source_target_pairs={{0,2},{2,0},{1,3},{3,1},{4,6},{6,4},{5,7},{7,5},{8,10},{10,8},{9,1... | collective-permute-start | bytes 12296 | tf_op jit(solution)/shard_map/ppermute | solution.py:222
  23.1 1.5 %gamma.3 = (bf16[2,1920,256]{2,1,0:T(8,128)(2,1)}, f32[1,8,128]{2,1,0:T(8,128)S(1)}) custom-call(bf16[272,256]{1,0:T(8,128)(2,1)S(1)} %multiply_convert_fusion.own, bf16[272,256]{1,0:T(8,128)(2,1)S(1)} %collective-permute-done.2.other, bf16[2,1920,256]{2,1,0:T(8,128)(2,1)S(1)} %get-tuple-element.14.held.three, ...), custom_call_target="tpu_custom_call", output_to_operand_aliasing={{0}: (4, {})} | custom-call | flops 503316480 | bytes 1474560 | tf_op jit(solution)/shard_map/gamma/pallas_call | solution.py:339
  24.6 0.6 %collective-permute-done.6 = f32[1,8,128]{2,1,0:T(8,128)S(1)} collective-permute-done((f32[1,8,128]{2,1,0:T(8,128)S(1)}, f32[1,8,128]{2,1,0:T(8,128)S(1)}, u32[]{:S(2)}, u32[]{:S(2)}) %collective-permute-start.6) | collective-permute-done | bytes 4128 | tf_op jit(solution)/shard_map/ppermute | solution.py:222
  25.2 0.6 %collective-permute-start.7 = (f32[1,8,128]{2,1,0:T(8,128)S(1)}, f32[1,8,128]{2,1,0:T(8,128)S(1)}, u32[]{:S(2)}, u32[]{:S(2)}) collective-permute-start(f32[1,8,128]{2,1,0:T(8,128)S(1)} %add.61), channel_id=1, source_target_pairs={{0,1},{1,0},{2,3},{3,2},{4,5},{5,4},{6,7},{7,6},{8,9},{9,8},{10,11... | collective-permute-start | bytes 12296 | tf_op jit(solution)/shard_map/ppermute | solution.py:222
  25.8 0.8 %collective-permute-done.7 = f32[1,8,128]{2,1,0:T(8,128)S(1)} collective-permute-done((f32[1,8,128]{2,1,0:T(8,128)S(1)}, f32[1,8,128]{2,1,0:T(8,128)S(1)}, u32[]{:S(2)}, u32[]{:S(2)}) %collective-permute-start.7) | collective-permute-done | bytes 4128 | tf_op jit(solution)/shard_map/ppermute | solution.py:222
  26.7 0.6 %dynamic-slice_bitcast_fusion = f32[3,96]{1,0:T(4,128)} fusion(f32[1,8,128]{2,1,0:T(8,128)S(1)} %add.62, s32[]{:T(128)S(6)} %select_n.68), kind=kLoop, calls=%fused_computation.8 | loop fusion | bytes 2308 | tf_op jit(solution)/shard_map/dynamic_slice | solution.py:391
  (14 shorter events, 0.1 us)
Async XLA Ops:
  0.6 6.7 %copy-start = (s32[1920]{0:T(1024)S(1)}, s32[1920]{0:T(1024)}, u32[]{:S(2)}) copy-start(s32[1920]{0:T(1024)} %firsts.1) | copy-start | bytes 23044
  0.6 6.7 %copy-start.2 = (f32[3,1920]{1,0:T(4,128)S(1)}, f32[3,1920]{1,0:T(4,128)}, u32[]{:S(2)}) copy-start(f32[3,1920]{1,0:T(4,128)} %weights.1) | copy-start | bytes 69124
  0.7 6.7 %copy-start.1 = (f32[8192]{0:T(1024)S(1)}, f32[8192]{0:T(1024)}, u32[]{:S(2)}) copy-start(f32[8192]{0:T(1024)} %param.11) | copy-start | bytes 98308
  0.7 6.7 %copy-start.5 = (f32[2]{0:T(128)S(1)}, f32[2]{0:T(128)}, u32[]{:S(2)}) copy-start(f32[2]{0:T(128)} %occupied.1) | copy-start | bytes 28
  0.7 6.7 %copy-start.3 = (s32[2,2]{1,0:T(2,128)S(1)}, s32[2,2]{1,0:T(2,128)}, u32[]{:S(2)}) copy-start(s32[2,2]{1,0:T(2,128)} %blocks.1) | copy-start | bytes 52
  0.7 6.7 %copy-start.4 = (s32[2]{0:T(128)S(1)}, s32[2]{0:T(128)}, u32[]{:S(2)}) copy-start(s32[2]{0:T(128)} %valid.1) | copy-start | bytes 28
  2.9 1.5 %collective-permute-start = (bf16[272,256]{1,0:T(8,128)(2,1)S(1)}, bf16[272,256]{1,0:T(8,128)(2,1)S(1)}, u32[]{:S(2)}, u32[]{:S(2)}) collective-permute-start(bf16[272,256]{1,0:T(8,128)(2,1)S(1)} %get-tuple-element.15), channel_id=1, source_target_pairs={{0,1},{1,0},{2,3},{3,2},{4,5},{5,4},{6,7},{7,6},{8,9},{9,8},{10,11... | collective-permute-start | bytes 417800 | tf_op jit(solution)/shard_map/ppermute | solution.py:222
  4.4 6.9 %collective-permute-start.1 = (bf16[272,256]{1,0:T(8,128)(2,1)S(1)}, bf16[272,256]{1,0:T(8,128)(2,1)S(1)}, u32[]{:S(2)}, u32[]{:S(2)}) collective-permute-start(bf16[272,256]{1,0:T(8,128)(2,1)S(1)} %fusion), channel_id=1, source_target_pairs={{0,2},{2,0},{1,3},{3,1},{4,6},{6,4},{5,7},{7,5},{8,10},{10,8},{9,1... | collective-permute-start | bytes 417800 | tf_op jit(solution)/shard_map/ppermute | solution.py:222
  11.4 1.4 %collective-permute-start.2 = (bf16[272,256]{1,0:T(8,128)(2,1)S(1)}, bf16[272,256]{1,0:T(8,128)(2,1)S(1)}, u32[]{:S(2)}, u32[]{:S(2)}) collective-permute-start(bf16[272,256]{1,0:T(8,128)(2,1)S(1)} %multiply_convert_fusion.own), channel_id=1, source_target_pairs={{0,1},{1,0},{2,3},{3,2},{4,5},{5,4},{6,7},{7,6},{8,9},{9,8},{10,11... | collective-permute-start | bytes 417800 | tf_op jit(solution)/shard_map/ppermute | solution.py:222
  14.2 1.2 %collective-permute-start.3 = (f32[2,2,8,128]{3,2,1,0:T(8,128)S(1)}, f32[2,2,8,128]{3,2,1,0:T(8,128)S(1)}, u32[]{:S(2)}, u32[]{:S(2)}) collective-permute-start(f32[2,2,8,128]{3,2,1,0:T(8,128)S(1)} %pad_maximum_fusion), channel_id=1, source_target_pairs={{0,1},{1,0},{2,3},{3,2},{4,5},{5,4},{6,7},{7,6},{8,9},{9,8},{10,11... | collective-permute-start | bytes 49160 | tf_op jit(solution)/shard_map/ppermute | solution.py:222
  15.4 6.1 %collective-permute-start.4 = (f32[2,8,128]{2,1,0:T(8,128)S(1)}, f32[2,8,128]{2,1,0:T(8,128)S(1)}, u32[]{:S(2)}, u32[]{:S(2)}) collective-permute-start(f32[2,8,128]{2,1,0:T(8,128)S(1)} %get-tuple-element.31), channel_id=1, source_target_pairs={{0,12},{1,9},{4,8},{5,13},{8,4},{9,1},{12,0},{13,5},{2,14},{3,11},... | collective-permute-start | bytes 24584 | tf_op jit(solution)/shard_map/ppermute | solution.py:377
  19.3 2.2 %collective-permute-start.5 = (f32[2,8,128]{2,1,0:T(8,128)S(1)}, f32[2,8,128]{2,1,0:T(8,128)S(1)}, u32[]{:S(2)}, u32[]{:S(2)}) collective-permute-start(f32[2,8,128]{2,1,0:T(8,128)S(1)} %get-tuple-element.30.mine), channel_id=1, source_target_pairs={{1,5},{5,1},{9,13},{13,9},{3,7},{7,3},{11,15},{15,11},{17,21},{21,... | collective-permute-start | bytes 24584 | tf_op jit(solution)/shard_map/ppermute | solution.py:378
  21.5 3.7 %collective-permute-start.6 = (f32[1,8,128]{2,1,0:T(8,128)S(1)}, f32[1,8,128]{2,1,0:T(8,128)S(1)}, u32[]{:S(2)}, u32[]{:S(2)}) collective-permute-start(f32[1,8,128]{2,1,0:T(8,128)S(1)} %get-tuple-element.32), channel_id=1, source_target_pairs={{0,2},{2,0},{1,3},{3,1},{4,6},{6,4},{5,7},{7,5},{8,10},{10,8},{9,1... | collective-permute-start | bytes 12296 | tf_op jit(solution)/shard_map/ppermute | solution.py:222
  25.2 1.5 %collective-permute-start.7 = (f32[1,8,128]{2,1,0:T(8,128)S(1)}, f32[1,8,128]{2,1,0:T(8,128)S(1)}, u32[]{:S(2)}, u32[]{:S(2)}) collective-permute-start(f32[1,8,128]{2,1,0:T(8,128)S(1)} %add.61), channel_id=1, source_target_pairs={{0,1},{1,0},{2,3},{3,2},{4,5},{5,4},{6,7},{7,6},{8,9},{9,8},{10,11... | collective-permute-start | bytes 12296 | tf_op jit(solution)/shard_map/ppermute | solution.py:222

commit v5 on v4

--- a/solution.py
+++ b/solution.py
@@ -11,8 +11,10 @@
 WID = VBW * DOM
 PACK = WID + 16
 LANES = 128
-SEG = 256
+SEG = 128
 SIZES = (960, 960)
+PACKED = 0
+PIECES = (1280, 640)
 OPPOSITE_SCALE = 1.3
 F32 = jnp.float32
 BF16 = jnp.bfloat16
@@ -22,12 +24,16 @@
     return lax.broadcasted_iota(jnp.int32, shape, dim)
 
 
+def slices(sizes):
+    return [pl.ds(sum(sizes[:k]), size) for k, size in enumerate(sizes)]
+
+
 def tdot(x, y):
     return lax.dot_general(x, y, (((0,), (0,)), ((), ())), preferred_element_type=F32)
 
 
 def make_factor(valid, blocks, occupied, energies, factor):
-    second = lax.axis_index("rep") == 1
+    second = lax.axis_index("rep") == PACKED
     virtual = [
         jnp.concatenate([energies[pl.ds(blocks[i, d], 1), :] for d in range(DOM)], axis=1) for i in range(2)
     ]
@@ -57,13 +63,10 @@
 
 
 def gram_part(second, pieces, held, out, ready=lambda k: None):
-    step = held.shape[1] // pieces
-
     def total(pairs):
         sums = None
-        for k in range(pieces):
+        for k, rows in enumerate(slices(pieces)):
             ready(k)
-            rows = pl.ds(k * step, step)
             terms = [tdot(held[i, rows, :], held[j, rows, :]) for i, j in pairs]
             sums = terms if sums is None else [x + y for x, y in zip(sums, terms)]
         return sums
@@ -84,38 +87,38 @@
 
 
 def send_kernel(pieces, three, send, held, sems):
-    step = three.shape[1] // pieces
     copies = []
-    for k in range(pieces):
-        rows = pl.ds(k * step, step)
+    for k, rows in enumerate(slices(pieces)):
         copies.append(pltpu.make_async_copy(three.at[:, rows, :], held.at[:, rows, :], sems.at[k]))
         copies[-1].start()
-    gram_part(lax.axis_index("rep") == 0, pieces, held, send, lambda k: copies[k].wait())
+    gram_part(lax.axis_index("rep") != PACKED, pieces, held, send, lambda k: copies[k].wait())
 
 
 def keep_kernel(held, keep):
-    gram_part(lax.axis_index("rep") == 1, 1, held, keep)
+    gram_part(lax.axis_index("rep") == PACKED, [held.shape[1]], held, keep)
 
 
 def prep_kernel(
-    per, window, valid, blocks, occupied, energies, firsts, index, weights, factor, columns, padded, starts
+    window, valid, blocks, occupied, energies, firsts, index, weights, factor, hot, padded, starts
 ):
     make_factor(valid, blocks, occupied, energies, factor)
     padded[...] = jnp.zeros(padded.shape, F32)
     padded[0:3, :] = weights[...]
+    lanes = iota((LANES, LANES), 1)
     for k in range(index.shape[0]):
         block = k * LANES // SEG
-        chunk = lax.div(firsts[block * SEG], per)
-        starts[block : block + 1, :] = jnp.full((1, LANES), chunk, jnp.int32)
-        relative = index[k : k + 1, :] - chunk * per
-        column = relative
-        for j in range(1, window):
-            column = column + jnp.where(relative >= j * per, LANES - per, 0)
-        columns[k : k + 1, :] = column
+        tile = lax.div(firsts[block * SEG], LANES)
+        starts[block : block + 1, :] = jnp.full((1, LANES), tile, jnp.int32)
+        column = index[k : k + 1, :] - tile * LANES
+        turned = jnp.broadcast_to(column.astype(F32), (LANES, LANES)).T.astype(jnp.int32)
+        for j in range(window):
+            hot[pl.ds(k * LANES, LANES), pl.ds(j * LANES, LANES)] = (
+                (turned == lanes + j * LANES).astype(F32).astype(BF16)
+            )
 
 
 def parts_of(own, other):
-    first = lax.axis_index("rep") == 0
+    first = lax.axis_index("rep") != PACKED
     return jnp.where(first, own[...], other[...]), jnp.where(first, other[...], own[...])
 
 
@@ -144,24 +147,16 @@
             emit(k, product[:, 0:LANES] + product[:, LANES:WID])
 
 
-def ahead_kernel(step, window, own, three, columns, ahead, hot):
-    lanes = iota((LANES, LANES), 1)
-    for k in range(columns.shape[0]):
-        turned = jnp.broadcast_to(columns[k : k + 1, :].astype(F32), (LANES, LANES)).T.astype(jnp.int32)
-        for j in range(window):
-            hot[pl.ds(k * LANES, LANES), pl.ds(j * LANES, LANES)] = (
-                (turned == lanes + j * LANES).astype(F32).astype(BF16)
-            )
-
+def ahead_kernel(step, own, three, ahead):
     def emit(k, partial):
         ahead[pl.ds(k, step), :] = partial
 
-    quadratic(lax.axis_index("rep") == 1, own, three, step, emit)
-
-
-def weight_kernel(window, step, starts, other, ahead, three, hot, padded, packs, stacked, terms, chunks, sem):
+    quadratic(lax.axis_index("rep") == PACKED, own, three, step, emit)
+
+
+def weight_kernel(window, per, step, starts, other, ahead, three, hot, padded, packs, sums, terms, tops, sem):
     rows = three.shape[1]
-    copy = pltpu.make_async_copy(starts, chunks, sem)
+    copy = pltpu.make_async_copy(starts, tops, sem)
     copy.start()
     terms[...] = jnp.zeros(terms.shape, F32)
 
@@ -172,22 +167,25 @@
             lanes = pl.ds(k + q, LANES)
             term = padded[:, lanes] * weight
             high = term.astype(BF16).astype(F32)
-            stacked[:, lanes] = jnp.concatenate([high, term - high], axis=0).astype(BF16)
-
-    quadratic(lax.axis_index("rep") == 0, other, three, step, emit)
-    sums = []
-    for start in range(0, rows, SEG):
-        part = pl.ds(start, min(SEG, rows - start))
-        both = jnp.dot(stacked[:, part], hot[part, :], preferred_element_type=F32)
-        sums.append(both[0:8, :] + both[8:16, :])
+            stacked = jnp.concatenate([high, term - high], axis=0).astype(BF16)
+            both = jnp.dot(stacked, hot[lanes, :], preferred_element_type=F32)
+            sums[(k + q) // LANES] = both[0:8, :] + both[8:16, :]
+
+    quadratic(lax.axis_index("rep") != PACKED, other, three, step, emit)
     copy.wait()
-    for block, value in enumerate(sums):
-        chunk = chunks[block, 0]
+    for block in range(rows // LANES):
+        value = sums[block]
+        tile = tops[block, 0]
         for j in range(window):
-            terms[chunk + j] += value[:, j * LANES : (j + 1) * LANES]
-    for pair in range(packs.shape[0]):
-        packs[pair, 0:4, :] = terms[2 * pair, 0:4, :]
-        packs[pair, 4:8, :] = terms[2 * pair + 1, 0:4, :]
+            terms[tile + j] += value[:, j * LANES : (j + 1) * LANES]
+    for owner in range(2 * packs.shape[0]):
+        tile, lane = owner * per // LANES, owner * per % LANES
+        value = terms[tile]
+        if lane:
+            value = pltpu.roll(value, LANES - lane, 1)
+        if lane + per > LANES:
+            value = jnp.where(iota(value.shape, 1) < LANES - lane, value, pltpu.roll(terms[tile + 1], LANES - lane, 1))
+        packs[owner // 2, owner % 2 * 4 : owner % 2 * 4 + 4, :] = value[0:4, :]
 
 
 def gamma_kernel(begin, step, own, other, three, mine, *rest):
@@ -237,7 +235,8 @@
     n_occ, n_aux, n_rep = lax.axis_size("occ"), lax.axis_size("aux"), lax.axis_size("rep")
     owners = n_occ * n_aux * n_rep
     per = shells // owners
-    window = (per + SEG - 2) // per + 1
+    window = (LANES + SEG - 2) // LANES + 1
+    tiles = -(-shells // LANES) + window
     vmem = pl.BlockSpec(memory_space=pltpu.VMEM)
     smem = pl.BlockSpec(memory_space=pltpu.SMEM)
     hbm = pl.BlockSpec(memory_space=pltpu.HBM)
@@ -250,11 +249,11 @@
         return pl.CostEstimate(flops=flops, bytes_accessed=size, transcendentals=0)
 
     send, held = pl.pallas_call(
-        functools.partial(send_kernel, 4),
+        functools.partial(send_kernel, PIECES),
         out_shape=(jax.ShapeDtypeStruct((PACK, WID), BF16), jax.ShapeDtypeStruct(three_index.shape, BF16)),
         in_specs=[hbm],
         out_specs=(vmem, vmem),
-        scratch_shapes=[pltpu.SemaphoreType.DMA((4,))],
+        scratch_shapes=[pltpu.SemaphoreType.DMA((len(PIECES),))],
         compiler_params=grant(51),
         cost_estimate=cost(4 * WID * WID * rows, 4 * WID * rows),
         name="send",
@@ -268,13 +267,13 @@
         cost_estimate=cost(4 * WID * WID * rows, 4 * WID * rows),
         name="keep",
     )(held)
-    factor, columns, padded, starts = pl.pallas_call(
-        functools.partial(prep_kernel, per, window),
+    factor, hot, padded, starts = pl.pallas_call(
+        functools.partial(prep_kernel, window),
         out_shape=(
             jax.ShapeDtypeStruct((PACK, WID), F32),
-            jax.ShapeDtypeStruct((rows // LANES, LANES), jnp.int32),
+            jax.ShapeDtypeStruct((rows, window * LANES), BF16),
             jax.ShapeDtypeStruct((8, rows), F32),
-            jax.ShapeDtypeStruct((8, LANES), jnp.int32),
+            jax.ShapeDtypeStruct((16, LANES), jnp.int32),
         ),
         in_specs=[smem, smem, smem, vmem, smem, vmem, vmem],
         out_specs=(vmem,) * 4,
@@ -299,28 +298,25 @@
     own = (sums * factor).astype(BF16)
     other = swap(own, "rep", 1)
 
-    step = rows // 3
-    ahead, hot = pl.pallas_call(
-        functools.partial(ahead_kernel, step, window),
-        out_shape=(
-            jax.ShapeDtypeStruct((rows, LANES), F32),
-            jax.ShapeDtypeStruct((rows, window * LANES), BF16),
-        ),
-        in_specs=[vmem] * 3,
-        out_specs=(vmem, vmem),
+    step = rows
+    ahead = pl.pallas_call(
+        functools.partial(ahead_kernel, step),
+        out_shape=jax.ShapeDtypeStruct((rows, LANES), F32),
+        in_specs=[vmem] * 2,
+        out_specs=vmem,
         compiler_params=grant(16),
         cost_estimate=cost(4 * WID * WID * rows, 4 * WID * rows),
         name="ahead",
-    )(own, held, columns)
+    )(own, held)
     part = pl.pallas_call(
-        functools.partial(weight_kernel, window, step),
+        functools.partial(weight_kernel, window, per, step),
         out_shape=jax.ShapeDtypeStruct((owners // 2, 8, LANES), F32),
         in_specs=[vmem] * 6,
         out_specs=vmem,
         scratch_shapes=[
-            pltpu.VMEM((16, rows), BF16),
-            pltpu.VMEM((owners + window, 8, LANES), F32),
-            pltpu.SMEM((8, LANES), jnp.int32),
+            pltpu.VMEM((rows // LANES, 8, window * LANES), F32),
+            pltpu.VMEM((tiles, 8, LANES), F32),
+            pltpu.SMEM((16, LANES), jnp.int32),
             pltpu.SemaphoreType.DMA,
         ],
         compiler_params=grant(16),

time: 27.4 us -> 27.1 us (0.989)
  waiting for transfers between devices: 6.3 us -> 5.76 us
    ppermute x6, waiting for transfers between devices: 6.29 us -> 5.75 us  [swap(): return lax.ppermute(x, axis, [(i, i ^ bit) for i in range(count)])]
  transfers between devices with their start and end apart: 8 -> 8, of which waited for: 6 -> 6; matrix products, arithmetic and copies ran while one was open for 0% -> 0% of each run, Pallas kernels for 20% -> 22%
where the time goes in v5:
time: 27.1 us; the launch traced here: 27 us
  starting transfers between devices  10.6 us (39%)
  Pallas kernels  8.93 us (33%)
  waiting for transfers between devices  5.76 us (21%)
  between operations  0.87 us (3%)
  local copies, waits for them, and re-layouts  0.64 us (2%)
    ppermute x6, starting transfers between devices, swap(): return lax.ppermute(x, axis, [(i, i ^ bit) for i in range(count)])  6.13 us
    ppermute x6, waiting for transfers between devices, swap(): return lax.ppermute(x, axis, [(i, i ^ bit) for i in range(count)])  5.75 us
    ppermute x1, starting transfers between devices, shards(): received = lax.ppermute(mine_sums[0], ('occ', 'rep'), across)  3.85 us
    pallas_call x2, Pallas kernels, beside(): pl.pallas_call(functools.partial(gamma_kernel, begin, size // 3), out_sha...  3.06 us
    pallas_call x1, Pallas kernels, shards(): pl.pallas_call(functools.partial(send_kernel, PIECES), out_shape=(jax.Sha...  2.01 us
    pallas_call x1, Pallas kernels, shards(): pl.pallas_call(functools.partial(prep_kernel, window), out_shape=(jax.Sha...  1.34 us
    pallas_call x1, Pallas kernels, shards(): pl.pallas_call(functools.partial(weight_kernel, window, per, step), out_s...  1.06 us
    pallas_call x1, Pallas kernels, shards(): pl.pallas_call(keep_kernel, out_shape=jax.ShapeDtypeStruct((PACK, WID), F...  0.74 us
  transfers between devices with their start and end apart: 8, of which 6 were waited for; matrix products, arithmetic and copies ran while one was open for 0% of the time, Pallas kernels for 22%

profile of v5, /device:TPU:0, one launch (start us, length us, event | category | flops | bytes accessed | tf_op | source)
XLA Modules:
  0.0 27.0 jit_solution(4219829405111323022)
XLA Ops:
  0.6 0.0 copy-start
  0.6 0.0 copy-start.2
  0.7 0.0 copy-start.1
  0.7 0.0 copy-start.5
  0.7 0.0 copy-start.3
  0.7 0.0 copy-start.4
  0.7 2.0 %send.1 = (bf16[272,256]{1,0:T(8,128)(2,1)S(1)}, bf16[2,1920,256]{2,1,0:T(8,128)(2,1)S(1)}) custom-call(bf16[2,1920,256]{2,1,0:T(8,128)(2,1)} %three.1), custom_call_target="tpu_custom_call" | custom-call | flops 503316480 | bytes 1966080 | tf_op jit(solution)/shard_map/send/pallas_call | solution.py:251
  2.7 0.8 %collective-permute-start = (bf16[272,256]{1,0:T(8,128)(2,1)S(1)}, bf16[272,256]{1,0:T(8,128)(2,1)S(1)}, u32[]{:S(2)}, u32[]{:S(2)}) collective-permute-start(bf16[272,256]{1,0:T(8,128)(2,1)S(1)} %get-tuple-element.13), channel_id=1, source_target_pairs={{0,1},{1,0},{2,3},{3,2},{4,5},{5,4},{6,7},{7,6},{8,9},{9,8},{10,11... | collective-permute-start | bytes 417800 | tf_op jit(solution)/shard_map/ppermute | solution.py:220
  3.5 0.7 %keep.1 = f32[272,256]{1,0:T(8,128)S(1)} custom-call(bf16[2,1920,256]{2,1,0:T(8,128)(2,1)S(1)} %get-tuple-element.12.held.three), custom_call_target="tpu_custom_call" | custom-call | flops 503316480 | bytes 1966080 | tf_op jit(solution)/shard_map/keep/pallas_call | solution.py:261
  4.2 0.3 collective-permute-done
  4.5 2.6 %collective-permute-start.1 = (bf16[272,256]{1,0:T(8,128)(2,1)S(1)}, bf16[272,256]{1,0:T(8,128)(2,1)S(1)}, u32[]{:S(2)}, u32[]{:S(2)}) collective-permute-start(bf16[272,256]{1,0:T(8,128)(2,1)S(1)} %fusion), channel_id=1, source_target_pairs={{0,2},{2,0},{1,3},{3,1},{4,6},{6,4},{5,7},{7,5},{8,10},{10,8},{9,1... | collective-permute-start | bytes 417800 | tf_op jit(solution)/shard_map/ppermute | solution.py:220
  7.2 0.0 copy-done
  7.2 1.3 %prep.1 = (f32[272,256]{1,0:T(8,128)S(1)}, bf16[1920,256]{1,0:T(8,128)(2,1)S(1)}, f32[8,1920]{1,0:T(8,128)S(1)}, s32[16,128]{1,0:T(8,128)S(1)}) custom-call(s32[2]{0:T(128)S(1)} %copy-done.4, s32[2,2]{1,0:T(2,128)S(1)} %copy-done.3, f32[2]{0:T(128)S(1)} %copy-done.5, f32[64,128]{1,0:T(8,128)S(1)} %bitcast.11, s32[1920]{0:T(1024)S(1)} %copy-done, ...), custom_call_target="tpu_custom_call" | custom-call | flops 1966080 | bytes 983040 | tf_op jit(solution)/shard_map/prep/pallas_call | solution.py:270
  8.6 2.6 %collective-permute-done.1 = bf16[272,256]{1,0:T(8,128)(2,1)S(1)} collective-permute-done((bf16[272,256]{1,0:T(8,128)(2,1)S(1)}, bf16[272,256]{1,0:T(8,128)(2,1)S(1)}, u32[]{:S(2)}, u32[]{:S(2)}) %collective-permute-start.1) | collective-permute-done | bytes 139296 | tf_op jit(solution)/shard_map/ppermute | solution.py:220
  11.2 0.1 multiply_convert_fusion.own
  11.2 0.1 collective-permute-start.2
  11.4 0.7 %ahead.1 = f32[1920,128]{1,0:T(8,128)S(1)} custom-call(bf16[272,256]{1,0:T(8,128)(2,1)S(1)} %multiply_convert_fusion.own, bf16[2,1920,256]{2,1,0:T(8,128)(2,1)S(1)} %get-tuple-element.12.held.three), custom_call_target="tpu_custom_call" | custom-call | flops 503316480 | bytes 1966080 | tf_op jit(solution)/shard_map/ahead/pallas_call | solution.py:302
  12.1 0.6 %collective-permute-done.2.other = bf16[272,256]{1,0:T(8,128)(2,1)S(1)} collective-permute-done((bf16[272,256]{1,0:T(8,128)(2,1)S(1)}, bf16[272,256]{1,0:T(8,128)(2,1)S(1)}, u32[]{:S(2)}, u32[]{:S(2)}) %collective-permute-start.2) | collective-permute-done | bytes 139296 | tf_op jit(solution)/shard_map/ppermute | solution.py:220
  12.7 1.1 %weight.1 = f32[8,8,128]{2,1,0:T(8,128)S(1)} custom-call(s32[16,128]{1,0:T(8,128)S(1)} %get-tuple-element.15.starts, bf16[272,256]{1,0:T(8,128)(2,1)S(1)} %collective-permute-done.2.other, f32[1920,128]{1,0:T(8,128)S(1)} %ahead.1, bf16[2,1920,256]{2,1,0:T(8,128)(2,1)S(1)} %get-tuple-element.12.held.three, bf16[1920,256]{1,0:T(8,128)(2,1)S(1)} %get-tuple-element.16.hot, ...), custom_call_target="tpu_custom_call" | custom-call | flops 503316480 | bytes 1966080 | tf_op jit(solution)/shard_map/weight/pallas_call | solution.py:311
  13.8 0.3 %collective-permute-start.3 = (f32[2,2,8,128]{3,2,1,0:T(8,128)S(1)}, f32[2,2,8,128]{3,2,1,0:T(8,128)S(1)}, u32[]{:S(2)}, u32[]{:S(2)}) collective-permute-start(f32[2,2,8,128]{3,2,1,0:T(8,128)S(1)} %pad_maximum_fusion), channel_id=1, source_target_pairs={{0,1},{1,0},{2,3},{3,2},{4,5},{5,4},{6,7},{7,6},{8,9},{9,8},{10,11... | collective-permute-start | bytes 49160 | tf_op jit(solution)/shard_map/ppermute | solution.py:220
  14.1 0.9 %collective-permute-done.3 = f32[2,2,8,128]{3,2,1,0:T(8,128)S(1)} collective-permute-done((f32[2,2,8,128]{3,2,1,0:T(8,128)S(1)}, f32[2,2,8,128]{3,2,1,0:T(8,128)S(1)}, u32[]{:S(2)}, u32[]{:S(2)}) %collective-permute-start.3) | collective-permute-done | bytes 16416 | tf_op jit(solution)/shard_map/ppermute | solution.py:220
  15.0 3.9 %collective-permute-start.4 = (f32[2,8,128]{2,1,0:T(8,128)S(1)}, f32[2,8,128]{2,1,0:T(8,128)S(1)}, u32[]{:S(2)}, u32[]{:S(2)}) collective-permute-start(f32[2,8,128]{2,1,0:T(8,128)S(1)} %get-tuple-element.27), channel_id=1, source_target_pairs={{0,12},{1,9},{4,8},{5,13},{8,4},{9,1},{12,0},{13,5},{2,14},{3,11},... | collective-permute-start | bytes 24584 | tf_op jit(solution)/shard_map/ppermute | solution.py:373
  18.9 0.6 %collective-permute-start.5 = (f32[2,8,128]{2,1,0:T(8,128)S(1)}, f32[2,8,128]{2,1,0:T(8,128)S(1)}, u32[]{:S(2)}, u32[]{:S(2)}) collective-permute-start(f32[2,8,128]{2,1,0:T(8,128)S(1)} %get-tuple-element.26.mine), channel_id=1, source_target_pairs={{1,5},{5,1},{9,13},{13,9},{3,7},{7,3},{11,15},{15,11},{17,21},{21,... | collective-permute-start | bytes 24584 | tf_op jit(solution)/shard_map/ppermute | solution.py:374
  19.5 1.5 %gamma.2 = (bf16[2,1920,256]{2,1,0:T(8,128)(2,1)}, f32[2,8,128]{2,1,0:T(8,128)S(1)}) custom-call(bf16[272,256]{1,0:T(8,128)(2,1)S(1)} %multiply_convert_fusion.own, bf16[272,256]{1,0:T(8,128)(2,1)S(1)} %collective-permute-done.2.other, bf16[2,1920,256]{2,1,0:T(8,128)(2,1)S(1)} %get-tuple-element.12.held.three, f32[2,8,128]{2,1,0:T(8,128)S(1)} %get-tuple-element.26.mine), custom_call_target="tpu_custom_call" | custom-call | flops 503316480 | bytes 1474560 | tf_op jit(solution)/shard_map/gamma/pallas_call | solution.py:335
  21.1 0.0 collective-permute-done.4
  21.1 0.0 collective-permute-done.5
  21.1 1.6 %collective-permute-start.6 = (f32[1,8,128]{2,1,0:T(8,128)S(1)}, f32[1,8,128]{2,1,0:T(8,128)S(1)}, u32[]{:S(2)}, u32[]{:S(2)}) collective-permute-start(f32[1,8,128]{2,1,0:T(8,128)S(1)} %get-tuple-element.28), channel_id=1, source_target_pairs={{0,2},{2,0},{1,3},{3,1},{4,6},{6,4},{5,7},{7,5},{8,10},{10,8},{9,1... | collective-permute-start | bytes 12296 | tf_op jit(solution)/shard_map/ppermute | solution.py:220
  22.7 1.5 %gamma.3 = (bf16[2,1920,256]{2,1,0:T(8,128)(2,1)}, f32[1,8,128]{2,1,0:T(8,128)S(1)}) custom-call(bf16[272,256]{1,0:T(8,128)(2,1)S(1)} %multiply_convert_fusion.own, bf16[272,256]{1,0:T(8,128)(2,1)S(1)} %collective-permute-done.2.other, bf16[2,1920,256]{2,1,0:T(8,128)(2,1)S(1)} %get-tuple-element.12.held.three, ...), custom_call_target="tpu_custom_call", output_to_operand_aliasing={{0}: (4, {})} | custom-call | flops 503316480 | bytes 1474560 | tf_op jit(solution)/shard_map/gamma/pallas_call | solution.py:335
  24.2 0.6 %collective-permute-done.6 = f32[1,8,128]{2,1,0:T(8,128)S(1)} collective-permute-done((f32[1,8,128]{2,1,0:T(8,128)S(1)}, f32[1,8,128]{2,1,0:T(8,128)S(1)}, u32[]{:S(2)}, u32[]{:S(2)}) %collective-permute-start.6) | collective-permute-done | bytes 4128 | tf_op jit(solution)/shard_map/ppermute | solution.py:220
  24.8 0.7 %collective-permute-start.7 = (f32[1,8,128]{2,1,0:T(8,128)S(1)}, f32[1,8,128]{2,1,0:T(8,128)S(1)}, u32[]{:S(2)}, u32[]{:S(2)}) collective-permute-start(f32[1,8,128]{2,1,0:T(8,128)S(1)} %add.61), channel_id=1, source_target_pairs={{0,1},{1,0},{2,3},{3,2},{4,5},{5,4},{6,7},{7,6},{8,9},{9,8},{10,11... | collective-permute-start | bytes 12296 | tf_op jit(solution)/shard_map/ppermute | solution.py:220
  25.6 0.8 %collective-permute-done.7 = f32[1,8,128]{2,1,0:T(8,128)S(1)} collective-permute-done((f32[1,8,128]{2,1,0:T(8,128)S(1)}, f32[1,8,128]{2,1,0:T(8,128)S(1)}, u32[]{:S(2)}, u32[]{:S(2)}) %collective-permute-start.7) | collective-permute-done | bytes 4128 | tf_op jit(solution)/shard_map/ppermute | solution.py:220
  26.4 0.6 %dynamic-slice_bitcast_fusion = f32[3,96]{1,0:T(4,128)} fusion(f32[1,8,128]{2,1,0:T(8,128)S(1)} %add.62, s32[]{:T(128)S(6)} %select_n.68), kind=kLoop, calls=%fused_computation.8 | loop fusion | bytes 2308 | tf_op jit(solution)/shard_map/dynamic_slice | solution.py:387
  (14 shorter events, 0.1 us)
Async XLA Ops:
  0.6 6.5 %copy-start = (s32[1920]{0:T(1024)S(1)}, s32[1920]{0:T(1024)}, u32[]{:S(2)}) copy-start(s32[1920]{0:T(1024)} %firsts.1) | copy-start | bytes 23044
  0.6 6.5 %copy-start.2 = (f32[3,1920]{1,0:T(4,128)S(1)}, f32[3,1920]{1,0:T(4,128)}, u32[]{:S(2)}) copy-start(f32[3,1920]{1,0:T(4,128)} %weights.1) | copy-start | bytes 69124
  0.7 6.5 %copy-start.1 = (f32[8192]{0:T(1024)S(1)}, f32[8192]{0:T(1024)}, u32[]{:S(2)}) copy-start(f32[8192]{0:T(1024)} %param.11) | copy-start | bytes 98308
  0.7 6.5 %copy-start.5 = (f32[2]{0:T(128)S(1)}, f32[2]{0:T(128)}, u32[]{:S(2)}) copy-start(f32[2]{0:T(128)} %occupied.1) | copy-start | bytes 28
  0.7 6.5 %copy-start.3 = (s32[2,2]{1,0:T(2,128)S(1)}, s32[2,2]{1,0:T(2,128)}, u32[]{:S(2)}) copy-start(s32[2,2]{1,0:T(2,128)} %blocks.1) | copy-start | bytes 52
  0.7 6.5 %copy-start.4 = (s32[2]{0:T(128)S(1)}, s32[2]{0:T(128)}, u32[]{:S(2)}) copy-start(s32[2]{0:T(128)} %valid.1) | copy-start | bytes 28
  2.7 1.8 %collective-permute-start = (bf16[272,256]{1,0:T(8,128)(2,1)S(1)}, bf16[272,256]{1,0:T(8,128)(2,1)S(1)}, u32[]{:S(2)}, u32[]{:S(2)}) collective-permute-start(bf16[272,256]{1,0:T(8,128)(2,1)S(1)} %get-tuple-element.13), channel_id=1, source_target_pairs={{0,1},{1,0},{2,3},{3,2},{4,5},{5,4},{6,7},{7,6},{8,9},{9,8},{10,11... | collective-permute-start | bytes 417800 | tf_op jit(solution)/shard_map/ppermute | solution.py:220
  4.5 6.6 %collective-permute-start.1 = (bf16[272,256]{1,0:T(8,128)(2,1)S(1)}, bf16[272,256]{1,0:T(8,128)(2,1)S(1)}, u32[]{:S(2)}, u32[]{:S(2)}) collective-permute-start(bf16[272,256]{1,0:T(8,128)(2,1)S(1)} %fusion), channel_id=1, source_target_pairs={{0,2},{2,0},{1,3},{3,1},{4,6},{6,4},{5,7},{7,5},{8,10},{10,8},{9,1... | collective-permute-start | bytes 417800 | tf_op jit(solution)/shard_map/ppermute | solution.py:220
  11.2 1.4 %collective-permute-start.2 = (bf16[272,256]{1,0:T(8,128)(2,1)S(1)}, bf16[272,256]{1,0:T(8,128)(2,1)S(1)}, u32[]{:S(2)}, u32[]{:S(2)}) collective-permute-start(bf16[272,256]{1,0:T(8,128)(2,1)S(1)} %multiply_convert_fusion.own), channel_id=1, source_target_pairs={{0,1},{1,0},{2,3},{3,2},{4,5},{5,4},{6,7},{7,6},{8,9},{9,8},{10,11... | collective-permute-start | bytes 417800 | tf_op jit(solution)/shard_map/ppermute | solution.py:220
  13.8 1.2 %collective-permute-start.3 = (f32[2,2,8,128]{3,2,1,0:T(8,128)S(1)}, f32[2,2,8,128]{3,2,1,0:T(8,128)S(1)}, u32[]{:S(2)}, u32[]{:S(2)}) collective-permute-start(f32[2,2,8,128]{3,2,1,0:T(8,128)S(1)} %pad_maximum_fusion), channel_id=1, source_target_pairs={{0,1},{1,0},{2,3},{3,2},{4,5},{5,4},{6,7},{7,6},{8,9},{9,8},{10,11... | collective-permute-start | bytes 49160 | tf_op jit(solution)/shard_map/ppermute | solution.py:220
  15.0 6.1 %collective-permute-start.4 = (f32[2,8,128]{2,1,0:T(8,128)S(1)}, f32[2,8,128]{2,1,0:T(8,128)S(1)}, u32[]{:S(2)}, u32[]{:S(2)}) collective-permute-start(f32[2,8,128]{2,1,0:T(8,128)S(1)} %get-tuple-element.27), channel_id=1, source_target_pairs={{0,12},{1,9},{4,8},{5,13},{8,4},{9,1},{12,0},{13,5},{2,14},{3,11},... | collective-permute-start | bytes 24584 | tf_op jit(solution)/shard_map/ppermute | solution.py:373
  18.9 2.2 %collective-permute-start.5 = (f32[2,8,128]{2,1,0:T(8,128)S(1)}, f32[2,8,128]{2,1,0:T(8,128)S(1)}, u32[]{:S(2)}, u32[]{:S(2)}) collective-permute-start(f32[2,8,128]{2,1,0:T(8,128)S(1)} %get-tuple-element.26.mine), channel_id=1, source_target_pairs={{1,5},{5,1},{9,13},{13,9},{3,7},{7,3},{11,15},{15,11},{17,21},{21,... | collective-permute-start | bytes 24584 | tf_op jit(solution)/shard_map/ppermute | solution.py:374
  21.1 3.7 %collective-permute-start.6 = (f32[1,8,128]{2,1,0:T(8,128)S(1)}, f32[1,8,128]{2,1,0:T(8,128)S(1)}, u32[]{:S(2)}, u32[]{:S(2)}) collective-permute-start(f32[1,8,128]{2,1,0:T(8,128)S(1)} %get-tuple-element.28), channel_id=1, source_target_pairs={{0,2},{2,0},{1,3},{3,1},{4,6},{6,4},{5,7},{7,5},{8,10},{10,8},{9,1... | collective-permute-start | bytes 12296 | tf_op jit(solution)/shard_map/ppermute | solution.py:220
  24.8 1.6 %collective-permute-start.7 = (f32[1,8,128]{2,1,0:T(8,128)S(1)}, f32[1,8,128]{2,1,0:T(8,128)S(1)}, u32[]{:S(2)}, u32[]{:S(2)}) collective-permute-start(f32[1,8,128]{2,1,0:T(8,128)S(1)} %add.61), channel_id=1, source_target_pairs={{0,1},{1,0},{2,3},{3,2},{4,5},{5,4},{6,7},{7,6},{8,9},{9,8},{10,11... | collective-permute-start | bytes 12296 | tf_op jit(solution)/shard_map/ppermute | solution.py:220

commit v6 on v5

--- a/solution.py
+++ b/solution.py
@@ -12,7 +12,6 @@
 PACK = WID + 16
 LANES = 128
 SEG = 128
-SIZES = (960, 960)
 PACKED = 0
 PIECES = (1280, 640)
 OPPOSITE_SCALE = 1.3
@@ -188,8 +187,15 @@
         packs[owner // 2, owner % 2 * 4 : owner % 2 * 4 + 4, :] = value[0:4, :]
 
 
-def gamma_kernel(begin, step, own, other, three, mine, *rest):
-    gamma, kept, table, out, sems = rest[-5:]
+def gamma_rows(table, three, begin, out):
+    rows = pl.ds(begin, out.shape[1])
+    both = jnp.concatenate([three[0, rows, :], three[1, rows, :]], axis=1)
+    g = jnp.dot(both, table[...], preferred_element_type=F32)
+    out[0] = g[:, 0:WID].astype(BF16)
+    out[1] = g[:, WID:].astype(BF16)
+
+
+def gamma_first(own, other, three, mine, kept, table, out):
     kept[...] = mine[...]
     part0, part1 = parts_of(own, other)
     a, b = iota((WID, WID), 0), iota((WID, WID), 1)
@@ -202,17 +208,22 @@
     table[0:WID, WID : 2 * WID] = t01
     table[WID : 2 * WID, 0:WID] = t01.T
     table[WID : 2 * WID, WID : 2 * WID] = jnp.where(a > b, packed, jnp.where(a == b, diagonal, turned)).astype(BF16)
-    copies = []
-    for k in range(out.shape[1] // step):
-        source, target = pl.ds(begin + k * step, step), pl.ds(k * step, step)
-        both = jnp.concatenate([three[0, source, :], three[1, source, :]], axis=1)
-        g = jnp.dot(both, table[...], preferred_element_type=F32)
-        out[0, target, :] = g[:, 0:WID].astype(BF16)
-        out[1, target, :] = g[:, WID:].astype(BF16)
-        copies.append(pltpu.make_async_copy(out.at[:, target, :], gamma.at[:, source, :], sems.at[k]))
-        copies[-1].start()
-    for copy in copies:
-        copy.wait()
+    gamma_rows(table, three, 0, out)
+
+
+def gamma_second(table, three, done, mine, gamma, kept, out, sem):
+    copy = pltpu.make_async_copy(done, gamma.at[:, pl.ds(0, done.shape[1]), :], sem)
+    copy.start()
+    kept[...] = mine[...]
+    gamma_rows(table, three, done.shape[1], out)
+    copy.wait()
+
+
+def gamma_last(done, mine, before, gamma, kept, sem):
+    copy = pltpu.make_async_copy(done, gamma.at[:, pl.ds(done.shape[1], done.shape[1]), :], sem)
+    copy.start()
+    kept[...] = mine[...]
+    copy.wait()
 
 
 def swap(x, axis, bit):
@@ -324,31 +335,11 @@
         name="weight",
     )(starts, other, ahead, held, hot, padded)
 
-    gamma = None
-    begin = 0
-
-    def beside(size, mine):
-        nonlocal gamma, begin
-        if not size:
-            return mine
-        before = () if gamma is None else (gamma,)
-        gamma, mine = pl.pallas_call(
-            functools.partial(gamma_kernel, begin, size // 3),
-            out_shape=(jax.ShapeDtypeStruct(three_index.shape, BF16), jax.ShapeDtypeStruct(mine.shape, F32)),
-            in_specs=[vmem] * 4 + [hbm] * len(before),
-            out_specs=(hbm, vmem),
-            input_output_aliases={4: 0} if before else {},
-            scratch_shapes=[
-                pltpu.VMEM((2 * WID, 2 * WID), BF16),
-                pltpu.VMEM((2, size, WID), BF16),
-                pltpu.SemaphoreType.DMA((3,)),
-            ],
-            compiler_params=grant(12),
-            cost_estimate=cost(8 * WID * WID * size, 6 * WID * size),
-            name="gamma",
-        )(own, other, held, mine, *before)
-        begin += size
-        return mine
+    halves = jax.ShapeDtypeStruct((2, rows // 2, WID), BF16)
+    whole = jax.ShapeDtypeStruct(three_index.shape, BF16)
+
+    def like(x):
+        return jax.ShapeDtypeStruct(x.shape, x.dtype)
 
     def block(x, index, count=1):
         return lax.dynamic_slice_in_dim(x, index * count, count, 0)
@@ -367,20 +358,50 @@
     far, near = jnp.where(first, low ^ 3, low ^ 2), jnp.where(first, low, low ^ 1)
     its_far, its_near = jnp.where(first, low ^ 2, low ^ 3), jnp.where(first, low ^ 1, low)
     mine = jnp.concatenate([block(part, far), block(part, near)], axis=0)
+    mine, table, done = pl.pallas_call(
+        gamma_first,
+        out_shape=(like(mine), jax.ShapeDtypeStruct((2 * WID, 2 * WID), BF16), halves),
+        in_specs=[vmem] * 4,
+        out_specs=(vmem,) * 3,
+        compiler_params=grant(12),
+        cost_estimate=cost(4 * WID * WID * rows, 4 * WID * rows),
+        name="gamma_first",
+    )(own, other, held, mine)
     mine_sums = mine + swap(jnp.concatenate([block(part, its_far), block(part, its_near)], axis=0), "rep", 1)
     across = [(2 * i + r, 2 * (i ^ (3 - r)) + r) for i in range(n_occ) for r in range(2)]
     beside_it = [(2 * i + 1, 2 * (i ^ 1) + 1) for i in range(n_occ)]
     received = lax.ppermute(mine_sums[0], ("occ", "rep"), across)
     received1 = lax.ppermute(mine_sums[1], ("occ", "rep"), beside_it)
-    kept = beside(SIZES[0], mine_sums[1])
+    gamma, kept, done = pl.pallas_call(
+        gamma_second,
+        out_shape=(whole, like(mine_sums[1]), halves),
+        in_specs=[vmem] * 4,
+        out_specs=(hbm, vmem, vmem),
+        scratch_shapes=[pltpu.SemaphoreType.DMA],
+        compiler_params=grant(12),
+        cost_estimate=cost(4 * WID * WID * rows, 4 * WID * rows),
+        name="gamma_second",
+    )(table, held, done, mine_sums[1])
     part = received + jnp.where(first, kept, received1)
 
-    sizes = list(SIZES[1:])
     bit = n_aux // 2
     while bit:
         half = part.shape[0] // 2
         up = (lax.axis_index("aux") // bit) % 2
-        mine = beside(sizes.pop(0) if sizes else 0, block(part, up, half))
+        mine = block(part, up, half)
+        if done is not None:
+            gamma, mine = pl.pallas_call(
+                gamma_last,
+                out_shape=(whole, like(mine)),
+                in_specs=[vmem, vmem, hbm],
+                out_specs=(hbm, vmem),
+                input_output_aliases={2: 0},
+                scratch_shapes=[pltpu.SemaphoreType.DMA],
+                compiler_params=grant(4),
+                cost_estimate=cost(4 * WID * WID * rows, 4 * WID * rows),
+                name="gamma_last",
+            )(done, mine, gamma)
+            done = None
         part = mine + swap(block(part, 1 - up, half), "aux", bit)
         bit //= 2
     part = part[0] + swap(part, "rep", 1)[0]

time: 27.1 us -> 26.4 us (0.974)
  waiting for transfers between devices: 5.76 us -> 5.35 us
  Pallas kernels: 8.93 us -> 8.57 us
    ppermute x6, waiting for transfers between devices: 5.75 us -> 5.34 us  [swap(): return lax.ppermute(x, axis, [(i, i ^ bit) for i in range(count)])]
    pallas_call x2 -> x3, Pallas kernels: 3.06 us -> 2.7 us  [the longest x1 0.97 us: shards(): pl.pallas_call(gamma_second, out_shape=(whole, like(mine_sums[1]), halves...]
  transfers between devices with their start and end apart: 8 -> 8, of which waited for: 6 -> 6; matrix products, arithmetic and copies ran while one was open for 0% -> 0% of each run, Pallas kernels for 22% -> 21%
where the time goes in v6:
time: 26.4 us; the launch traced here: 26.3 us
  starting transfers between devices  10.7 us (41%)
  Pallas kernels  8.57 us (32%)
  waiting for transfers between devices  5.35 us (20%)
  between operations  0.9 us (3%)
  local copies, waits for them, and re-layouts  0.64 us (2%)
    ppermute x6, starting transfers between devices, swap(): return lax.ppermute(x, axis, [(i, i ^ bit) for i in range(count)])  6.11 us
    ppermute x6, waiting for transfers between devices, swap(): return lax.ppermute(x, axis, [(i, i ^ bit) for i in range(count)])  5.34 us
    ppermute x1, starting transfers between devices, shards(): received = lax.ppermute(mine_sums[0], ('occ', 'rep'), across)  3.91 us
    pallas_call x1, Pallas kernels, shards(): pl.pallas_call(functools.partial(send_kernel, PIECES), out_shape=(jax.Sha...  2.01 us
    pallas_call x1, Pallas kernels, shards(): pl.pallas_call(functools.partial(prep_kernel, window), out_shape=(jax.Sha...  1.34 us
    pallas_call x1, Pallas kernels, shards(): pl.pallas_call(functools.partial(weight_kernel, window, per, step), out_s...  1.07 us
    pallas_call x1, Pallas kernels, shards(): pl.pallas_call(gamma_second, out_shape=(whole, like(mine_sums[1]), halves...  0.97 us
    pallas_call x1, Pallas kernels, shards(): pl.pallas_call(gamma_last, out_shape=(whole, like(mine)), in_specs=[vmem,...  0.95 us
  transfers between devices with their start and end apart: 8, of which 6 were waited for; matrix products, arithmetic and copies ran while one was open for 0% of the time, Pallas kernels for 21%

profile of v6, /device:TPU:0, one launch (start us, length us, event | category | flops | bytes accessed | tf_op | source)
XLA Modules:
  0.0 26.3 jit_solution(7615233558844308000)
XLA Ops:
  0.6 0.0 copy-start.1
  0.6 0.0 copy-start
  0.7 0.0 copy-start.5
  0.7 0.0 copy-start.2
  0.7 0.0 copy-start.4
  0.7 2.0 %send.1 = (bf16[272,256]{1,0:T(8,128)(2,1)S(1)}, bf16[2,1920,256]{2,1,0:T(8,128)(2,1)S(1)}) custom-call(bf16[2,1920,256]{2,1,0:T(8,128)(2,1)} %three.1), custom_call_target="tpu_custom_call" | custom-call | flops 503316480 | bytes 1966080 | tf_op jit(solution)/shard_map/send/pallas_call | solution.py:262
  2.7 0.8 %collective-permute-start = (bf16[272,256]{1,0:T(8,128)(2,1)S(1)}, bf16[272,256]{1,0:T(8,128)(2,1)S(1)}, u32[]{:S(2)}, u32[]{:S(2)}) collective-permute-start(bf16[272,256]{1,0:T(8,128)(2,1)S(1)} %get-tuple-element.17), channel_id=1, source_target_pairs={{0,1},{1,0},{2,3},{3,2},{4,5},{5,4},{6,7},{7,6},{8,9},{9,8},{10,11... | collective-permute-start | bytes 417800 | tf_op jit(solution)/shard_map/ppermute | solution.py:231
  3.5 0.7 %keep.1 = f32[272,256]{1,0:T(8,128)S(1)} custom-call(bf16[2,1920,256]{2,1,0:T(8,128)(2,1)S(1)} %get-tuple-element.16.held.three), custom_call_target="tpu_custom_call" | custom-call | flops 503316480 | bytes 1966080 | tf_op jit(solution)/shard_map/keep/pallas_call | solution.py:272
  4.2 0.3 collective-permute-done
  4.5 2.6 %collective-permute-start.1 = (bf16[272,256]{1,0:T(8,128)(2,1)S(1)}, bf16[272,256]{1,0:T(8,128)(2,1)S(1)}, u32[]{:S(2)}, u32[]{:S(2)}) collective-permute-start(bf16[272,256]{1,0:T(8,128)(2,1)S(1)} %fusion), channel_id=1, source_target_pairs={{0,2},{2,0},{1,3},{3,1},{4,6},{6,4},{5,7},{7,5},{8,10},{10,8},{9,1... | collective-permute-start | bytes 417800 | tf_op jit(solution)/shard_map/ppermute | solution.py:231
  7.2 0.0 copy-done
  7.2 1.3 %prep.1 = (f32[272,256]{1,0:T(8,128)S(1)}, bf16[1920,256]{1,0:T(8,128)(2,1)S(1)}, f32[8,1920]{1,0:T(8,128)S(1)}, s32[16,128]{1,0:T(8,128)S(1)}) custom-call(s32[2]{0:T(128)S(1)} %copy-done.4, s32[2,2]{1,0:T(2,128)S(1)} %copy-done.3, f32[2]{0:T(128)S(1)} %copy-done.5, f32[64,128]{1,0:T(8,128)S(1)} %bitcast.11, s32[1920]{0:T(1024)S(1)} %copy-done, ...), custom_call_target="tpu_custom_call" | custom-call | flops 1966080 | bytes 983040 | tf_op jit(solution)/shard_map/prep/pallas_call | solution.py:281
  8.6 2.6 %collective-permute-done.1 = bf16[272,256]{1,0:T(8,128)(2,1)S(1)} collective-permute-done((bf16[272,256]{1,0:T(8,128)(2,1)S(1)}, bf16[272,256]{1,0:T(8,128)(2,1)S(1)}, u32[]{:S(2)}, u32[]{:S(2)}) %collective-permute-start.1) | collective-permute-done | bytes 139296 | tf_op jit(solution)/shard_map/ppermute | solution.py:231
  11.2 0.1 multiply_convert_fusion.own
  11.2 0.1 collective-permute-start.2
  11.4 0.7 %ahead.1 = f32[1920,128]{1,0:T(8,128)S(1)} custom-call(bf16[272,256]{1,0:T(8,128)(2,1)S(1)} %multiply_convert_fusion.own, bf16[2,1920,256]{2,1,0:T(8,128)(2,1)S(1)} %get-tuple-element.16.held.three), custom_call_target="tpu_custom_call" | custom-call | flops 503316480 | bytes 1966080 | tf_op jit(solution)/shard_map/ahead/pallas_call | solution.py:313
  12.1 0.6 %collective-permute-done.2.other = bf16[272,256]{1,0:T(8,128)(2,1)S(1)} collective-permute-done((bf16[272,256]{1,0:T(8,128)(2,1)S(1)}, bf16[272,256]{1,0:T(8,128)(2,1)S(1)}, u32[]{:S(2)}, u32[]{:S(2)}) %collective-permute-start.2) | collective-permute-done | bytes 139296 | tf_op jit(solution)/shard_map/ppermute | solution.py:231
  12.7 1.1 %weight.1 = f32[8,8,128]{2,1,0:T(8,128)S(1)} custom-call(s32[16,128]{1,0:T(8,128)S(1)} %get-tuple-element.19.starts, bf16[272,256]{1,0:T(8,128)(2,1)S(1)} %collective-permute-done.2.other, f32[1920,128]{1,0:T(8,128)S(1)} %ahead.1, bf16[2,1920,256]{2,1,0:T(8,128)(2,1)S(1)} %get-tuple-element.16.held.three, bf16[1920,256]{1,0:T(8,128)(2,1)S(1)} %get-tuple-element.20.hot, ...), custom_call_target="tpu_custom_call" | custom-call | flops 503316480 | bytes 1966080 | tf_op jit(solution)/shard_map/weight/pallas_call | solution.py:322
  13.8 0.3 %collective-permute-start.3 = (f32[2,2,8,128]{3,2,1,0:T(8,128)S(1)}, f32[2,2,8,128]{3,2,1,0:T(8,128)S(1)}, u32[]{:S(2)}, u32[]{:S(2)}) collective-permute-start(f32[2,2,8,128]{3,2,1,0:T(8,128)S(1)} %pad_maximum_fusion.1), channel_id=1, source_target_pairs={{0,1},{1,0},{2,3},{3,2},{4,5},{5,4},{6,7},{7,6},{8,9},{9,8},{10,11... | collective-permute-start | bytes 49160 | tf_op jit(solution)/shard_map/ppermute | solution.py:231
  14.1 0.8 %gamma_first.1 = (f32[2,2,8,128]{3,2,1,0:T(8,128)S(1)}, bf16[512,512]{1,0:T(8,128)(2,1)S(1)}, bf16[2,960,256]{2,1,0:T(8,128)(2,1)S(1)}) custom-call(bf16[272,256]{1,0:T(8,128)(2,1)S(1)} %multiply_convert_fusion.own, bf16[272,256]{1,0:T(8,128)(2,1)S(1)} %collective-permute-done.2.other, bf16[2,1920,256]{2,1,0:T(8,128)(2,1)S(1)} %get-tuple-element.16.held.three, ...), custom_call_target="tpu_custom_call" | custom-call | flops 503316480 | bytes 1966080 | tf_op jit(solution)/shard_map/gamma_first/pallas_call | solution.py:361
  14.9 0.1 collective-permute-done.3
  15.0 3.9 %collective-permute-start.4 = (f32[2,8,128]{2,1,0:T(8,128)S(1)}, f32[2,8,128]{2,1,0:T(8,128)S(1)}, u32[]{:S(2)}, u32[]{:S(2)}) collective-permute-start(f32[2,8,128]{2,1,0:T(8,128)S(1)} %get-tuple-element.34), channel_id=1, source_target_pairs={{0,12},{1,9},{4,8},{5,13},{8,4},{9,1},{12,0},{13,5},{2,14},{3,11},... | collective-permute-start | bytes 24584 | tf_op jit(solution)/shard_map/ppermute | solution.py:373
  18.9 0.6 %collective-permute-start.5 = (f32[2,8,128]{2,1,0:T(8,128)S(1)}, f32[2,8,128]{2,1,0:T(8,128)S(1)}, u32[]{:S(2)}, u32[]{:S(2)}) collective-permute-start(f32[2,8,128]{2,1,0:T(8,128)S(1)} %get-tuple-element.35.mine), channel_id=1, source_target_pairs={{1,5},{5,1},{9,13},{13,9},{3,7},{7,3},{11,15},{15,11},{17,21},{21,... | collective-permute-start | bytes 24584 | tf_op jit(solution)/shard_map/ppermute | solution.py:374
  19.6 1.0 %gamma_second.1 = (bf16[2,1920,256]{2,1,0:T(8,128)(2,1)}, f32[2,8,128]{2,1,0:T(8,128)S(1)}, bf16[2,960,256]{2,1,0:T(8,128)(2,1)S(1)}) custom-call(bf16[512,512]{1,0:T(8,128)(2,1)S(1)} %get-tuple-element.22.table, bf16[2,1920,256]{2,1,0:T(8,128)(2,1)S(1)} %get-tuple-element.16.held.three, bf16[2,960,256]{2,1,0:T(8,128)(2,1)S(1)} %get-tuple-element.23.done, ...), custom_call_target="tpu_custom_call" | custom-call | flops 503316480 | bytes 1966080 | tf_op jit(solution)/shard_map/gamma_second/pallas_call | solution.py:375
  20.6 0.0 collective-permute-done.4
  20.6 0.0 collective-permute-done.5
  20.6 1.7 %collective-permute-start.6 = (f32[1,8,128]{2,1,0:T(8,128)S(1)}, f32[1,8,128]{2,1,0:T(8,128)S(1)}, u32[]{:S(2)}, u32[]{:S(2)}) collective-permute-start(f32[1,8,128]{2,1,0:T(8,128)S(1)} %get-tuple-element.36), channel_id=1, source_target_pairs={{0,2},{2,0},{1,3},{3,1},{4,6},{6,4},{5,7},{7,5},{8,10},{10,8},{9,1... | collective-permute-start | bytes 12296 | tf_op jit(solution)/shard_map/ppermute | solution.py:231
  22.4 1.0 %gamma_last.1 = (bf16[2,1920,256]{2,1,0:T(8,128)(2,1)}, f32[1,8,128]{2,1,0:T(8,128)S(1)}) custom-call(bf16[2,960,256]{2,1,0:T(8,128)(2,1)S(1)} %get-tuple-element.25.done, f32[1,8,128]{2,1,0:T(8,128)S(1)} %get-tuple-element.37.mine, bf16[2,1920,256]{2,1,0:T(8,128)(2,1)} %get-tuple-element.27.before), custom_call_target="tpu_custom_call", output_to_operand_aliasing={{0}: (2, {})} | custom-call | flops 503316480 | bytes 1966080 | tf_op jit(solution)/shard_map/gamma_last/pallas_call | solution.py:393
  23.3 1.0 %collective-permute-done.6 = f32[1,8,128]{2,1,0:T(8,128)S(1)} collective-permute-done((f32[1,8,128]{2,1,0:T(8,128)S(1)}, f32[1,8,128]{2,1,0:T(8,128)S(1)}, u32[]{:S(2)}, u32[]{:S(2)}) %collective-permute-start.6) | collective-permute-done | bytes 4128 | tf_op jit(solution)/shard_map/ppermute | solution.py:231
  24.3 0.5 %collective-permute-start.7 = (f32[1,8,128]{2,1,0:T(8,128)S(1)}, f32[1,8,128]{2,1,0:T(8,128)S(1)}, u32[]{:S(2)}, u32[]{:S(2)}) collective-permute-start(f32[1,8,128]{2,1,0:T(8,128)S(1)} %add.61), channel_id=1, source_target_pairs={{0,1},{1,0},{2,3},{3,2},{4,5},{5,4},{6,7},{7,6},{8,9},{9,8},{10,11... | collective-permute-start | bytes 12296 | tf_op jit(solution)/shard_map/ppermute | solution.py:231
  24.8 0.8 %collective-permute-done.7 = f32[1,8,128]{2,1,0:T(8,128)S(1)} collective-permute-done((f32[1,8,128]{2,1,0:T(8,128)S(1)}, f32[1,8,128]{2,1,0:T(8,128)S(1)}, u32[]{:S(2)}, u32[]{:S(2)}) %collective-permute-start.7) | collective-permute-done | bytes 4128 | tf_op jit(solution)/shard_map/ppermute | solution.py:231
  25.7 0.6 %dynamic-slice_bitcast_fusion = f32[3,96]{1,0:T(4,128)} fusion(f32[1,8,128]{2,1,0:T(8,128)S(1)} %add.62, s32[]{:T(128)S(6)} %select_n.68), kind=kLoop, calls=%fused_computation.8 | loop fusion | bytes 2308 | tf_op jit(solution)/shard_map/dynamic_slice | solution.py:408
  (16 shorter events, 0.1 us)
Async XLA Ops:
  0.6 6.5 %copy-start.1 = (f32[8192]{0:T(1024)S(1)}, f32[8192]{0:T(1024)}, u32[]{:S(2)}) copy-start(f32[8192]{0:T(1024)} %param.11) | copy-start | bytes 98308
  0.6 6.5 %copy-start = (s32[1920]{0:T(1024)S(1)}, s32[1920]{0:T(1024)}, u32[]{:S(2)}) copy-start(s32[1920]{0:T(1024)} %firsts.1) | copy-start | bytes 23044
  0.7 6.5 %copy-start.5 = (f32[2]{0:T(128)S(1)}, f32[2]{0:T(128)}, u32[]{:S(2)}) copy-start(f32[2]{0:T(128)} %occupied.1) | copy-start | bytes 28
  0.7 6.5 %copy-start.2 = (f32[3,1920]{1,0:T(4,128)S(1)}, f32[3,1920]{1,0:T(4,128)}, u32[]{:S(2)}) copy-start(f32[3,1920]{1,0:T(4,128)} %weights.1) | copy-start | bytes 69124
  0.7 6.5 %copy-start.4 = (s32[2]{0:T(128)S(1)}, s32[2]{0:T(128)}, u32[]{:S(2)}) copy-start(s32[2]{0:T(128)} %valid.1) | copy-start | bytes 28
  0.7 6.5 %copy-start.3 = (s32[2,2]{1,0:T(2,128)S(1)}, s32[2,2]{1,0:T(2,128)}, u32[]{:S(2)}) copy-start(s32[2,2]{1,0:T(2,128)} %blocks.1) | copy-start | bytes 52
  2.7 1.8 %collective-permute-start = (bf16[272,256]{1,0:T(8,128)(2,1)S(1)}, bf16[272,256]{1,0:T(8,128)(2,1)S(1)}, u32[]{:S(2)}, u32[]{:S(2)}) collective-permute-start(bf16[272,256]{1,0:T(8,128)(2,1)S(1)} %get-tuple-element.17), channel_id=1, source_target_pairs={{0,1},{1,0},{2,3},{3,2},{4,5},{5,4},{6,7},{7,6},{8,9},{9,8},{10,11... | collective-permute-start | bytes 417800 | tf_op jit(solution)/shard_map/ppermute | solution.py:231
  4.5 6.6 %collective-permute-start.1 = (bf16[272,256]{1,0:T(8,128)(2,1)S(1)}, bf16[272,256]{1,0:T(8,128)(2,1)S(1)}, u32[]{:S(2)}, u32[]{:S(2)}) collective-permute-start(bf16[272,256]{1,0:T(8,128)(2,1)S(1)} %fusion), channel_id=1, source_target_pairs={{0,2},{2,0},{1,3},{3,1},{4,6},{6,4},{5,7},{7,5},{8,10},{10,8},{9,1... | collective-permute-start | bytes 417800 | tf_op jit(solution)/shard_map/ppermute | solution.py:231
  11.2 1.4 %collective-permute-start.2 = (bf16[272,256]{1,0:T(8,128)(2,1)S(1)}, bf16[272,256]{1,0:T(8,128)(2,1)S(1)}, u32[]{:S(2)}, u32[]{:S(2)}) collective-permute-start(bf16[272,256]{1,0:T(8,128)(2,1)S(1)} %multiply_convert_fusion.own), channel_id=1, source_target_pairs={{0,1},{1,0},{2,3},{3,2},{4,5},{5,4},{6,7},{7,6},{8,9},{9,8},{10,11... | collective-permute-start | bytes 417800 | tf_op jit(solution)/shard_map/ppermute | solution.py:231
  13.8 1.2 %collective-permute-start.3 = (f32[2,2,8,128]{3,2,1,0:T(8,128)S(1)}, f32[2,2,8,128]{3,2,1,0:T(8,128)S(1)}, u32[]{:S(2)}, u32[]{:S(2)}) collective-permute-start(f32[2,2,8,128]{3,2,1,0:T(8,128)S(1)} %pad_maximum_fusion.1), channel_id=1, source_target_pairs={{0,1},{1,0},{2,3},{3,2},{4,5},{5,4},{6,7},{7,6},{8,9},{9,8},{10,11... | collective-permute-start | bytes 49160 | tf_op jit(solution)/shard_map/ppermute | solution.py:231
  15.0 5.6 %collective-permute-start.4 = (f32[2,8,128]{2,1,0:T(8,128)S(1)}, f32[2,8,128]{2,1,0:T(8,128)S(1)}, u32[]{:S(2)}, u32[]{:S(2)}) collective-permute-start(f32[2,8,128]{2,1,0:T(8,128)S(1)} %get-tuple-element.34), channel_id=1, source_target_pairs={{0,12},{1,9},{4,8},{5,13},{8,4},{9,1},{12,0},{13,5},{2,14},{3,11},... | collective-permute-start | bytes 24584 | tf_op jit(solution)/shard_map/ppermute | solution.py:373
  18.9 1.7 %collective-permute-start.5 = (f32[2,8,128]{2,1,0:T(8,128)S(1)}, f32[2,8,128]{2,1,0:T(8,128)S(1)}, u32[]{:S(2)}, u32[]{:S(2)}) collective-permute-start(f32[2,8,128]{2,1,0:T(8,128)S(1)} %get-tuple-element.35.mine), channel_id=1, source_target_pairs={{1,5},{5,1},{9,13},{13,9},{3,7},{7,3},{11,15},{15,11},{17,21},{21,... | collective-permute-start | bytes 24584 | tf_op jit(solution)/shard_map/ppermute | solution.py:374
  20.6 3.7 %collective-permute-start.6 = (f32[1,8,128]{2,1,0:T(8,128)S(1)}, f32[1,8,128]{2,1,0:T(8,128)S(1)}, u32[]{:S(2)}, u32[]{:S(2)}) collective-permute-start(f32[1,8,128]{2,1,0:T(8,128)S(1)} %get-tuple-element.36), channel_id=1, source_target_pairs={{0,2},{2,0},{1,3},{3,1},{4,6},{6,4},{5,7},{7,5},{8,10},{10,8},{9,1... | collective-permute-start | bytes 12296 | tf_op jit(solution)/shard_map/ppermute | solution.py:231
  24.3 1.4 %collective-permute-start.7 = (f32[1,8,128]{2,1,0:T(8,128)S(1)}, f32[1,8,128]{2,1,0:T(8,128)S(1)}, u32[]{:S(2)}, u32[]{:S(2)}) collective-permute-start(f32[1,8,128]{2,1,0:T(8,128)S(1)} %add.61), channel_id=1, source_target_pairs={{0,1},{1,0},{2,3},{3,2},{4,5},{5,4},{6,7},{7,6},{8,9},{9,8},{10,11... | collective-permute-start | bytes 12296 | tf_op jit(solution)/shard_map/ppermute | solution.py:231

commit v7 on v6

--- a/solution.py
+++ b/solution.py
@@ -355,8 +355,8 @@
 
     low = place % 4
     first = core == 0
-    far, near = jnp.where(first, low ^ 3, low ^ 2), jnp.where(first, low, low ^ 1)
-    its_far, its_near = jnp.where(first, low ^ 2, low ^ 3), jnp.where(first, low ^ 1, low)
+    far, near = jnp.where(first, low ^ 1, low ^ 2), jnp.where(first, low, low ^ 3)
+    its_far, its_near = jnp.where(first, low ^ 2, low ^ 1), jnp.where(first, low ^ 3, low)
     mine = jnp.concatenate([block(part, far), block(part, near)], axis=0)
     mine, table, done = pl.pallas_call(
         gamma_first,
@@ -368,10 +368,11 @@
         name="gamma_first",
     )(own, other, held, mine)
     mine_sums = mine + swap(jnp.concatenate([block(part, its_far), block(part, its_near)], axis=0), "rep", 1)
-    across = [(2 * i + r, 2 * (i ^ (3 - r)) + r) for i in range(n_occ) for r in range(2)]
-    beside_it = [(2 * i + 1, 2 * (i ^ 1) + 1) for i in range(n_occ)]
+    pairs = [(i, r) for i in range(n_occ) for r in range(2)]
+    across = [(2 * i + r, 2 * (i ^ (2 if r else 1)) + r) for i, r in pairs]
+    beside = [(2 * i + r, 2 * (i ^ (3 if r else 1)) + r) for i, r in pairs]
     received = lax.ppermute(mine_sums[0], ("occ", "rep"), across)
-    received1 = lax.ppermute(mine_sums[1], ("occ", "rep"), beside_it)
+    received1 = lax.ppermute(mine_sums[1], ("occ", "rep"), beside)
     gamma, kept, done = pl.pallas_call(
         gamma_second,
         out_shape=(whole, like(mine_sums[1]), halves),

time: 26.4 us -> 26.3 us (level)
  starting transfers between devices: 10.7 us -> 7.99 us
  waiting for transfers between devices: 5.35 us -> 7.98 us
    ppermute x1, starting transfers between devices: 3.91 us -> 1.88 us  [shards(): received = lax.ppermute(mine_sums[0], ('occ', 'rep'), across)]
    ppermute x1, waiting for transfers between devices: 0.01 us -> 1.82 us  [shards(): received1 = lax.ppermute(mine_sums[1], ('occ', 'rep'), beside)]
    ppermute x1, waiting for transfers between devices: 0.01 us -> 0.65 us  [shards(): received = lax.ppermute(mine_sums[0], ('occ', 'rep'), across)]
    ppermute x1, starting transfers between devices: 0.65 us -> 0.2 us  [shards(): received1 = lax.ppermute(mine_sums[1], ('occ', 'rep'), beside)]
  transfers between devices with their start and end apart: 8 -> 8, of which waited for: 6 -> 8; matrix products, arithmetic and copies ran while one was open for 0% -> 0% of each run, Pallas kernels for 21% -> 21%
where the time goes in v7:
time: 26.3 us; the launch traced here: 26.2 us
  Pallas kernels  8.57 us (33%)
  starting transfers between devices  7.99 us (30%)
  waiting for transfers between devices  7.98 us (30%)
  between operations  0.86 us (3%)
  local copies, waits for them, and re-layouts  0.64 us (2%)
    ppermute x6, starting transfers between devices, swap(): return lax.ppermute(x, axis, [(i, i ^ bit) for i in range(count)])  5.91 us
    ppermute x6, waiting for transfers between devices, swap(): return lax.ppermute(x, axis, [(i, i ^ bit) for i in range(count)])  5.52 us
    pallas_call x1, Pallas kernels, shards(): pl.pallas_call(functools.partial(send_kernel, PIECES), out_shape=(jax.Sha...  2.01 us
    ppermute x1, starting transfers between devices, shards(): received = lax.ppermute(mine_sums[0], ('occ', 'rep'), across)  1.88 us
    ppermute x1, waiting for transfers between devices, shards(): received1 = lax.ppermute(mine_sums[1], ('occ', 'rep'), beside)  1.82 us
    pallas_call x1, Pallas kernels, shards(): pl.pallas_call(functools.partial(prep_kernel, window), out_shape=(jax.Sha...  1.34 us
    pallas_call x1, Pallas kernels, shards(): pl.pallas_call(functools.partial(weight_kernel, window, per, step), out_s...  1.07 us
    pallas_call x1, Pallas kernels, shards(): pl.pallas_call(gamma_second, out_shape=(whole, like(mine_sums[1]), halves...  0.97 us
  transfers between devices with their start and end apart: 8, of which 8 were waited for; matrix products, arithmetic and copies ran while one was open for 0% of the time, Pallas kernels for 21%

profile of v7, /device:TPU:0, one launch (start us, length us, event | category | flops | bytes accessed | tf_op | source)
XLA Modules:
  0.0 26.2 jit_solution(10559786278381795035)
XLA Ops:
  0.6 0.0 copy-start.1
  0.6 0.0 copy-start
  0.7 0.0 copy-start.5
  0.7 0.0 copy-start.2
  0.7 0.0 copy-start.4
  0.7 0.0 copy-start.3
  0.7 2.0 %send.1 = (bf16[272,256]{1,0:T(8,128)(2,1)S(1)}, bf16[2,1920,256]{2,1,0:T(8,128)(2,1)S(1)}) custom-call(bf16[2,1920,256]{2,1,0:T(8,128)(2,1)} %three.1), custom_call_target="tpu_custom_call" | custom-call | flops 503316480 | bytes 1966080 | tf_op jit(solution)/shard_map/send/pallas_call | solution.py:262
  2.7 0.8 %collective-permute-start = (bf16[272,256]{1,0:T(8,128)(2,1)S(1)}, bf16[272,256]{1,0:T(8,128)(2,1)S(1)}, u32[]{:S(2)}, u32[]{:S(2)}) collective-permute-start(bf16[272,256]{1,0:T(8,128)(2,1)S(1)} %get-tuple-element.17), channel_id=1, source_target_pairs={{0,1},{1,0},{2,3},{3,2},{4,5},{5,4},{6,7},{7,6},{8,9},{9,8},{10,11... | collective-permute-start | bytes 417800 | tf_op jit(solution)/shard_map/ppermute | solution.py:231
  3.5 0.7 %keep.1 = f32[272,256]{1,0:T(8,128)S(1)} custom-call(bf16[2,1920,256]{2,1,0:T(8,128)(2,1)S(1)} %get-tuple-element.16.held.three), custom_call_target="tpu_custom_call" | custom-call | flops 503316480 | bytes 1966080 | tf_op jit(solution)/shard_map/keep/pallas_call | solution.py:272
  4.2 0.3 collective-permute-done
  4.5 2.6 %collective-permute-start.1 = (bf16[272,256]{1,0:T(8,128)(2,1)S(1)}, bf16[272,256]{1,0:T(8,128)(2,1)S(1)}, u32[]{:S(2)}, u32[]{:S(2)}) collective-permute-start(bf16[272,256]{1,0:T(8,128)(2,1)S(1)} %fusion), channel_id=1, source_target_pairs={{0,2},{2,0},{1,3},{3,1},{4,6},{6,4},{5,7},{7,5},{8,10},{10,8},{9,1... | collective-permute-start | bytes 417800 | tf_op jit(solution)/shard_map/ppermute | solution.py:231
  7.2 1.3 %prep.1 = (f32[272,256]{1,0:T(8,128)S(1)}, bf16[1920,256]{1,0:T(8,128)(2,1)S(1)}, f32[8,1920]{1,0:T(8,128)S(1)}, s32[16,128]{1,0:T(8,128)S(1)}) custom-call(s32[2]{0:T(128)S(1)} %copy-done.4, s32[2,2]{1,0:T(2,128)S(1)} %copy-done.3, f32[2]{0:T(128)S(1)} %copy-done.5, f32[64,128]{1,0:T(8,128)S(1)} %bitcast.11, s32[1920]{0:T(1024)S(1)} %copy-done, ...), custom_call_target="tpu_custom_call" | custom-call | flops 1966080 | bytes 983040 | tf_op jit(solution)/shard_map/prep/pallas_call | solution.py:281
  8.6 2.6 %collective-permute-done.1 = bf16[272,256]{1,0:T(8,128)(2,1)S(1)} collective-permute-done((bf16[272,256]{1,0:T(8,128)(2,1)S(1)}, bf16[272,256]{1,0:T(8,128)(2,1)S(1)}, u32[]{:S(2)}, u32[]{:S(2)}) %collective-permute-start.1) | collective-permute-done | bytes 139296 | tf_op jit(solution)/shard_map/ppermute | solution.py:231
  11.2 0.1 multiply_convert_fusion.own
  11.2 0.1 collective-permute-start.2
  11.4 0.7 %ahead.1 = f32[1920,128]{1,0:T(8,128)S(1)} custom-call(bf16[272,256]{1,0:T(8,128)(2,1)S(1)} %multiply_convert_fusion.own, bf16[2,1920,256]{2,1,0:T(8,128)(2,1)S(1)} %get-tuple-element.16.held.three), custom_call_target="tpu_custom_call" | custom-call | flops 503316480 | bytes 1966080 | tf_op jit(solution)/shard_map/ahead/pallas_call | solution.py:313
  12.1 0.6 %collective-permute-done.2.other = bf16[272,256]{1,0:T(8,128)(2,1)S(1)} collective-permute-done((bf16[272,256]{1,0:T(8,128)(2,1)S(1)}, bf16[272,256]{1,0:T(8,128)(2,1)S(1)}, u32[]{:S(2)}, u32[]{:S(2)}) %collective-permute-start.2) | collective-permute-done | bytes 139296 | tf_op jit(solution)/shard_map/ppermute | solution.py:231
  12.7 1.1 %weight.1 = f32[8,8,128]{2,1,0:T(8,128)S(1)} custom-call(s32[16,128]{1,0:T(8,128)S(1)} %get-tuple-element.19.starts, bf16[272,256]{1,0:T(8,128)(2,1)S(1)} %collective-permute-done.2.other, f32[1920,128]{1,0:T(8,128)S(1)} %ahead.1, bf16[2,1920,256]{2,1,0:T(8,128)(2,1)S(1)} %get-tuple-element.16.held.three, bf16[1920,256]{1,0:T(8,128)(2,1)S(1)} %get-tuple-element.20.hot, ...), custom_call_target="tpu_custom_call" | custom-call | flops 503316480 | bytes 1966080 | tf_op jit(solution)/shard_map/weight/pallas_call | solution.py:322
  13.8 0.3 %collective-permute-start.3 = (f32[2,2,8,128]{3,2,1,0:T(8,128)S(1)}, f32[2,2,8,128]{3,2,1,0:T(8,128)S(1)}, u32[]{:S(2)}, u32[]{:S(2)}) collective-permute-start(f32[2,2,8,128]{3,2,1,0:T(8,128)S(1)} %pad_maximum_fusion.1), channel_id=1, source_target_pairs={{0,1},{1,0},{2,3},{3,2},{4,5},{5,4},{6,7},{7,6},{8,9},{9,8},{10,11... | collective-permute-start | bytes 49160 | tf_op jit(solution)/shard_map/ppermute | solution.py:231
  14.1 0.8 %gamma_first.1 = (f32[2,2,8,128]{3,2,1,0:T(8,128)S(1)}, bf16[512,512]{1,0:T(8,128)(2,1)S(1)}, bf16[2,960,256]{2,1,0:T(8,128)(2,1)S(1)}) custom-call(bf16[272,256]{1,0:T(8,128)(2,1)S(1)} %multiply_convert_fusion.own, bf16[272,256]{1,0:T(8,128)(2,1)S(1)} %collective-permute-done.2.other, bf16[2,1920,256]{2,1,0:T(8,128)(2,1)S(1)} %get-tuple-element.16.held.three, ...), custom_call_target="tpu_custom_call" | custom-call | flops 503316480 | bytes 1966080 | tf_op jit(solution)/shard_map/gamma_first/pallas_call | solution.py:361
  14.9 0.1 collective-permute-done.3
  15.0 1.9 %collective-permute-start.4 = (f32[2,8,128]{2,1,0:T(8,128)S(1)}, f32[2,8,128]{2,1,0:T(8,128)S(1)}, u32[]{:S(2)}, u32[]{:S(2)}) collective-permute-start(f32[2,8,128]{2,1,0:T(8,128)S(1)} %get-tuple-element.34), channel_id=1, source_target_pairs={{0,4},{1,9},{4,0},{5,13},{8,12},{9,1},{12,8},{13,5},{2,6},{3,11},{... | collective-permute-start | bytes 24584 | tf_op jit(solution)/shard_map/ppermute | solution.py:374
  16.9 0.2 collective-permute-start.5
  17.1 1.0 %gamma_second.1 = (bf16[2,1920,256]{2,1,0:T(8,128)(2,1)}, f32[2,8,128]{2,1,0:T(8,128)S(1)}, bf16[2,960,256]{2,1,0:T(8,128)(2,1)S(1)}) custom-call(bf16[512,512]{1,0:T(8,128)(2,1)S(1)} %get-tuple-element.22.table, bf16[2,1920,256]{2,1,0:T(8,128)(2,1)S(1)} %get-tuple-element.16.held.three, bf16[2,960,256]{2,1,0:T(8,128)(2,1)S(1)} %get-tuple-element.23.done, ...), custom_call_target="tpu_custom_call" | custom-call | flops 503316480 | bytes 1966080 | tf_op jit(solution)/shard_map/gamma_second/pallas_call | solution.py:376
  18.1 0.6 %collective-permute-done.4 = f32[2,8,128]{2,1,0:T(8,128)S(1)} collective-permute-done((f32[2,8,128]{2,1,0:T(8,128)S(1)}, f32[2,8,128]{2,1,0:T(8,128)S(1)}, u32[]{:S(2)}, u32[]{:S(2)}) %collective-permute-start.4) | collective-permute-done | bytes 8224 | tf_op jit(solution)/shard_map/ppermute | solution.py:374
  18.7 1.8 %collective-permute-done.5 = f32[2,8,128]{2,1,0:T(8,128)S(1)} collective-permute-done((f32[2,8,128]{2,1,0:T(8,128)S(1)}, f32[2,8,128]{2,1,0:T(8,128)S(1)}, u32[]{:S(2)}, u32[]{:S(2)}) %collective-permute-start.5) | collective-permute-done | bytes 8224 | tf_op jit(solution)/shard_map/ppermute | solution.py:375
  20.6 1.6 %collective-permute-start.6 = (f32[1,8,128]{2,1,0:T(8,128)S(1)}, f32[1,8,128]{2,1,0:T(8,128)S(1)}, u32[]{:S(2)}, u32[]{:S(2)}) collective-permute-start(f32[1,8,128]{2,1,0:T(8,128)S(1)} %get-tuple-element.36), channel_id=1, source_target_pairs={{0,2},{2,0},{1,3},{3,1},{4,6},{6,4},{5,7},{7,5},{8,10},{10,8},{9,1... | collective-permute-start | bytes 12296 | tf_op jit(solution)/shard_map/ppermute | solution.py:231
  22.1 1.0 %gamma_last.1 = (bf16[2,1920,256]{2,1,0:T(8,128)(2,1)}, f32[1,8,128]{2,1,0:T(8,128)S(1)}) custom-call(bf16[2,960,256]{2,1,0:T(8,128)(2,1)S(1)} %get-tuple-element.25.done, f32[1,8,128]{2,1,0:T(8,128)S(1)} %get-tuple-element.37.mine, bf16[2,1920,256]{2,1,0:T(8,128)(2,1)} %get-tuple-element.27.before), custom_call_target="tpu_custom_call", output_to_operand_aliasing={{0}: (2, {})} | custom-call | flops 503316480 | bytes 1966080 | tf_op jit(solution)/shard_map/gamma_last/pallas_call | solution.py:394
  23.1 1.2 %collective-permute-done.6 = f32[1,8,128]{2,1,0:T(8,128)S(1)} collective-permute-done((f32[1,8,128]{2,1,0:T(8,128)S(1)}, f32[1,8,128]{2,1,0:T(8,128)S(1)}, u32[]{:S(2)}, u32[]{:S(2)}) %collective-permute-start.6) | collective-permute-done | bytes 4128 | tf_op jit(solution)/shard_map/ppermute | solution.py:231
  24.2 0.5 %collective-permute-start.7 = (f32[1,8,128]{2,1,0:T(8,128)S(1)}, f32[1,8,128]{2,1,0:T(8,128)S(1)}, u32[]{:S(2)}, u32[]{:S(2)}) collective-permute-start(f32[1,8,128]{2,1,0:T(8,128)S(1)} %add.61), channel_id=1, source_target_pairs={{0,1},{1,0},{2,3},{3,2},{4,5},{5,4},{6,7},{7,6},{8,9},{9,8},{10,11... | collective-permute-start | bytes 12296 | tf_op jit(solution)/shard_map/ppermute | solution.py:231
  24.8 0.8 %collective-permute-done.7 = f32[1,8,128]{2,1,0:T(8,128)S(1)} collective-permute-done((f32[1,8,128]{2,1,0:T(8,128)S(1)}, f32[1,8,128]{2,1,0:T(8,128)S(1)}, u32[]{:S(2)}, u32[]{:S(2)}) %collective-permute-start.7) | collective-permute-done | bytes 4128 | tf_op jit(solution)/shard_map/ppermute | solution.py:231
  25.6 0.6 %dynamic-slice_bitcast_fusion = f32[3,96]{1,0:T(4,128)} fusion(f32[1,8,128]{2,1,0:T(8,128)S(1)} %add.62, s32[]{:T(128)S(6)} %select_n.68), kind=kLoop, calls=%fused_computation.8 | loop fusion | bytes 2308 | tf_op jit(solution)/shard_map/dynamic_slice | solution.py:409
  (16 shorter events, 0.1 us)
Async XLA Ops:
  0.6 6.5 %copy-start.1 = (f32[8192]{0:T(1024)S(1)}, f32[8192]{0:T(1024)}, u32[]{:S(2)}) copy-start(f32[8192]{0:T(1024)} %param.11) | copy-start | bytes 98308
  0.6 6.5 %copy-start = (s32[1920]{0:T(1024)S(1)}, s32[1920]{0:T(1024)}, u32[]{:S(2)}) copy-start(s32[1920]{0:T(1024)} %firsts.1) | copy-start | bytes 23044
  0.7 6.5 %copy-start.5 = (f32[2]{0:T(128)S(1)}, f32[2]{0:T(128)}, u32[]{:S(2)}) copy-start(f32[2]{0:T(128)} %occupied.1) | copy-start | bytes 28
  0.7 6.5 %copy-start.2 = (f32[3,1920]{1,0:T(4,128)S(1)}, f32[3,1920]{1,0:T(4,128)}, u32[]{:S(2)}) copy-start(f32[3,1920]{1,0:T(4,128)} %weights.1) | copy-start | bytes 69124
  0.7 6.5 %copy-start.4 = (s32[2]{0:T(128)S(1)}, s32[2]{0:T(128)}, u32[]{:S(2)}) copy-start(s32[2]{0:T(128)} %valid.1) | copy-start | bytes 28
  0.7 6.5 %copy-start.3 = (s32[2,2]{1,0:T(2,128)S(1)}, s32[2,2]{1,0:T(2,128)}, u32[]{:S(2)}) copy-start(s32[2,2]{1,0:T(2,128)} %blocks.1) | copy-start | bytes 52
  2.7 1.8 %collective-permute-start = (bf16[272,256]{1,0:T(8,128)(2,1)S(1)}, bf16[272,256]{1,0:T(8,128)(2,1)S(1)}, u32[]{:S(2)}, u32[]{:S(2)}) collective-permute-start(bf16[272,256]{1,0:T(8,128)(2,1)S(1)} %get-tuple-element.17), channel_id=1, source_target_pairs={{0,1},{1,0},{2,3},{3,2},{4,5},{5,4},{6,7},{7,6},{8,9},{9,8},{10,11... | collective-permute-start | bytes 417800 | tf_op jit(solution)/shard_map/ppermute | solution.py:231
  4.5 6.6 %collective-permute-start.1 = (bf16[272,256]{1,0:T(8,128)(2,1)S(1)}, bf16[272,256]{1,0:T(8,128)(2,1)S(1)}, u32[]{:S(2)}, u32[]{:S(2)}) collective-permute-start(bf16[272,256]{1,0:T(8,128)(2,1)S(1)} %fusion), channel_id=1, source_target_pairs={{0,2},{2,0},{1,3},{3,1},{4,6},{6,4},{5,7},{7,5},{8,10},{10,8},{9,1... | collective-permute-start | bytes 417800 | tf_op jit(solution)/shard_map/ppermute | solution.py:231
  11.2 1.4 %collective-permute-start.2 = (bf16[272,256]{1,0:T(8,128)(2,1)S(1)}, bf16[272,256]{1,0:T(8,128)(2,1)S(1)}, u32[]{:S(2)}, u32[]{:S(2)}) collective-permute-start(bf16[272,256]{1,0:T(8,128)(2,1)S(1)} %multiply_convert_fusion.own), channel_id=1, source_target_pairs={{0,1},{1,0},{2,3},{3,2},{4,5},{5,4},{6,7},{7,6},{8,9},{9,8},{10,11... | collective-permute-start | bytes 417800 | tf_op jit(solution)/shard_map/ppermute | solution.py:231
  13.8 1.2 %collective-permute-start.3 = (f32[2,2,8,128]{3,2,1,0:T(8,128)S(1)}, f32[2,2,8,128]{3,2,1,0:T(8,128)S(1)}, u32[]{:S(2)}, u32[]{:S(2)}) collective-permute-start(f32[2,2,8,128]{3,2,1,0:T(8,128)S(1)} %pad_maximum_fusion.1), channel_id=1, source_target_pairs={{0,1},{1,0},{2,3},{3,2},{4,5},{5,4},{6,7},{7,6},{8,9},{9,8},{10,11... | collective-permute-start | bytes 49160 | tf_op jit(solution)/shard_map/ppermute | solution.py:231
  15.0 3.7 %collective-permute-start.4 = (f32[2,8,128]{2,1,0:T(8,128)S(1)}, f32[2,8,128]{2,1,0:T(8,128)S(1)}, u32[]{:S(2)}, u32[]{:S(2)}) collective-permute-start(f32[2,8,128]{2,1,0:T(8,128)S(1)} %get-tuple-element.34), channel_id=1, source_target_pairs={{0,4},{1,9},{4,0},{5,13},{8,12},{9,1},{12,8},{13,5},{2,6},{3,11},{... | collective-permute-start | bytes 24584 | tf_op jit(solution)/shard_map/ppermute | solution.py:374
  16.9 3.7 %collective-permute-start.5 = (f32[2,8,128]{2,1,0:T(8,128)S(1)}, f32[2,8,128]{2,1,0:T(8,128)S(1)}, u32[]{:S(2)}, u32[]{:S(2)}) collective-permute-start(f32[2,8,128]{2,1,0:T(8,128)S(1)} %get-tuple-element.35.mine), channel_id=1, source_target_pairs={{0,4},{1,13},{4,0},{5,9},{8,12},{9,5},{12,8},{13,1},{2,6},{3,15},{... | collective-permute-start | bytes 24584 | tf_op jit(solution)/shard_map/ppermute | solution.py:375
  20.6 3.7 %collective-permute-start.6 = (f32[1,8,128]{2,1,0:T(8,128)S(1)}, f32[1,8,128]{2,1,0:T(8,128)S(1)}, u32[]{:S(2)}, u32[]{:S(2)}) collective-permute-start(f32[1,8,128]{2,1,0:T(8,128)S(1)} %get-tuple-element.36), channel_id=1, source_target_pairs={{0,2},{2,0},{1,3},{3,1},{4,6},{6,4},{5,7},{7,5},{8,10},{10,8},{9,1... | collective-permute-start | bytes 12296 | tf_op jit(solution)/shard_map/ppermute | solution.py:231
  24.2 1.3 %collective-permute-start.7 = (f32[1,8,128]{2,1,0:T(8,128)S(1)}, f32[1,8,128]{2,1,0:T(8,128)S(1)}, u32[]{:S(2)}, u32[]{:S(2)}) collective-permute-start(f32[1,8,128]{2,1,0:T(8,128)S(1)} %add.61), channel_id=1, source_target_pairs={{0,1},{1,0},{2,3},{3,2},{4,5},{5,4},{6,7},{7,6},{8,9},{9,8},{10,11... | collective-permute-start | bytes 12296 | tf_op jit(solution)/shard_map/ppermute | solution.py:231

commit v8 on v7

--- a/solution.py
+++ b/solution.py
@@ -121,6 +121,12 @@
     return jnp.where(first, own[...], other[...]), jnp.where(first, other[...], own[...])
 
 
+def sums_kernel(mine, received, sums, rounded):
+    total = mine[...] + received[...].astype(F32)
+    sums[...] = total
+    rounded[...] = total.astype(BF16)
+
+
 def quadratic(second, part, three, step, emit):
     blocks = range(0, three.shape[1], step)
     a, b = iota((WID, WID), 0), iota((WID, WID), 1)
@@ -153,10 +159,9 @@
     quadratic(lax.axis_index("rep") == PACKED, own, three, step, emit)
 
 
-def weight_kernel(window, per, step, starts, other, ahead, three, hot, padded, packs, sums, terms, tops, sem):
+def weight_kernel(window, per, step, starts, other, ahead, three, hot, padded, packs, sums, terms):
     rows = three.shape[1]
-    copy = pltpu.make_async_copy(starts, tops, sem)
-    copy.start()
+    tops = [starts[block, 0] for block in range(rows // LANES)]
     terms[...] = jnp.zeros(terms.shape, F32)
 
     def emit(k, partial):
@@ -171,10 +176,9 @@
             sums[(k + q) // LANES] = both[0:8, :] + both[8:16, :]
 
     quadratic(lax.axis_index("rep") != PACKED, other, three, step, emit)
-    copy.wait()
     for block in range(rows // LANES):
         value = sums[block]
-        tile = tops[block, 0]
+        tile = tops[block]
         for j in range(window):
             terms[tile + j] += value[:, j * LANES : (j + 1) * LANES]
     for owner in range(2 * packs.shape[0]):
@@ -211,19 +215,18 @@
     gamma_rows(table, three, 0, out)
 
 
-def gamma_second(table, three, done, mine, gamma, kept, out, sem):
-    copy = pltpu.make_async_copy(done, gamma.at[:, pl.ds(0, done.shape[1]), :], sem)
-    copy.start()
+def gamma_second(table, three, done, mine, gamma, kept, out, sems):
+    size = done.shape[1]
+    copies = [
+        pltpu.make_async_copy(done, gamma.at[:, pl.ds(0, size), :], sems.at[0]),
+        pltpu.make_async_copy(out, gamma.at[:, pl.ds(size, size), :], sems.at[1]),
+    ]
+    copies[0].start()
     kept[...] = mine[...]
-    gamma_rows(table, three, done.shape[1], out)
-    copy.wait()
-
-
-def gamma_last(done, mine, before, gamma, kept, sem):
-    copy = pltpu.make_async_copy(done, gamma.at[:, pl.ds(done.shape[1], done.shape[1]), :], sem)
-    copy.start()
-    kept[...] = mine[...]
-    copy.wait()
+    gamma_rows(table, three, size, out)
+    copies[1].start()
+    for copy in copies:
+        copy.wait()
 
 
 def swap(x, axis, bit):
@@ -301,10 +304,18 @@
         centre_weights,
     )
 
-    sums = keep + swap(send, "rep", 1).astype(F32)
+    sums, rounded = pl.pallas_call(
+        sums_kernel,
+        out_shape=(jax.ShapeDtypeStruct((PACK, WID), F32), jax.ShapeDtypeStruct((PACK, WID), BF16)),
+        in_specs=[vmem] * 2,
+        out_specs=(vmem, vmem),
+        compiler_params=grant(4),
+        name="sums",
+    )(keep, swap(send, "rep", 1))
     bit = 1
     while bit < n_aux:
-        sums = sums + swap(sums.astype(BF16), "aux", bit).astype(F32)
+        sums = sums + swap(rounded, "aux", bit).astype(F32)
+        rounded = sums.astype(BF16)
         bit *= 2
     own = (sums * factor).astype(BF16)
     other = swap(own, "rep", 1)
@@ -327,8 +338,6 @@
         scratch_shapes=[
             pltpu.VMEM((rows // LANES, 8, window * LANES), F32),
             pltpu.VMEM((tiles, 8, LANES), F32),
-            pltpu.SMEM((16, LANES), jnp.int32),
-            pltpu.SemaphoreType.DMA,
         ],
         compiler_params=grant(16),
         cost_estimate=cost(4 * WID * WID * rows, 4 * WID * rows),
@@ -373,12 +382,12 @@
     beside = [(2 * i + r, 2 * (i ^ (3 if r else 1)) + r) for i, r in pairs]
     received = lax.ppermute(mine_sums[0], ("occ", "rep"), across)
     received1 = lax.ppermute(mine_sums[1], ("occ", "rep"), beside)
-    gamma, kept, done = pl.pallas_call(
+    gamma, kept = pl.pallas_call(
         gamma_second,
-        out_shape=(whole, like(mine_sums[1]), halves),
+        out_shape=(whole, like(mine_sums[1])),
         in_specs=[vmem] * 4,
-        out_specs=(hbm, vmem, vmem),
-        scratch_shapes=[pltpu.SemaphoreType.DMA],
+        out_specs=(hbm, vmem),
+        scratch_shapes=[pltpu.VMEM(halves.shape, BF16), pltpu.SemaphoreType.DMA((2,))],
         compiler_params=grant(12),
         cost_estimate=cost(4 * WID * WID * rows, 4 * WID * rows),
         name="gamma_second",
@@ -390,19 +399,6 @@
         half = part.shape[0] // 2
         up = (lax.axis_index("aux") // bit) % 2
         mine = block(part, up, half)
-        if done is not None:
-            gamma, mine = pl.pallas_call(
-                gamma_last,
-                out_shape=(whole, like(mine)),
-                in_specs=[vmem, vmem, hbm],
-                out_specs=(hbm, vmem),
-                input_output_aliases={2: 0},
-                scratch_shapes=[pltpu.SemaphoreType.DMA],
-                compiler_params=grant(4),
-                cost_estimate=cost(4 * WID * WID * rows, 4 * WID * rows),
-                name="gamma_last",
-            )(done, mine, gamma)
-            done = None
         part = mine + swap(block(part, 1 - up, half), "aux", bit)
         bit //= 2
     part = part[0] + swap(part, "rep", 1)[0]

time: 26.3 us -> 26.3 us (level)
  waiting for transfers between devices: 7.98 us -> 8.28 us
    ppermute x6, waiting for transfers between devices: 5.52 us -> 6.49 us  [swap(): return lax.ppermute(x, axis, [(i, i ^ bit) for i in range(count)])]
    ppermute x1, waiting for transfers between devices: 0.65 us -> 0.01 us  [shards(): received = lax.ppermute(mine_sums[0], ('occ', 'rep'), across)]
  transfers between devices with their start and end apart: 8 -> 8, of which waited for: 8 -> 7; matrix products, arithmetic and copies ran while one was open for 0% -> 0% of each run, Pallas kernels for 21% -> 20%
where the time goes in v8:
time: 26.3 us; the launch traced here: 26.1 us
  Pallas kernels  8.34 us (32%)
  waiting for transfers between devices  8.28 us (31%)
  starting transfers between devices  7.93 us (30%)
  between operations  0.86 us (3%)
  local copies, waits for them, and re-layouts  0.64 us (2%)
    ppermute x6, waiting for transfers between devices, swap(): return lax.ppermute(x, axis, [(i, i ^ bit) for i in range(count)])  6.49 us
    ppermute x6, starting transfers between devices, swap(): return lax.ppermute(x, axis, [(i, i ^ bit) for i in range(count)])  5.85 us
    pallas_call x1, Pallas kernels, shards(): pl.pallas_call(functools.partial(send_kernel, PIECES), out_shape=(jax.Sha...  2.01 us
    ppermute x1, starting transfers between devices, shards(): received = lax.ppermute(mine_sums[0], ('occ', 'rep'), across)  1.88 us
    ppermute x1, waiting for transfers between devices, shards(): received1 = lax.ppermute(mine_sums[1], ('occ', 'rep'), beside)  1.79 us
    pallas_call x1, Pallas kernels, shards(): pl.pallas_call(gamma_second, out_shape=(whole, like(mine_sums[1])), in_sp...  1.64 us
    pallas_call x1, Pallas kernels, shards(): pl.pallas_call(functools.partial(prep_kernel, window), out_shape=(jax.Sha...  1.34 us
    pallas_call x1, Pallas kernels, shards(): pl.pallas_call(functools.partial(weight_kernel, window, per, step), out_s...  1.09 us
  transfers between devices with their start and end apart: 8, of which 7 were waited for; matrix products, arithmetic and copies ran while one was open for 0% of the time, Pallas kernels for 20%

profile of v8, /device:TPU:0, one launch (start us, length us, event | category | flops | bytes accessed | tf_op | source)
XLA Modules:
  0.0 26.1 jit_solution(10314173376141668736)
XLA Ops:
  0.6 0.0 copy-start.1
  0.6 0.0 copy-start
  0.7 0.0 copy-start.5
  0.7 0.0 copy-start.2
  0.7 0.0 copy-start.4
  0.7 2.0 %send.1 = (bf16[272,256]{1,0:T(8,128)(2,1)S(1)}, bf16[2,1920,256]{2,1,0:T(8,128)(2,1)S(1)}) custom-call(bf16[2,1920,256]{2,1,0:T(8,128)(2,1)} %three.1), custom_call_target="tpu_custom_call" | custom-call | flops 503316480 | bytes 1966080 | tf_op jit(solution)/shard_map/send/pallas_call | solution.py:265
  2.7 0.8 %collective-permute-start = (bf16[272,256]{1,0:T(8,128)(2,1)S(1)}, bf16[272,256]{1,0:T(8,128)(2,1)S(1)}, u32[]{:S(2)}, u32[]{:S(2)}) collective-permute-start(bf16[272,256]{1,0:T(8,128)(2,1)S(1)} %get-tuple-element.16), channel_id=1, source_target_pairs={{0,1},{1,0},{2,3},{3,2},{4,5},{5,4},{6,7},{7,6},{8,9},{9,8},{10,11... | collective-permute-start | bytes 417800 | tf_op jit(solution)/shard_map/ppermute | solution.py:234
  3.5 0.7 %keep.1.mine = f32[272,256]{1,0:T(8,128)S(1)} custom-call(bf16[2,1920,256]{2,1,0:T(8,128)(2,1)S(1)} %get-tuple-element.15.held.three), custom_call_target="tpu_custom_call" | custom-call | flops 503316480 | bytes 1966080 | tf_op jit(solution)/shard_map/keep/pallas_call | solution.py:275
  4.2 0.3 collective-permute-done.received
  4.5 2.6 %collective-permute-start.1 = (bf16[272,256]{1,0:T(8,128)(2,1)S(1)}, bf16[272,256]{1,0:T(8,128)(2,1)S(1)}, u32[]{:S(2)}, u32[]{:S(2)}) collective-permute-start(bf16[272,256]{1,0:T(8,128)(2,1)S(1)} %get-tuple-element.18), channel_id=1, source_target_pairs={{0,2},{2,0},{1,3},{3,1},{4,6},{6,4},{5,7},{7,5},{8,10},{10,8},{9,1... | collective-permute-start | bytes 417800 | tf_op jit(solution)/shard_map/ppermute | solution.py:234
  7.2 0.0 copy-done.1
  7.2 0.0 copy-done.4
  7.2 0.0 copy-done.3
  7.2 1.3 %prep.1 = (f32[272,256]{1,0:T(8,128)S(1)}, bf16[1920,256]{1,0:T(8,128)(2,1)S(1)}, f32[8,1920]{1,0:T(8,128)S(1)}, s32[16,128]{1,0:T(8,128)S(1)}) custom-call(s32[2]{0:T(128)S(1)} %copy-done.4, s32[2,2]{1,0:T(2,128)S(1)} %copy-done.3, f32[2]{0:T(128)S(1)} %copy-done.5, f32[64,128]{1,0:T(8,128)S(1)} %bitcast.11, s32[1920]{0:T(1024)S(1)} %copy-done, ...), custom_call_target="tpu_custom_call" | custom-call | flops 1966080 | bytes 983040 | tf_op jit(solution)/shard_map/prep/pallas_call | solution.py:284
  8.6 2.6 %collective-permute-done.1 = bf16[272,256]{1,0:T(8,128)(2,1)S(1)} collective-permute-done((bf16[272,256]{1,0:T(8,128)(2,1)S(1)}, bf16[272,256]{1,0:T(8,128)(2,1)S(1)}, u32[]{:S(2)}, u32[]{:S(2)}) %collective-permute-start.1) | collective-permute-done | bytes 139296 | tf_op jit(solution)/shard_map/ppermute | solution.py:234
  11.2 0.1 collective-permute-start.2
  11.4 0.7 %ahead.1 = f32[1920,128]{1,0:T(8,128)S(1)} custom-call(bf16[272,256]{1,0:T(8,128)(2,1)S(1)} %multiply_convert_fusion.own, bf16[2,1920,256]{2,1,0:T(8,128)(2,1)S(1)} %get-tuple-element.15.held.three), custom_call_target="tpu_custom_call" | custom-call | flops 503316480 | bytes 1966080 | tf_op jit(solution)/shard_map/ahead/pallas_call | solution.py:324
  12.1 0.6 %collective-permute-done.2.other = bf16[272,256]{1,0:T(8,128)(2,1)S(1)} collective-permute-done((bf16[272,256]{1,0:T(8,128)(2,1)S(1)}, bf16[272,256]{1,0:T(8,128)(2,1)S(1)}, u32[]{:S(2)}, u32[]{:S(2)}) %collective-permute-start.2) | collective-permute-done | bytes 139296 | tf_op jit(solution)/shard_map/ppermute | solution.py:234
  12.6 1.1 %weight.1 = f32[8,8,128]{2,1,0:T(8,128)S(1)} custom-call(s32[16,128]{1,0:T(8,128)S(1)} %get-tuple-element.20.starts, bf16[272,256]{1,0:T(8,128)(2,1)S(1)} %collective-permute-done.2.other, f32[1920,128]{1,0:T(8,128)S(1)} %ahead.1, bf16[2,1920,256]{2,1,0:T(8,128)(2,1)S(1)} %get-tuple-element.15.held.three, bf16[1920,256]{1,0:T(8,128)(2,1)S(1)} %get-tuple-element.21.hot, ...), custom_call_target="tpu_custom_call" | custom-call | flops 503316480 | bytes 1966080 | tf_op jit(solution)/shard_map/weight/pallas_call | solution.py:333
  13.8 0.3 %collective-permute-start.3 = (f32[2,2,8,128]{3,2,1,0:T(8,128)S(1)}, f32[2,2,8,128]{3,2,1,0:T(8,128)S(1)}, u32[]{:S(2)}, u32[]{:S(2)}) collective-permute-start(f32[2,2,8,128]{3,2,1,0:T(8,128)S(1)} %pad_maximum_fusion.1), channel_id=1, source_target_pairs={{0,1},{1,0},{2,3},{3,2},{4,5},{5,4},{6,7},{7,6},{8,9},{9,8},{10,11... | collective-permute-start | bytes 49160 | tf_op jit(solution)/shard_map/ppermute | solution.py:234
  14.1 0.8 %gamma_first.1 = (f32[2,2,8,128]{3,2,1,0:T(8,128)S(1)}, bf16[512,512]{1,0:T(8,128)(2,1)S(1)}, bf16[2,960,256]{2,1,0:T(8,128)(2,1)S(1)}) custom-call(bf16[272,256]{1,0:T(8,128)(2,1)S(1)} %multiply_convert_fusion.own, bf16[272,256]{1,0:T(8,128)(2,1)S(1)} %collective-permute-done.2.other, bf16[2,1920,256]{2,1,0:T(8,128)(2,1)S(1)} %get-tuple-element.15.held.three, ...), custom_call_target="tpu_custom_call" | custom-call | flops 503316480 | bytes 1966080 | tf_op jit(solution)/shard_map/gamma_first/pallas_call | solution.py:370
  14.9 0.1 collective-permute-done.3
  15.0 1.9 %collective-permute-start.4 = (f32[2,8,128]{2,1,0:T(8,128)S(1)}, f32[2,8,128]{2,1,0:T(8,128)S(1)}, u32[]{:S(2)}, u32[]{:S(2)}) collective-permute-start(f32[2,8,128]{2,1,0:T(8,128)S(1)} %get-tuple-element.32), channel_id=1, source_target_pairs={{0,4},{1,9},{4,0},{5,13},{8,12},{9,1},{12,8},{13,5},{2,6},{3,11},{... | collective-permute-start | bytes 24584 | tf_op jit(solution)/shard_map/ppermute | solution.py:383
  16.9 0.2 collective-permute-start.5
  17.1 1.6 %gamma_second.1 = (bf16[2,1920,256]{2,1,0:T(8,128)(2,1)}, f32[2,8,128]{2,1,0:T(8,128)S(1)}) custom-call(bf16[512,512]{1,0:T(8,128)(2,1)S(1)} %get-tuple-element.23.table, bf16[2,1920,256]{2,1,0:T(8,128)(2,1)S(1)} %get-tuple-element.15.held.three, bf16[2,960,256]{2,1,0:T(8,128)(2,1)S(1)} %get-tuple-element.24.done, f32[2,8,128]{2,1,0:T(8,128)S(1)} %get-tuple-element.33.mine), custom_call_target="tpu_custom_call" | custom-call | flops 503316480 | bytes 1966080 | tf_op jit(solution)/shard_map/gamma_second/pallas_call | solution.py:385
  18.8 0.0 collective-permute-done.4
  18.8 1.8 %collective-permute-done.5 = f32[2,8,128]{2,1,0:T(8,128)S(1)} collective-permute-done((f32[2,8,128]{2,1,0:T(8,128)S(1)}, f32[2,8,128]{2,1,0:T(8,128)S(1)}, u32[]{:S(2)}, u32[]{:S(2)}) %collective-permute-start.5) | collective-permute-done | bytes 8224 | tf_op jit(solution)/shard_map/ppermute | solution.py:384
  20.6 1.5 %collective-permute-start.6 = (f32[1,8,128]{2,1,0:T(8,128)S(1)}, f32[1,8,128]{2,1,0:T(8,128)S(1)}, u32[]{:S(2)}, u32[]{:S(2)}) collective-permute-start(f32[1,8,128]{2,1,0:T(8,128)S(1)} %constant_dynamic-slice_fusion), channel_id=1, source_target_pairs={{0,2},{2,0},{1,3},{3,1},{4,6},{6,4},{5,7},{7,5},{8,10},{10,8},{9,1... | collective-permute-start | bytes 12296 | tf_op jit(solution)/shard_map/ppermute | solution.py:234
  22.1 2.1 %collective-permute-done.6 = f32[1,8,128]{2,1,0:T(8,128)S(1)} collective-permute-done((f32[1,8,128]{2,1,0:T(8,128)S(1)}, f32[1,8,128]{2,1,0:T(8,128)S(1)}, u32[]{:S(2)}, u32[]{:S(2)}) %collective-permute-start.6) | collective-permute-done | bytes 4128 | tf_op jit(solution)/shard_map/ppermute | solution.py:234
  24.2 0.5 %collective-permute-start.7 = (f32[1,8,128]{2,1,0:T(8,128)S(1)}, f32[1,8,128]{2,1,0:T(8,128)S(1)}, u32[]{:S(2)}, u32[]{:S(2)}) collective-permute-start(f32[1,8,128]{2,1,0:T(8,128)S(1)} %dynamic-slice_add_fusion), channel_id=1, source_target_pairs={{0,1},{1,0},{2,3},{3,2},{4,5},{5,4},{6,7},{7,6},{8,9},{9,8},{10,11... | collective-permute-start | bytes 12296 | tf_op jit(solution)/shard_map/ppermute | solution.py:234
  24.7 0.8 %collective-permute-done.7 = f32[1,8,128]{2,1,0:T(8,128)S(1)} collective-permute-done((f32[1,8,128]{2,1,0:T(8,128)S(1)}, f32[1,8,128]{2,1,0:T(8,128)S(1)}, u32[]{:S(2)}, u32[]{:S(2)}) %collective-permute-start.7) | collective-permute-done | bytes 4128 | tf_op jit(solution)/shard_map/ppermute | solution.py:234
  25.5 0.6 %dynamic-slice_bitcast_fusion = f32[3,96]{1,0:T(4,128)} fusion(f32[1,8,128]{2,1,0:T(8,128)S(1)} %add.58, s32[]{:T(128)S(6)} %select_n.68), kind=kLoop, calls=%fused_computation.7 | loop fusion | bytes 2308 | tf_op jit(solution)/shard_map/dynamic_slice | solution.py:405
  (15 shorter events, 0.1 us)
Async XLA Ops:
  0.6 6.6 %copy-start.1 = (f32[8192]{0:T(1024)S(1)}, f32[8192]{0:T(1024)}, u32[]{:S(2)}) copy-start(f32[8192]{0:T(1024)} %param.11) | copy-start | bytes 98308
  0.6 6.5 %copy-start = (s32[1920]{0:T(1024)S(1)}, s32[1920]{0:T(1024)}, u32[]{:S(2)}) copy-start(s32[1920]{0:T(1024)} %firsts.1) | copy-start | bytes 23044
  0.7 6.5 %copy-start.5 = (f32[2]{0:T(128)S(1)}, f32[2]{0:T(128)}, u32[]{:S(2)}) copy-start(f32[2]{0:T(128)} %occupied.1) | copy-start | bytes 28
  0.7 6.5 %copy-start.2 = (f32[3,1920]{1,0:T(4,128)S(1)}, f32[3,1920]{1,0:T(4,128)}, u32[]{:S(2)}) copy-start(f32[3,1920]{1,0:T(4,128)} %weights.1) | copy-start | bytes 69124
  0.7 6.5 %copy-start.4 = (s32[2]{0:T(128)S(1)}, s32[2]{0:T(128)}, u32[]{:S(2)}) copy-start(s32[2]{0:T(128)} %valid.1) | copy-start | bytes 28
  0.7 6.5 %copy-start.3 = (s32[2,2]{1,0:T(2,128)S(1)}, s32[2,2]{1,0:T(2,128)}, u32[]{:S(2)}) copy-start(s32[2,2]{1,0:T(2,128)} %blocks.1) | copy-start | bytes 52
  2.7 1.8 %collective-permute-start = (bf16[272,256]{1,0:T(8,128)(2,1)S(1)}, bf16[272,256]{1,0:T(8,128)(2,1)S(1)}, u32[]{:S(2)}, u32[]{:S(2)}) collective-permute-start(bf16[272,256]{1,0:T(8,128)(2,1)S(1)} %get-tuple-element.16), channel_id=1, source_target_pairs={{0,1},{1,0},{2,3},{3,2},{4,5},{5,4},{6,7},{7,6},{8,9},{9,8},{10,11... | collective-permute-start | bytes 417800 | tf_op jit(solution)/shard_map/ppermute | solution.py:234
  4.5 6.6 %collective-permute-start.1 = (bf16[272,256]{1,0:T(8,128)(2,1)S(1)}, bf16[272,256]{1,0:T(8,128)(2,1)S(1)}, u32[]{:S(2)}, u32[]{:S(2)}) collective-permute-start(bf16[272,256]{1,0:T(8,128)(2,1)S(1)} %get-tuple-element.18), channel_id=1, source_target_pairs={{0,2},{2,0},{1,3},{3,1},{4,6},{6,4},{5,7},{7,5},{8,10},{10,8},{9,1... | collective-permute-start | bytes 417800 | tf_op jit(solution)/shard_map/ppermute | solution.py:234
  11.2 1.4 %collective-permute-start.2 = (bf16[272,256]{1,0:T(8,128)(2,1)S(1)}, bf16[272,256]{1,0:T(8,128)(2,1)S(1)}, u32[]{:S(2)}, u32[]{:S(2)}) collective-permute-start(bf16[272,256]{1,0:T(8,128)(2,1)S(1)} %multiply_convert_fusion.own), channel_id=1, source_target_pairs={{0,1},{1,0},{2,3},{3,2},{4,5},{5,4},{6,7},{7,6},{8,9},{9,8},{10,11... | collective-permute-start | bytes 417800 | tf_op jit(solution)/shard_map/ppermute | solution.py:234
  13.8 1.2 %collective-permute-start.3 = (f32[2,2,8,128]{3,2,1,0:T(8,128)S(1)}, f32[2,2,8,128]{3,2,1,0:T(8,128)S(1)}, u32[]{:S(2)}, u32[]{:S(2)}) collective-permute-start(f32[2,2,8,128]{3,2,1,0:T(8,128)S(1)} %pad_maximum_fusion.1), channel_id=1, source_target_pairs={{0,1},{1,0},{2,3},{3,2},{4,5},{5,4},{6,7},{7,6},{8,9},{9,8},{10,11... | collective-permute-start | bytes 49160 | tf_op jit(solution)/shard_map/ppermute | solution.py:234
  15.0 3.7 %collective-permute-start.4 = (f32[2,8,128]{2,1,0:T(8,128)S(1)}, f32[2,8,128]{2,1,0:T(8,128)S(1)}, u32[]{:S(2)}, u32[]{:S(2)}) collective-permute-start(f32[2,8,128]{2,1,0:T(8,128)S(1)} %get-tuple-element.32), channel_id=1, source_target_pairs={{0,4},{1,9},{4,0},{5,13},{8,12},{9,1},{12,8},{13,5},{2,6},{3,11},{... | collective-permute-start | bytes 24584 | tf_op jit(solution)/shard_map/ppermute | solution.py:383
  16.9 3.7 %collective-permute-start.5 = (f32[2,8,128]{2,1,0:T(8,128)S(1)}, f32[2,8,128]{2,1,0:T(8,128)S(1)}, u32[]{:S(2)}, u32[]{:S(2)}) collective-permute-start(f32[2,8,128]{2,1,0:T(8,128)S(1)} %get-tuple-element.33.mine), channel_id=1, source_target_pairs={{0,4},{1,13},{4,0},{5,9},{8,12},{9,5},{12,8},{13,1},{2,6},{3,15},{... | collective-permute-start | bytes 24584 | tf_op jit(solution)/shard_map/ppermute | solution.py:384
  20.6 3.6 %collective-permute-start.6 = (f32[1,8,128]{2,1,0:T(8,128)S(1)}, f32[1,8,128]{2,1,0:T(8,128)S(1)}, u32[]{:S(2)}, u32[]{:S(2)}) collective-permute-start(f32[1,8,128]{2,1,0:T(8,128)S(1)} %constant_dynamic-slice_fusion), channel_id=1, source_target_pairs={{0,2},{2,0},{1,3},{3,1},{4,6},{6,4},{5,7},{7,5},{8,10},{10,8},{9,1... | collective-permute-start | bytes 12296 | tf_op jit(solution)/shard_map/ppermute | solution.py:234
  24.2 1.3 %collective-permute-start.7 = (f32[1,8,128]{2,1,0:T(8,128)S(1)}, f32[1,8,128]{2,1,0:T(8,128)S(1)}, u32[]{:S(2)}, u32[]{:S(2)}) collective-permute-start(f32[1,8,128]{2,1,0:T(8,128)S(1)} %dynamic-slice_add_fusion), channel_id=1, source_target_pairs={{0,1},{1,0},{2,3},{3,2},{4,5},{5,4},{6,7},{7,6},{8,9},{9,8},{10,11... | collective-permute-start | bytes 12296 | tf_op jit(solution)/shard_map/ppermute | solution.py:234

commit v9 on v8

--- a/solution.py
+++ b/solution.py
@@ -9,7 +9,7 @@
 VBW = 128
 DOM = 2
 WID = VBW * DOM
-PACK = WID + 16
+PACK = WID + 8
 LANES = 128
 SEG = 128
 PACKED = 0

time: 26.3 us -> 26.1 us (level)
  no operation moved by 1% of the time
where the time goes in v9:
time: 26.1 us; the launch traced here: 26 us
  Pallas kernels  8.32 us (32%)
  waiting for transfers between devices  8.21 us (31%)
  starting transfers between devices  7.89 us (30%)
  between operations  0.85 us (3%)
  local copies, waits for them, and re-layouts  0.64 us (2%)
    ppermute x6, waiting for transfers between devices, swap(): return lax.ppermute(x, axis, [(i, i ^ bit) for i in range(count)])  6.41 us
    ppermute x6, starting transfers between devices, swap(): return lax.ppermute(x, axis, [(i, i ^ bit) for i in range(count)])  5.8 us
    pallas_call x1, Pallas kernels, shards(): pl.pallas_call(functools.partial(send_kernel, PIECES), out_shape=(jax.Sha...  2.01 us
    ppermute x1, starting transfers between devices, shards(): received = lax.ppermute(mine_sums[0], ('occ', 'rep'), across)  1.88 us
    ppermute x1, waiting for transfers between devices, shards(): received1 = lax.ppermute(mine_sums[1], ('occ', 'rep'), beside)  1.8 us
    pallas_call x1, Pallas kernels, shards(): pl.pallas_call(gamma_second, out_shape=(whole, like(mine_sums[1])), in_sp...  1.63 us
    pallas_call x1, Pallas kernels, shards(): pl.pallas_call(functools.partial(prep_kernel, window), out_shape=(jax.Sha...  1.34 us
    pallas_call x1, Pallas kernels, shards(): pl.pallas_call(functools.partial(weight_kernel, window, per, step), out_s...  1.07 us
  transfers between devices with their start and end apart: 8, of which 7 were waited for; matrix products, arithmetic and copies ran while one was open for 0% of the time, Pallas kernels for 20%

profile of v9, /device:TPU:0, one launch (start us, length us, event | category | flops | bytes accessed | tf_op | source)
XLA Modules:
  0.0 26.0 jit_solution(11233185381813390889)
XLA Ops:
  0.6 0.0 copy-start.1
  0.6 0.0 copy-start
  0.7 0.0 copy-start.5
  0.7 0.0 copy-start.2
  0.7 0.0 copy-start.4
  0.7 0.0 copy-start.3
  0.7 2.0 %send.1 = (bf16[264,256]{1,0:T(8,128)(2,1)S(1)}, bf16[2,1920,256]{2,1,0:T(8,128)(2,1)S(1)}) custom-call(bf16[2,1920,256]{2,1,0:T(8,128)(2,1)} %three.1), custom_call_target="tpu_custom_call" | custom-call | flops 503316480 | bytes 1966080 | tf_op jit(solution)/shard_map/send/pallas_call | solution.py:265
  2.7 0.8 %collective-permute-start = (bf16[264,256]{1,0:T(8,128)(2,1)S(1)}, bf16[264,256]{1,0:T(8,128)(2,1)S(1)}, u32[]{:S(2)}, u32[]{:S(2)}) collective-permute-start(bf16[264,256]{1,0:T(8,128)(2,1)S(1)} %get-tuple-element.16), channel_id=1, source_target_pairs={{0,1},{1,0},{2,3},{3,2},{4,5},{5,4},{6,7},{7,6},{8,9},{9,8},{10,11... | collective-permute-start | bytes 405512 | tf_op jit(solution)/shard_map/ppermute | solution.py:234
  3.5 0.7 %keep.1.mine = f32[264,256]{1,0:T(8,128)S(1)} custom-call(bf16[2,1920,256]{2,1,0:T(8,128)(2,1)S(1)} %get-tuple-element.15.held.three), custom_call_target="tpu_custom_call" | custom-call | flops 503316480 | bytes 1966080 | tf_op jit(solution)/shard_map/keep/pallas_call | solution.py:275
  4.2 0.2 collective-permute-done.received
  4.5 2.6 %collective-permute-start.1 = (bf16[264,256]{1,0:T(8,128)(2,1)S(1)}, bf16[264,256]{1,0:T(8,128)(2,1)S(1)}, u32[]{:S(2)}, u32[]{:S(2)}) collective-permute-start(bf16[264,256]{1,0:T(8,128)(2,1)S(1)} %get-tuple-element.18), channel_id=1, source_target_pairs={{0,2},{2,0},{1,3},{3,1},{4,6},{6,4},{5,7},{7,5},{8,10},{10,8},{9,1... | collective-permute-start | bytes 405512 | tf_op jit(solution)/shard_map/ppermute | solution.py:234
  7.2 0.0 copy-done
  7.2 1.3 %prep.1 = (f32[264,256]{1,0:T(8,128)S(1)}, bf16[1920,256]{1,0:T(8,128)(2,1)S(1)}, f32[8,1920]{1,0:T(8,128)S(1)}, s32[16,128]{1,0:T(8,128)S(1)}) custom-call(s32[2]{0:T(128)S(1)} %copy-done.4, s32[2,2]{1,0:T(2,128)S(1)} %copy-done.3, f32[2]{0:T(128)S(1)} %copy-done.5, f32[64,128]{1,0:T(8,128)S(1)} %bitcast.11, s32[1920]{0:T(1024)S(1)} %copy-done, ...), custom_call_target="tpu_custom_call" | custom-call | flops 1966080 | bytes 983040 | tf_op jit(solution)/shard_map/prep/pallas_call | solution.py:284
  8.6 2.5 %collective-permute-done.1 = bf16[264,256]{1,0:T(8,128)(2,1)S(1)} collective-permute-done((bf16[264,256]{1,0:T(8,128)(2,1)S(1)}, bf16[264,256]{1,0:T(8,128)(2,1)S(1)}, u32[]{:S(2)}, u32[]{:S(2)}) %collective-permute-start.1) | collective-permute-done | bytes 135200 | tf_op jit(solution)/shard_map/ppermute | solution.py:234
  11.1 0.1 multiply_convert_fusion.own
  11.1 0.1 collective-permute-start.2
  11.3 0.7 %ahead.1 = f32[1920,128]{1,0:T(8,128)S(1)} custom-call(bf16[264,256]{1,0:T(8,128)(2,1)S(1)} %multiply_convert_fusion.own, bf16[2,1920,256]{2,1,0:T(8,128)(2,1)S(1)} %get-tuple-element.15.held.three), custom_call_target="tpu_custom_call" | custom-call | flops 503316480 | bytes 1966080 | tf_op jit(solution)/shard_map/ahead/pallas_call | solution.py:324
  12.0 0.6 %collective-permute-done.2.other = bf16[264,256]{1,0:T(8,128)(2,1)S(1)} collective-permute-done((bf16[264,256]{1,0:T(8,128)(2,1)S(1)}, bf16[264,256]{1,0:T(8,128)(2,1)S(1)}, u32[]{:S(2)}, u32[]{:S(2)}) %collective-permute-start.2) | collective-permute-done | bytes 135200 | tf_op jit(solution)/shard_map/ppermute | solution.py:234
  12.6 1.1 %weight.1 = f32[8,8,128]{2,1,0:T(8,128)S(1)} custom-call(s32[16,128]{1,0:T(8,128)S(1)} %get-tuple-element.20.starts, bf16[264,256]{1,0:T(8,128)(2,1)S(1)} %collective-permute-done.2.other, f32[1920,128]{1,0:T(8,128)S(1)} %ahead.1, bf16[2,1920,256]{2,1,0:T(8,128)(2,1)S(1)} %get-tuple-element.15.held.three, bf16[1920,256]{1,0:T(8,128)(2,1)S(1)} %get-tuple-element.21.hot, ...), custom_call_target="tpu_custom_call" | custom-call | flops 503316480 | bytes 1966080 | tf_op jit(solution)/shard_map/weight/pallas_call | solution.py:333
  13.7 0.3 %collective-permute-start.3 = (f32[2,2,8,128]{3,2,1,0:T(8,128)S(1)}, f32[2,2,8,128]{3,2,1,0:T(8,128)S(1)}, u32[]{:S(2)}, u32[]{:S(2)}) collective-permute-start(f32[2,2,8,128]{3,2,1,0:T(8,128)S(1)} %pad_maximum_fusion.1), channel_id=1, source_target_pairs={{0,1},{1,0},{2,3},{3,2},{4,5},{5,4},{6,7},{7,6},{8,9},{9,8},{10,11... | collective-permute-start | bytes 49160 | tf_op jit(solution)/shard_map/ppermute | solution.py:234
  14.0 0.8 %gamma_first.1 = (f32[2,2,8,128]{3,2,1,0:T(8,128)S(1)}, bf16[512,512]{1,0:T(8,128)(2,1)S(1)}, bf16[2,960,256]{2,1,0:T(8,128)(2,1)S(1)}) custom-call(bf16[264,256]{1,0:T(8,128)(2,1)S(1)} %multiply_convert_fusion.own, bf16[264,256]{1,0:T(8,128)(2,1)S(1)} %collective-permute-done.2.other, bf16[2,1920,256]{2,1,0:T(8,128)(2,1)S(1)} %get-tuple-element.15.held.three, ...), custom_call_target="tpu_custom_call" | custom-call | flops 503316480 | bytes 1966080 | tf_op jit(solution)/shard_map/gamma_first/pallas_call | solution.py:370
  14.8 0.1 collective-permute-done.3
  14.9 1.9 %collective-permute-start.4 = (f32[2,8,128]{2,1,0:T(8,128)S(1)}, f32[2,8,128]{2,1,0:T(8,128)S(1)}, u32[]{:S(2)}, u32[]{:S(2)}) collective-permute-start(f32[2,8,128]{2,1,0:T(8,128)S(1)} %get-tuple-element.32), channel_id=1, source_target_pairs={{0,4},{1,9},{4,0},{5,13},{8,12},{9,1},{12,8},{13,5},{2,6},{3,11},{... | collective-permute-start | bytes 24584 | tf_op jit(solution)/shard_map/ppermute | solution.py:383
  16.8 0.2 collective-permute-start.5
  17.0 1.6 %gamma_second.1 = (bf16[2,1920,256]{2,1,0:T(8,128)(2,1)}, f32[2,8,128]{2,1,0:T(8,128)S(1)}) custom-call(bf16[512,512]{1,0:T(8,128)(2,1)S(1)} %get-tuple-element.23.table, bf16[2,1920,256]{2,1,0:T(8,128)(2,1)S(1)} %get-tuple-element.15.held.three, bf16[2,960,256]{2,1,0:T(8,128)(2,1)S(1)} %get-tuple-element.24.done, f32[2,8,128]{2,1,0:T(8,128)S(1)} %get-tuple-element.33.mine), custom_call_target="tpu_custom_call" | custom-call | flops 503316480 | bytes 1966080 | tf_op jit(solution)/shard_map/gamma_second/pallas_call | solution.py:385
  18.7 0.0 collective-permute-done.4
  18.7 1.8 %collective-permute-done.5 = f32[2,8,128]{2,1,0:T(8,128)S(1)} collective-permute-done((f32[2,8,128]{2,1,0:T(8,128)S(1)}, f32[2,8,128]{2,1,0:T(8,128)S(1)}, u32[]{:S(2)}, u32[]{:S(2)}) %collective-permute-start.5) | collective-permute-done | bytes 8224 | tf_op jit(solution)/shard_map/ppermute | solution.py:384
  20.5 1.5 %collective-permute-start.6 = (f32[1,8,128]{2,1,0:T(8,128)S(1)}, f32[1,8,128]{2,1,0:T(8,128)S(1)}, u32[]{:S(2)}, u32[]{:S(2)}) collective-permute-start(f32[1,8,128]{2,1,0:T(8,128)S(1)} %constant_dynamic-slice_fusion), channel_id=1, source_target_pairs={{0,2},{2,0},{1,3},{3,1},{4,6},{6,4},{5,7},{7,5},{8,10},{10,8},{9,1... | collective-permute-start | bytes 12296 | tf_op jit(solution)/shard_map/ppermute | solution.py:234
  22.0 2.1 %collective-permute-done.6 = f32[1,8,128]{2,1,0:T(8,128)S(1)} collective-permute-done((f32[1,8,128]{2,1,0:T(8,128)S(1)}, f32[1,8,128]{2,1,0:T(8,128)S(1)}, u32[]{:S(2)}, u32[]{:S(2)}) %collective-permute-start.6) | collective-permute-done | bytes 4128 | tf_op jit(solution)/shard_map/ppermute | solution.py:234
  24.1 0.5 %collective-permute-start.7 = (f32[1,8,128]{2,1,0:T(8,128)S(1)}, f32[1,8,128]{2,1,0:T(8,128)S(1)}, u32[]{:S(2)}, u32[]{:S(2)}) collective-permute-start(f32[1,8,128]{2,1,0:T(8,128)S(1)} %dynamic-slice_add_fusion), channel_id=1, source_target_pairs={{0,1},{1,0},{2,3},{3,2},{4,5},{5,4},{6,7},{7,6},{8,9},{9,8},{10,11... | collective-permute-start | bytes 12296 | tf_op jit(solution)/shard_map/ppermute | solution.py:234
  24.6 0.8 %collective-permute-done.7 = f32[1,8,128]{2,1,0:T(8,128)S(1)} collective-permute-done((f32[1,8,128]{2,1,0:T(8,128)S(1)}, f32[1,8,128]{2,1,0:T(8,128)S(1)}, u32[]{:S(2)}, u32[]{:S(2)}) %collective-permute-start.7) | collective-permute-done | bytes 4128 | tf_op jit(solution)/shard_map/ppermute | solution.py:234
  25.4 0.6 %dynamic-slice_bitcast_fusion = f32[3,96]{1,0:T(4,128)} fusion(f32[1,8,128]{2,1,0:T(8,128)S(1)} %add.58, s32[]{:T(128)S(6)} %select_n.68), kind=kLoop, calls=%fused_computation.7 | loop fusion | bytes 2308 | tf_op jit(solution)/shard_map/dynamic_slice | solution.py:405
  (15 shorter events, 0.1 us)
Async XLA Ops:
  0.6 6.5 %copy-start.1 = (f32[8192]{0:T(1024)S(1)}, f32[8192]{0:T(1024)}, u32[]{:S(2)}) copy-start(f32[8192]{0:T(1024)} %param.11) | copy-start | bytes 98308
  0.6 6.5 %copy-start = (s32[1920]{0:T(1024)S(1)}, s32[1920]{0:T(1024)}, u32[]{:S(2)}) copy-start(s32[1920]{0:T(1024)} %firsts.1) | copy-start | bytes 23044
  0.7 6.5 %copy-start.5 = (f32[2]{0:T(128)S(1)}, f32[2]{0:T(128)}, u32[]{:S(2)}) copy-start(f32[2]{0:T(128)} %occupied.1) | copy-start | bytes 28
  0.7 6.5 %copy-start.2 = (f32[3,1920]{1,0:T(4,128)S(1)}, f32[3,1920]{1,0:T(4,128)}, u32[]{:S(2)}) copy-start(f32[3,1920]{1,0:T(4,128)} %weights.1) | copy-start | bytes 69124
  0.7 6.5 %copy-start.4 = (s32[2]{0:T(128)S(1)}, s32[2]{0:T(128)}, u32[]{:S(2)}) copy-start(s32[2]{0:T(128)} %valid.1) | copy-start | bytes 28
  0.7 6.5 %copy-start.3 = (s32[2,2]{1,0:T(2,128)S(1)}, s32[2,2]{1,0:T(2,128)}, u32[]{:S(2)}) copy-start(s32[2,2]{1,0:T(2,128)} %blocks.1) | copy-start | bytes 52
  2.7 1.8 %collective-permute-start = (bf16[264,256]{1,0:T(8,128)(2,1)S(1)}, bf16[264,256]{1,0:T(8,128)(2,1)S(1)}, u32[]{:S(2)}, u32[]{:S(2)}) collective-permute-start(bf16[264,256]{1,0:T(8,128)(2,1)S(1)} %get-tuple-element.16), channel_id=1, source_target_pairs={{0,1},{1,0},{2,3},{3,2},{4,5},{5,4},{6,7},{7,6},{8,9},{9,8},{10,11... | collective-permute-start | bytes 405512 | tf_op jit(solution)/shard_map/ppermute | solution.py:234
  4.5 6.5 %collective-permute-start.1 = (bf16[264,256]{1,0:T(8,128)(2,1)S(1)}, bf16[264,256]{1,0:T(8,128)(2,1)S(1)}, u32[]{:S(2)}, u32[]{:S(2)}) collective-permute-start(bf16[264,256]{1,0:T(8,128)(2,1)S(1)} %get-tuple-element.18), channel_id=1, source_target_pairs={{0,2},{2,0},{1,3},{3,1},{4,6},{6,4},{5,7},{7,5},{8,10},{10,8},{9,1... | collective-permute-start | bytes 405512 | tf_op jit(solution)/shard_map/ppermute | solution.py:234
  11.1 1.4 %collective-permute-start.2 = (bf16[264,256]{1,0:T(8,128)(2,1)S(1)}, bf16[264,256]{1,0:T(8,128)(2,1)S(1)}, u32[]{:S(2)}, u32[]{:S(2)}) collective-permute-start(bf16[264,256]{1,0:T(8,128)(2,1)S(1)} %multiply_convert_fusion.own), channel_id=1, source_target_pairs={{0,1},{1,0},{2,3},{3,2},{4,5},{5,4},{6,7},{7,6},{8,9},{9,8},{10,11... | collective-permute-start | bytes 405512 | tf_op jit(solution)/shard_map/ppermute | solution.py:234
  13.7 1.2 %collective-permute-start.3 = (f32[2,2,8,128]{3,2,1,0:T(8,128)S(1)}, f32[2,2,8,128]{3,2,1,0:T(8,128)S(1)}, u32[]{:S(2)}, u32[]{:S(2)}) collective-permute-start(f32[2,2,8,128]{3,2,1,0:T(8,128)S(1)} %pad_maximum_fusion.1), channel_id=1, source_target_pairs={{0,1},{1,0},{2,3},{3,2},{4,5},{5,4},{6,7},{7,6},{8,9},{9,8},{10,11... | collective-permute-start | bytes 49160 | tf_op jit(solution)/shard_map/ppermute | solution.py:234
  14.9 3.7 %collective-permute-start.4 = (f32[2,8,128]{2,1,0:T(8,128)S(1)}, f32[2,8,128]{2,1,0:T(8,128)S(1)}, u32[]{:S(2)}, u32[]{:S(2)}) collective-permute-start(f32[2,8,128]{2,1,0:T(8,128)S(1)} %get-tuple-element.32), channel_id=1, source_target_pairs={{0,4},{1,9},{4,0},{5,13},{8,12},{9,1},{12,8},{13,5},{2,6},{3,11},{... | collective-permute-start | bytes 24584 | tf_op jit(solution)/shard_map/ppermute | solution.py:383
  16.8 3.7 %collective-permute-start.5 = (f32[2,8,128]{2,1,0:T(8,128)S(1)}, f32[2,8,128]{2,1,0:T(8,128)S(1)}, u32[]{:S(2)}, u32[]{:S(2)}) collective-permute-start(f32[2,8,128]{2,1,0:T(8,128)S(1)} %get-tuple-element.33.mine), channel_id=1, source_target_pairs={{0,4},{1,13},{4,0},{5,9},{8,12},{9,5},{12,8},{13,1},{2,6},{3,15},{... | collective-permute-start | bytes 24584 | tf_op jit(solution)/shard_map/ppermute | solution.py:384
  20.5 3.6 %collective-permute-start.6 = (f32[1,8,128]{2,1,0:T(8,128)S(1)}, f32[1,8,128]{2,1,0:T(8,128)S(1)}, u32[]{:S(2)}, u32[]{:S(2)}) collective-permute-start(f32[1,8,128]{2,1,0:T(8,128)S(1)} %constant_dynamic-slice_fusion), channel_id=1, source_target_pairs={{0,2},{2,0},{1,3},{3,1},{4,6},{6,4},{5,7},{7,5},{8,10},{10,8},{9,1... | collective-permute-start | bytes 12296 | tf_op jit(solution)/shard_map/ppermute | solution.py:234
  24.1 1.3 %collective-permute-start.7 = (f32[1,8,128]{2,1,0:T(8,128)S(1)}, f32[1,8,128]{2,1,0:T(8,128)S(1)}, u32[]{:S(2)}, u32[]{:S(2)}) collective-permute-start(f32[1,8,128]{2,1,0:T(8,128)S(1)} %dynamic-slice_add_fusion), channel_id=1, source_target_pairs={{0,1},{1,0},{2,3},{3,2},{4,5},{5,4},{6,7},{7,6},{8,9},{9,8},{10,11... | collective-permute-start | bytes 12296 | tf_op jit(solution)/shard_map/ppermute | solution.py:234

commit v10 on v9

--- a/solution.py
+++ b/solution.py
@@ -13,7 +13,7 @@
 LANES = 128
 SEG = 128
 PACKED = 0
-PIECES = (1280, 640)
+PIECES = (960, 960)
 OPPOSITE_SCALE = 1.3
 F32 = jnp.float32
 BF16 = jnp.bfloat16

time: 26.1 us -> 26.2 us (level)
  no operation moved by 1% of the time
where the time goes in v10:
time: 26.2 us; the launch traced here: 26 us
  Pallas kernels  8.35 us (32%)
  waiting for transfers between devices  8.21 us (31%)
  starting transfers between devices  7.89 us (30%)
  between operations  0.85 us (3%)
  local copies, waits for them, and re-layouts  0.64 us (2%)
    ppermute x6, waiting for transfers between devices, swap(): return lax.ppermute(x, axis, [(i, i ^ bit) for i in range(count)])  6.4 us
    ppermute x6, starting transfers between devices, swap(): return lax.ppermute(x, axis, [(i, i ^ bit) for i in range(count)])  5.8 us
    pallas_call x1, Pallas kernels, shards(): pl.pallas_call(functools.partial(send_kernel, PIECES), out_shape=(jax.Sha...  2.04 us
    ppermute x1, starting transfers between devices, shards(): received = lax.ppermute(mine_sums[0], ('occ', 'rep'), across)  1.88 us
    ppermute x1, waiting for transfers between devices, shards(): received1 = lax.ppermute(mine_sums[1], ('occ', 'rep'), beside)  1.8 us
    pallas_call x1, Pallas kernels, shards(): pl.pallas_call(gamma_second, out_shape=(whole, like(mine_sums[1])), in_sp...  1.63 us
    pallas_call x1, Pallas kernels, shards(): pl.pallas_call(functools.partial(prep_kernel, window), out_shape=(jax.Sha...  1.34 us
    pallas_call x1, Pallas kernels, shards(): pl.pallas_call(functools.partial(weight_kernel, window, per, step), out_s...  1.07 us
  transfers between devices with their start and end apart: 8, of which 7 were waited for; matrix products, arithmetic and copies ran while one was open for 0% of the time, Pallas kernels for 20%

profile of v10, /device:TPU:0, one launch (start us, length us, event | category | flops | bytes accessed | tf_op | source)
XLA Modules:
  0.0 26.0 jit_solution(6167243752988057977)
XLA Ops:
  0.6 0.0 copy-start.1
  0.6 0.0 copy-start
  0.7 0.0 copy-start.5
  0.7 0.0 copy-start.2
  0.7 0.0 copy-start.4
  0.7 2.0 %send.1 = (bf16[264,256]{1,0:T(8,128)(2,1)S(1)}, bf16[2,1920,256]{2,1,0:T(8,128)(2,1)S(1)}) custom-call(bf16[2,1920,256]{2,1,0:T(8,128)(2,1)} %three.1), custom_call_target="tpu_custom_call" | custom-call | flops 503316480 | bytes 1966080 | tf_op jit(solution)/shard_map/send/pallas_call | solution.py:265
  2.7 0.8 %collective-permute-start = (bf16[264,256]{1,0:T(8,128)(2,1)S(1)}, bf16[264,256]{1,0:T(8,128)(2,1)S(1)}, u32[]{:S(2)}, u32[]{:S(2)}) collective-permute-start(bf16[264,256]{1,0:T(8,128)(2,1)S(1)} %get-tuple-element.16), channel_id=1, source_target_pairs={{0,1},{1,0},{2,3},{3,2},{4,5},{5,4},{6,7},{7,6},{8,9},{9,8},{10,11... | collective-permute-start | bytes 405512 | tf_op jit(solution)/shard_map/ppermute | solution.py:234
  3.5 0.7 %keep.1.mine = f32[264,256]{1,0:T(8,128)S(1)} custom-call(bf16[2,1920,256]{2,1,0:T(8,128)(2,1)S(1)} %get-tuple-element.15.held.three), custom_call_target="tpu_custom_call" | custom-call | flops 503316480 | bytes 1966080 | tf_op jit(solution)/shard_map/keep/pallas_call | solution.py:275
  4.3 0.2 collective-permute-done.received
  4.6 2.6 %collective-permute-start.1 = (bf16[264,256]{1,0:T(8,128)(2,1)S(1)}, bf16[264,256]{1,0:T(8,128)(2,1)S(1)}, u32[]{:S(2)}, u32[]{:S(2)}) collective-permute-start(bf16[264,256]{1,0:T(8,128)(2,1)S(1)} %get-tuple-element.18), channel_id=1, source_target_pairs={{0,2},{2,0},{1,3},{3,1},{4,6},{6,4},{5,7},{7,5},{8,10},{10,8},{9,1... | collective-permute-start | bytes 405512 | tf_op jit(solution)/shard_map/ppermute | solution.py:234
  7.2 0.0 copy-done
  7.2 0.0 copy-done.2
  7.2 1.3 %prep.1 = (f32[264,256]{1,0:T(8,128)S(1)}, bf16[1920,256]{1,0:T(8,128)(2,1)S(1)}, f32[8,1920]{1,0:T(8,128)S(1)}, s32[16,128]{1,0:T(8,128)S(1)}) custom-call(s32[2]{0:T(128)S(1)} %copy-done.4, s32[2,2]{1,0:T(2,128)S(1)} %copy-done.3, f32[2]{0:T(128)S(1)} %copy-done.5, f32[64,128]{1,0:T(8,128)S(1)} %bitcast.11, s32[1920]{0:T(1024)S(1)} %copy-done, ...), custom_call_target="tpu_custom_call" | custom-call | flops 1966080 | bytes 983040 | tf_op jit(solution)/shard_map/prep/pallas_call | solution.py:284
  8.6 2.5 %collective-permute-done.1 = bf16[264,256]{1,0:T(8,128)(2,1)S(1)} collective-permute-done((bf16[264,256]{1,0:T(8,128)(2,1)S(1)}, bf16[264,256]{1,0:T(8,128)(2,1)S(1)}, u32[]{:S(2)}, u32[]{:S(2)}) %collective-permute-start.1) | collective-permute-done | bytes 135200 | tf_op jit(solution)/shard_map/ppermute | solution.py:234
  11.1 0.1 multiply_convert_fusion.own
  11.2 0.1 collective-permute-start.2
  11.3 0.7 %ahead.1 = f32[1920,128]{1,0:T(8,128)S(1)} custom-call(bf16[264,256]{1,0:T(8,128)(2,1)S(1)} %multiply_convert_fusion.own, bf16[2,1920,256]{2,1,0:T(8,128)(2,1)S(1)} %get-tuple-element.15.held.three), custom_call_target="tpu_custom_call" | custom-call | flops 503316480 | bytes 1966080 | tf_op jit(solution)/shard_map/ahead/pallas_call | solution.py:324
  12.0 0.6 %collective-permute-done.2.other = bf16[264,256]{1,0:T(8,128)(2,1)S(1)} collective-permute-done((bf16[264,256]{1,0:T(8,128)(2,1)S(1)}, bf16[264,256]{1,0:T(8,128)(2,1)S(1)}, u32[]{:S(2)}, u32[]{:S(2)}) %collective-permute-start.2) | collective-permute-done | bytes 135200 | tf_op jit(solution)/shard_map/ppermute | solution.py:234
  12.6 1.1 %weight.1 = f32[8,8,128]{2,1,0:T(8,128)S(1)} custom-call(s32[16,128]{1,0:T(8,128)S(1)} %get-tuple-element.20.starts, bf16[264,256]{1,0:T(8,128)(2,1)S(1)} %collective-permute-done.2.other, f32[1920,128]{1,0:T(8,128)S(1)} %ahead.1, bf16[2,1920,256]{2,1,0:T(8,128)(2,1)S(1)} %get-tuple-element.15.held.three, bf16[1920,256]{1,0:T(8,128)(2,1)S(1)} %get-tuple-element.21.hot, ...), custom_call_target="tpu_custom_call" | custom-call | flops 503316480 | bytes 1966080 | tf_op jit(solution)/shard_map/weight/pallas_call | solution.py:333
  13.7 0.3 %collective-permute-start.3 = (f32[2,2,8,128]{3,2,1,0:T(8,128)S(1)}, f32[2,2,8,128]{3,2,1,0:T(8,128)S(1)}, u32[]{:S(2)}, u32[]{:S(2)}) collective-permute-start(f32[2,2,8,128]{3,2,1,0:T(8,128)S(1)} %pad_maximum_fusion.1), channel_id=1, source_target_pairs={{0,1},{1,0},{2,3},{3,2},{4,5},{5,4},{6,7},{7,6},{8,9},{9,8},{10,11... | collective-permute-start | bytes 49160 | tf_op jit(solution)/shard_map/ppermute | solution.py:234
  14.0 0.8 %gamma_first.1 = (f32[2,2,8,128]{3,2,1,0:T(8,128)S(1)}, bf16[512,512]{1,0:T(8,128)(2,1)S(1)}, bf16[2,960,256]{2,1,0:T(8,128)(2,1)S(1)}) custom-call(bf16[264,256]{1,0:T(8,128)(2,1)S(1)} %multiply_convert_fusion.own, bf16[264,256]{1,0:T(8,128)(2,1)S(1)} %collective-permute-done.2.other, bf16[2,1920,256]{2,1,0:T(8,128)(2,1)S(1)} %get-tuple-element.15.held.three, ...), custom_call_target="tpu_custom_call" | custom-call | flops 503316480 | bytes 1966080 | tf_op jit(solution)/shard_map/gamma_first/pallas_call | solution.py:370
  14.8 0.1 collective-permute-done.3
  15.0 1.9 %collective-permute-start.4 = (f32[2,8,128]{2,1,0:T(8,128)S(1)}, f32[2,8,128]{2,1,0:T(8,128)S(1)}, u32[]{:S(2)}, u32[]{:S(2)}) collective-permute-start(f32[2,8,128]{2,1,0:T(8,128)S(1)} %get-tuple-element.32), channel_id=1, source_target_pairs={{0,4},{1,9},{4,0},{5,13},{8,12},{9,1},{12,8},{13,5},{2,6},{3,11},{... | collective-permute-start | bytes 24584 | tf_op jit(solution)/shard_map/ppermute | solution.py:383
  16.8 0.2 collective-permute-start.5
  17.1 1.6 %gamma_second.1 = (bf16[2,1920,256]{2,1,0:T(8,128)(2,1)}, f32[2,8,128]{2,1,0:T(8,128)S(1)}) custom-call(bf16[512,512]{1,0:T(8,128)(2,1)S(1)} %get-tuple-element.23.table, bf16[2,1920,256]{2,1,0:T(8,128)(2,1)S(1)} %get-tuple-element.15.held.three, bf16[2,960,256]{2,1,0:T(8,128)(2,1)S(1)} %get-tuple-element.24.done, f32[2,8,128]{2,1,0:T(8,128)S(1)} %get-tuple-element.33.mine), custom_call_target="tpu_custom_call" | custom-call | flops 503316480 | bytes 1966080 | tf_op jit(solution)/shard_map/gamma_second/pallas_call | solution.py:385
  18.7 0.0 collective-permute-done.4
  18.7 1.8 %collective-permute-done.5 = f32[2,8,128]{2,1,0:T(8,128)S(1)} collective-permute-done((f32[2,8,128]{2,1,0:T(8,128)S(1)}, f32[2,8,128]{2,1,0:T(8,128)S(1)}, u32[]{:S(2)}, u32[]{:S(2)}) %collective-permute-start.5) | collective-permute-done | bytes 8224 | tf_op jit(solution)/shard_map/ppermute | solution.py:384
  20.5 1.5 %collective-permute-start.6 = (f32[1,8,128]{2,1,0:T(8,128)S(1)}, f32[1,8,128]{2,1,0:T(8,128)S(1)}, u32[]{:S(2)}, u32[]{:S(2)}) collective-permute-start(f32[1,8,128]{2,1,0:T(8,128)S(1)} %constant_dynamic-slice_fusion), channel_id=1, source_target_pairs={{0,2},{2,0},{1,3},{3,1},{4,6},{6,4},{5,7},{7,5},{8,10},{10,8},{9,1... | collective-permute-start | bytes 12296 | tf_op jit(solution)/shard_map/ppermute | solution.py:234
  22.0 2.1 %collective-permute-done.6 = f32[1,8,128]{2,1,0:T(8,128)S(1)} collective-permute-done((f32[1,8,128]{2,1,0:T(8,128)S(1)}, f32[1,8,128]{2,1,0:T(8,128)S(1)}, u32[]{:S(2)}, u32[]{:S(2)}) %collective-permute-start.6) | collective-permute-done | bytes 4128 | tf_op jit(solution)/shard_map/ppermute | solution.py:234
  24.1 0.5 %collective-permute-start.7 = (f32[1,8,128]{2,1,0:T(8,128)S(1)}, f32[1,8,128]{2,1,0:T(8,128)S(1)}, u32[]{:S(2)}, u32[]{:S(2)}) collective-permute-start(f32[1,8,128]{2,1,0:T(8,128)S(1)} %dynamic-slice_add_fusion), channel_id=1, source_target_pairs={{0,1},{1,0},{2,3},{3,2},{4,5},{5,4},{6,7},{7,6},{8,9},{9,8},{10,11... | collective-permute-start | bytes 12296 | tf_op jit(solution)/shard_map/ppermute | solution.py:234
  24.6 0.8 %collective-permute-done.7 = f32[1,8,128]{2,1,0:T(8,128)S(1)} collective-permute-done((f32[1,8,128]{2,1,0:T(8,128)S(1)}, f32[1,8,128]{2,1,0:T(8,128)S(1)}, u32[]{:S(2)}, u32[]{:S(2)}) %collective-permute-start.7) | collective-permute-done | bytes 4128 | tf_op jit(solution)/shard_map/ppermute | solution.py:234
  25.4 0.6 %dynamic-slice_bitcast_fusion = f32[3,96]{1,0:T(4,128)} fusion(f32[1,8,128]{2,1,0:T(8,128)S(1)} %add.58, s32[]{:T(128)S(6)} %select_n.68), kind=kLoop, calls=%fused_computation.7 | loop fusion | bytes 2308 | tf_op jit(solution)/shard_map/dynamic_slice | solution.py:405
  (15 shorter events, 0.1 us)
Async XLA Ops:
  0.6 6.6 %copy-start.1 = (f32[8192]{0:T(1024)S(1)}, f32[8192]{0:T(1024)}, u32[]{:S(2)}) copy-start(f32[8192]{0:T(1024)} %param.11) | copy-start | bytes 98308
  0.6 6.6 %copy-start = (s32[1920]{0:T(1024)S(1)}, s32[1920]{0:T(1024)}, u32[]{:S(2)}) copy-start(s32[1920]{0:T(1024)} %firsts.1) | copy-start | bytes 23044
  0.7 6.6 %copy-start.5 = (f32[2]{0:T(128)S(1)}, f32[2]{0:T(128)}, u32[]{:S(2)}) copy-start(f32[2]{0:T(128)} %occupied.1) | copy-start | bytes 28
  0.7 6.6 %copy-start.2 = (f32[3,1920]{1,0:T(4,128)S(1)}, f32[3,1920]{1,0:T(4,128)}, u32[]{:S(2)}) copy-start(f32[3,1920]{1,0:T(4,128)} %weights.1) | copy-start | bytes 69124
  0.7 6.5 %copy-start.4 = (s32[2]{0:T(128)S(1)}, s32[2]{0:T(128)}, u32[]{:S(2)}) copy-start(s32[2]{0:T(128)} %valid.1) | copy-start | bytes 28
  0.7 6.5 %copy-start.3 = (s32[2,2]{1,0:T(2,128)S(1)}, s32[2,2]{1,0:T(2,128)}, u32[]{:S(2)}) copy-start(s32[2,2]{1,0:T(2,128)} %blocks.1) | copy-start | bytes 52
  2.7 1.8 %collective-permute-start = (bf16[264,256]{1,0:T(8,128)(2,1)S(1)}, bf16[264,256]{1,0:T(8,128)(2,1)S(1)}, u32[]{:S(2)}, u32[]{:S(2)}) collective-permute-start(bf16[264,256]{1,0:T(8,128)(2,1)S(1)} %get-tuple-element.16), channel_id=1, source_target_pairs={{0,1},{1,0},{2,3},{3,2},{4,5},{5,4},{6,7},{7,6},{8,9},{9,8},{10,11... | collective-permute-start | bytes 405512 | tf_op jit(solution)/shard_map/ppermute | solution.py:234
  4.6 6.5 %collective-permute-start.1 = (bf16[264,256]{1,0:T(8,128)(2,1)S(1)}, bf16[264,256]{1,0:T(8,128)(2,1)S(1)}, u32[]{:S(2)}, u32[]{:S(2)}) collective-permute-start(bf16[264,256]{1,0:T(8,128)(2,1)S(1)} %get-tuple-element.18), channel_id=1, source_target_pairs={{0,2},{2,0},{1,3},{3,1},{4,6},{6,4},{5,7},{7,5},{8,10},{10,8},{9,1... | collective-permute-start | bytes 405512 | tf_op jit(solution)/shard_map/ppermute | solution.py:234
  11.2 1.4 %collective-permute-start.2 = (bf16[264,256]{1,0:T(8,128)(2,1)S(1)}, bf16[264,256]{1,0:T(8,128)(2,1)S(1)}, u32[]{:S(2)}, u32[]{:S(2)}) collective-permute-start(bf16[264,256]{1,0:T(8,128)(2,1)S(1)} %multiply_convert_fusion.own), channel_id=1, source_target_pairs={{0,1},{1,0},{2,3},{3,2},{4,5},{5,4},{6,7},{7,6},{8,9},{9,8},{10,11... | collective-permute-start | bytes 405512 | tf_op jit(solution)/shard_map/ppermute | solution.py:234
  13.7 1.2 %collective-permute-start.3 = (f32[2,2,8,128]{3,2,1,0:T(8,128)S(1)}, f32[2,2,8,128]{3,2,1,0:T(8,128)S(1)}, u32[]{:S(2)}, u32[]{:S(2)}) collective-permute-start(f32[2,2,8,128]{3,2,1,0:T(8,128)S(1)} %pad_maximum_fusion.1), channel_id=1, source_target_pairs={{0,1},{1,0},{2,3},{3,2},{4,5},{5,4},{6,7},{7,6},{8,9},{9,8},{10,11... | collective-permute-start | bytes 49160 | tf_op jit(solution)/shard_map/ppermute | solution.py:234
  15.0 3.7 %collective-permute-start.4 = (f32[2,8,128]{2,1,0:T(8,128)S(1)}, f32[2,8,128]{2,1,0:T(8,128)S(1)}, u32[]{:S(2)}, u32[]{:S(2)}) collective-permute-start(f32[2,8,128]{2,1,0:T(8,128)S(1)} %get-tuple-element.32), channel_id=1, source_target_pairs={{0,4},{1,9},{4,0},{5,13},{8,12},{9,1},{12,8},{13,5},{2,6},{3,11},{... | collective-permute-start | bytes 24584 | tf_op jit(solution)/shard_map/ppermute | solution.py:383
  16.8 3.7 %collective-permute-start.5 = (f32[2,8,128]{2,1,0:T(8,128)S(1)}, f32[2,8,128]{2,1,0:T(8,128)S(1)}, u32[]{:S(2)}, u32[]{:S(2)}) collective-permute-start(f32[2,8,128]{2,1,0:T(8,128)S(1)} %get-tuple-element.33.mine), channel_id=1, source_target_pairs={{0,4},{1,13},{4,0},{5,9},{8,12},{9,5},{12,8},{13,1},{2,6},{3,15},{... | collective-permute-start | bytes 24584 | tf_op jit(solution)/shard_map/ppermute | solution.py:384
  20.5 3.6 %collective-permute-start.6 = (f32[1,8,128]{2,1,0:T(8,128)S(1)}, f32[1,8,128]{2,1,0:T(8,128)S(1)}, u32[]{:S(2)}, u32[]{:S(2)}) collective-permute-start(f32[1,8,128]{2,1,0:T(8,128)S(1)} %constant_dynamic-slice_fusion), channel_id=1, source_target_pairs={{0,2},{2,0},{1,3},{3,1},{4,6},{6,4},{5,7},{7,5},{8,10},{10,8},{9,1... | collective-permute-start | bytes 12296 | tf_op jit(solution)/shard_map/ppermute | solution.py:234
  24.1 1.3 %collective-permute-start.7 = (f32[1,8,128]{2,1,0:T(8,128)S(1)}, f32[1,8,128]{2,1,0:T(8,128)S(1)}, u32[]{:S(2)}, u32[]{:S(2)}) collective-permute-start(f32[1,8,128]{2,1,0:T(8,128)S(1)} %dynamic-slice_add_fusion), channel_id=1, source_target_pairs={{0,1},{1,0},{2,3},{3,2},{4,5},{5,4},{6,7},{7,6},{8,9},{9,8},{10,11... | collective-permute-start | bytes 12296 | tf_op jit(solution)/shard_map/ppermute | solution.py:234
